TPU v7x, 128 devices: a whole 4x4x4 slice. The times are simulated.
128 devices in a mesh: brick: 16 (over y, x), sub: 8 (over z, core).
Axes of the slice: x: 4, y: 4, z: 4, core: 2. Of those that a mesh axis runs over, the one named last changes fastest.
Arguments:
- field_start: float32 [8192, 16, 256], P(('brick', 'sub')), may hold values from -6 to 6
- source: float32 [8192, 16, 256], P(('brick', 'sub')), may hold values from -24 to 24
- diffusion: float32 [8192, 16, 256], P(('brick', 'sub')), may hold values from 0.2 to 5
- decay_rate: float32 [8192, 16, 256], P(('brick', 'sub')), may hold values from 0.5 to 8
- neighbour: int32 [8192, 6], P(('brick', 'sub')), may hold values from -1 to 49151, as said below
- coarse_source: int32 [1024], P(('brick', 'sub')), may hold values from 0 to 1023, as said below
Outputs:
- smoothed: float32 [8192, 16, 256], P(('brick', 'sub'))
- moved_coarse: float32 [1024, 3, 16, 256], P(('brick', 'sub'))
Inputs may be any that keep to these rules, and one draw needn't show every extreme that they name: `neighbour`: bricks are numbered 64 per device in the order of the joined axis brick+sub. A brick borders only bricks of its own device or of the devices one step away along brick or along sub. Face f of a brick borders face f xor 1 of another brick or nothing (-1), and the relation is symmetric. At most 16 faces of one device border the device one step along brick, and at most 16 the device one step along sub; some pairs of devices reach each. `coarse_source`: A permutation of the level-2 bricks. A level-2 brick moves only between devices of the same index along sub. Each device receives 1 of its slots' bricks from each of 8 devices (possibly itself) and hands 1 of its own to each of 8.
All inputs are finite; a program needn't handle non-finite values.
Results may differ from a plain program's by a relative error of at most 0.00007.
Values sent between devices are 32-bit elements; how exact they have to be, the bound alone decides.
No kernel may reach another device: no remote copies, remote signals or barrier semaphores. Data moves between devices by JAX's collectives and lax.ppermute only.
A program may use at most 128 MiB of HBM per device.

v0:
```python
import functools

import jax
import jax.numpy as jnp
from jax import lax
from jax.experimental import pallas as pl
from jax.experimental.pallas import tpu as pltpu
from jax.sharding import PartitionSpec as P

EDGE = 4
LZ = 4
SWEEPS = 2
OMEGA = 0.8

SIDE = 16
PLANE = SIDE * SIDE
HALF = PLANE // 2
BRK = EDGE * EDGE * LZ
FACES = 6 * BRK
COARSE_DEV = BRK // 8
CAP = 16
PEERS = 4
ZERO_BRICK = BRK
MESSAGE_BRICK = BRK + 1
SLOT_BRICK = MESSAGE_BRICK + PEERS
EXT_BRICKS = SLOT_BRICK + PEERS * CAP
SEND_ROW = 6
ODD_ROW = 7
F32 = jnp.float32
I32 = jnp.int32
VMEM_LIMIT = 40 * 1024 * 1024


def native_place(face):
    return SIDE - 1 if face % 2 == 0 else 0


def lane_iota(shape):
    return lax.broadcasted_iota(I32, shape, len(shape) - 1)


def row_iota(shape):
    return lax.broadcasted_iota(I32, shape, len(shape) - 2)


def brick_rows(index):
    return pl.ds(pl.multiple_of(index * SIDE, SIDE), SIDE)


def peers_of(subs):
    brick_at = lax.axis_index("brick")
    sub_at = lax.axis_index("sub")
    me = brick_at * subs + sub_at
    brick_step = jnp.where(brick_at % 2 == 0, subs, -subs)
    sub_step = jnp.where(sub_at % 2 == 0, 1, -1)
    return me, [me + brick_step, me - brick_step, me + sub_step, me - sub_step]


def route_kernel(subs, links_ref, table_ref, staged, sem):
    me, peers = peers_of(subs)
    links_row = links_ref[...]
    eye = (row_iota((BRK, BRK)) == lane_iota((BRK, BRK))).astype(F32)

    def turned(values):
        return lax.dot_general(
            eye, values.astype(F32), (((1,), (1,)), ((), ())), preferred_element_type=F32
        ).astype(I32)

    links_col = turned(links_row >> 8) * 256 + turned(links_row & 255)

    def keyed(links, own_face):
        key = jnp.full(links.shape, -1, I32)
        floor = jnp.full(links.shape, -1, I32)
        for number, peer in enumerate(peers):
            base = peer * FACES
            there = (links >= 0) & (links >= base) & (links < base + FACES)
            order = jnp.where(peer > me, own_face, links)
            key = jnp.where(there, order + number * 65536, key)
            floor = jnp.where(there, number * 65536, floor)
        return key, floor

    key_row, floor_row = keyed(links_row, lane_iota((6, BRK)) * 6 + row_iota((6, BRK)))
    key_col, floor_col = keyed(links_col, row_iota((BRK, 6)) * 6 + lane_iota((BRK, 6)))

    slot_lane = lane_iota((BRK, BRK))
    brick_sub = row_iota((BRK, BRK))
    listed = jnp.zeros((BRK, BRK), F32)
    odd = jnp.zeros((1, BRK), F32)
    for face in range(6):
        mine = key_col[:, face : face + 1]
        least = floor_col[:, face : face + 1]
        count = jnp.zeros((BRK, BRK), F32)
        for other in range(6):
            theirs = key_row[other : other + 1, :]
            count = count + ((theirs < mine) & (theirs >= least)).astype(F32)
        rank = jnp.sum(count, axis=1, keepdims=True).astype(I32)
        slot = jnp.where(mine >= 0, (least >> 16) * CAP + rank, -1)
        listed = listed + jnp.where(slot == slot_lane, (brick_sub + (face * BRK + 1)).astype(F32), 0.0)
        mine = key_row[face : face + 1, :]
        least = floor_row[face : face + 1, :]
        count = jnp.zeros((BRK, BRK), F32)
        for other in range(6):
            theirs = key_col[:, other : other + 1]
            count = count + ((theirs < mine) & (theirs >= least)).astype(F32)
        rank = jnp.sum(count, axis=0, keepdims=True).astype(I32)
        message = least >> 16
        place = native_place(face)
        if face // 2 == 0:
            plain = message < 2
        elif face // 2 == 2:
            plain = message >= 2
        else:
            plain = message < 0
        far = mine >= 0
        odd = odd + (far & jnp.logical_not(plain)).astype(F32)
        links = links_row[face : face + 1, :]
        local = links - me * FACES
        near = (links >= 0) & (local >= 0) & (local < FACES)
        near_brick = ((local - (face ^ 1)) * 10923) >> 16
        far_code = jnp.where(
            plain,
            (MESSAGE_BRICK + message) * SIDE + rank,
            (SLOT_BRICK + message * CAP + rank) * SIDE + place,
        )
        code = jnp.where(
            near, near_brick * SIDE + place, jnp.where(far, far_code, ZERO_BRICK * SIDE)
        )
        staged[face : face + 1, 0:BRK] = code
    staged[SEND_ROW : SEND_ROW + 1, 0:BRK] = jnp.sum(listed, axis=0, keepdims=True).astype(I32) - 1
    staged[ODD_ROW : ODD_ROW + 1, 0:BRK] = jnp.broadcast_to(
        jnp.sum(odd, axis=1, keepdims=True).astype(I32), (1, BRK)
    )
    copy = pltpu.make_async_copy(staged, table_ref, sem)
    copy.start()
    copy.wait()


def picker(shape, lane_axis, make):
    lane = lax.broadcasted_iota(I32, shape, lane_axis)
    inner = lax.broadcasted_iota(I32, shape, 1 - lane_axis)
    return make(lane, inner).astype(F32)


def exact_dot(left, right):
    return jnp.dot(left, right, precision=lax.Precision.HIGHEST, preferred_element_type=F32)


def column_rule(place):
    return lambda lane, inner: lane == inner * SIDE + place


def lanes_rule(place):
    return lambda lane, inner: lane == place * SIDE + inner


def fold_rule(lane, inner):
    return lane % SIDE == inner


def band_mask():
    return lane_iota((SIDE, PLANE)) // SIDE == row_iota((SIDE, PLANE))


def compacted(brick, rule):
    return exact_dot(brick, picker((PLANE, SIDE), 0, rule))


def spread(compact, rule):
    return exact_dot(compact, picker((SIDE, PLANE), 1, rule))


def compact_face(ref, brick, face):
    place = (face & 1) * (SIDE - 1)
    kind = face >> 1
    cells = ref[brick_rows(brick), :]
    row = ref[pl.ds(brick * SIDE + place, 1), :]
    from_x = compacted(cells, column_rule(place))
    from_y = compacted(cells, lanes_rule(place))
    from_z = compacted(jnp.where(band_mask(), row, 0.0), fold_rule)
    return jnp.where(kind == 0, from_x, jnp.where(kind == 1, from_y, from_z))


def fits(face, message):
    return face < 2 if message < 2 else face >= 4


def pack(ref, table, message, out_ref, base):
    if message < 2:
        column = lane_iota((SIDE, HALF)) % SIDE
        low = jnp.zeros((SIDE, HALF), F32)
        high = jnp.zeros((SIDE, HALF), F32)
        for slot in range(CAP):
            entry = jnp.maximum(table[SEND_ROW, message * CAP + slot], 0)
            rows = brick_rows(entry & (BRK - 1))
            turn = (slot - ((entry >> 6) & 1) * (SIDE - 1)) & (HALF - 1)
            here = column == slot
            low = jnp.where(here, pltpu.roll(ref[rows, 0:HALF], turn, 1), low)
            high = jnp.where(here, pltpu.roll(ref[rows, HALF:PLANE], turn, 1), high)
        out_ref[base : base + SIDE, 0:HALF] = low
        out_ref[base : base + SIDE, HALF:PLANE] = high
    else:
        for slot in range(CAP):
            entry = jnp.maximum(table[SEND_ROW, message * CAP + slot], 0)
            row = (entry & (BRK - 1)) * SIDE + ((entry >> 6) & 1) * (SIDE - 1)
            out_ref[base + slot : base + slot + 1, :] = ref[pl.ds(row, 1), :]

    @pl.when(table[ODD_ROW, 0] > 0)
    def _():
        def step(slot, carry):
            entry = table[SEND_ROW, message * CAP + slot]
            face = entry >> 6

            @pl.when((entry >= 0) & jnp.logical_not(fits(face, message)))
            def _():
                compact = compact_face(ref, entry & (BRK - 1), face)
                if message < 2:
                    cells = spread(compact, column_rule(slot))
                    here = lane_iota((SIDE, PLANE)) % SIDE == slot
                    out_ref[base : base + SIDE, :] = jnp.where(
                        here, cells, out_ref[base : base + SIDE, :]
                    )
                else:
                    cells = jnp.where(band_mask(), spread(compact, fold_rule), 0.0)
                    here = row_iota((SIDE, PLANE)) == slot
                    out_ref[base : base + SIDE, :] = jnp.where(
                        here, jnp.sum(cells, axis=0, keepdims=True), out_ref[base : base + SIDE, :]
                    )

            return carry

        lax.fori_loop(0, CAP, step, 0)


def fill_extended(ext, field_ref, messages, base, table):
    ext[0 : BRK * SIDE, :] = field_ref[...]
    ext[ZERO_BRICK * SIDE : (ZERO_BRICK + 1) * SIDE, :] = jnp.zeros((SIDE, PLANE), F32)
    for message in range(PEERS):
        at = (MESSAGE_BRICK + message) * SIDE
        ext[at : at + SIDE, :] = messages[message][base : base + SIDE, :]

    @pl.when(table[ODD_ROW, 0] > 0)
    def _():
        for message in range(PEERS):
            at = (MESSAGE_BRICK + message) * SIDE

            def step(slot, carry):
                entry = table[SEND_ROW, message * CAP + slot]
                face = entry >> 6

                @pl.when((entry >= 0) & jnp.logical_not(fits(face, message)))
                def _():
                    cells = ext[at : at + SIDE, :]
                    if message < 2:
                        compact = compacted(cells, column_rule(slot))
                    else:
                        row = jnp.sum(
                            jnp.where(row_iota((SIDE, PLANE)) == slot, cells, 0.0), axis=0, keepdims=True
                        )
                        compact = compacted(jnp.where(band_mask(), row, 0.0), fold_rule)
                    place = (1 - (face & 1)) * (SIDE - 1)
                    kind = face >> 1
                    from_x = spread(compact, column_rule(place))
                    from_y = spread(compact, lanes_rule(place))
                    row = jnp.where(band_mask(), spread(compact, fold_rule), 0.0)
                    from_z = jnp.broadcast_to(jnp.sum(row, axis=0, keepdims=True), (SIDE, PLANE))
                    ext[brick_rows(SLOT_BRICK + message * CAP + slot), :] = jnp.where(
                        kind == 0, from_x, jnp.where(kind == 1, from_y, from_z)
                    )

                return carry

            lax.fori_loop(0, CAP, step, 0)


def beside(ext, table, brick, low, high):
    lane = lane_iota((SIDE, HALF))
    column = lane % SIDE
    row = row_iota((SIDE, HALF))

    def entry(face):
        code = table[face, brick]
        return code >> 4, code & (SIDE - 1)

    source, place = entry(0)
    rows = brick_rows(source)
    turn = (HALF - place) & (HALF - 1)
    here = column == 0
    x_lower = (
        jnp.where(here, pltpu.roll(ext[rows, 0:HALF], turn, 1), pltpu.roll(low, 1, 1)),
        jnp.where(here, pltpu.roll(ext[rows, HALF:PLANE], turn, 1), pltpu.roll(high, 1, 1)),
    )
    source, place = entry(1)
    rows = brick_rows(source)
    turn = SIDE - 1 - place
    here = column == SIDE - 1
    x_upper = (
        jnp.where(here, pltpu.roll(ext[rows, 0:HALF], turn, 1), pltpu.roll(low, HALF - 1, 1)),
        jnp.where(here, pltpu.roll(ext[rows, HALF:PLANE], turn, 1), pltpu.roll(high, HALF - 1, 1)),
    )
    source, place = entry(2)
    part = pl.multiple_of((place >> 3) * HALF, HALF)
    turn = (HALF - (place & 7) * SIDE) & (HALF - 1)
    ghost = pltpu.roll(ext[brick_rows(source), pl.ds(part, HALF)], turn, 1)
    turned_low = pltpu.roll(low, SIDE, 1)
    turned_high = pltpu.roll(high, SIDE, 1)
    here = lane < SIDE
    y_lower = (jnp.where(here, ghost, turned_low), jnp.where(here, turned_low, turned_high))
    source, place = entry(3)
    part = pl.multiple_of((place >> 3) * HALF, HALF)
    turn = HALF - SIDE - (place & 7) * SIDE
    ghost = pltpu.roll(ext[brick_rows(source), pl.ds(part, HALF)], turn, 1)
    turned_low = pltpu.roll(low, HALF - SIDE, 1)
    turned_high = pltpu.roll(high, HALF - SIDE, 1)
    here = lane >= HALF - SIDE
    y_upper = (jnp.where(here, turned_high, turned_low), jnp.where(here, ghost, turned_high))
    source, place = entry(4)
    ghost = ext[pl.ds(source * SIDE + place, 1), :]
    here = row == 0
    z_lower = (
        jnp.where(here, ghost[:, 0:HALF], pltpu.roll(low, 1, 0)),
        jnp.where(here, ghost[:, HALF:PLANE], pltpu.roll(high, 1, 0)),
    )
    source, place = entry(5)
    ghost = ext[pl.ds(source * SIDE + place, 1), :]
    here = row == SIDE - 1
    z_upper = (
        jnp.where(here, ghost[:, 0:HALF], pltpu.roll(low, SIDE - 1, 0)),
        jnp.where(here, ghost[:, HALF:PLANE], pltpu.roll(high, SIDE - 1, 0)),
    )
    return [x_lower, x_upper, y_lower, y_upper, z_lower, z_upper]


LANES = (slice(0, HALF), slice(HALF, PLANE))
DIAGONAL = 6
SCALE = 7


def pack_kernel(table, field_ref, kappa_ref, *outs):
    for message in range(PEERS):
        pack(field_ref, table, message, outs[message], 0)
        pack(kappa_ref, table, message, outs[message], SIDE)


def first_kernel(table, field_ref, kappa_ref, source_ref, decay_ref, m0, m1, m2, m3, new_ref, coef_ref, o0, o1, o2, o3, ext, kappa_ext):
    messages = (m0, m1, m2, m3)
    fill_extended(ext, field_ref, messages, 0, table)
    fill_extended(kappa_ext, kappa_ref, messages, SIDE, table)

    def step(brick, carry):
        rows = brick_rows(brick)
        field = [ext[rows, lanes] for lanes in LANES]
        kappa = [kappa_ext[rows, lanes] for lanes in LANES]
        around = beside(ext, table, brick, *field)
        kappa_around = beside(kappa_ext, table, brick, *kappa)
        for half, lanes in enumerate(LANES):
            diagonal = decay_ref[rows, lanes]
            total = source_ref[rows, lanes]
            for face in range(6):
                link = 0.5 * (kappa[half] + kappa_around[face][half])
                coef_ref[face, rows, lanes] = link
                diagonal = diagonal + link
                total = total + link * around[face][half]
            scale = OMEGA / diagonal
            coef_ref[DIAGONAL, rows, lanes] = diagonal
            coef_ref[SCALE, rows, lanes] = scale
            new_ref[rows, lanes] = (1.0 - OMEGA) * field[half] + scale * total
        return carry

    lax.fori_loop(0, BRK, step, 0)
    for message, out in enumerate((o0, o1, o2, o3)):
        pack(new_ref, table, message, out, 0)


def sweep_kernel(table, field_ref, source_ref, coef_ref, m0, m1, m2, m3, new_ref, o0, o1, o2, o3, ext):
    fill_extended(ext, field_ref, (m0, m1, m2, m3), 0, table)

    def step(brick, carry):
        rows = brick_rows(brick)
        field = [ext[rows, lanes] for lanes in LANES]
        around = beside(ext, table, brick, *field)
        for half, lanes in enumerate(LANES):
            total = source_ref[rows, lanes]
            for face in range(6):
                total = total + coef_ref[face, rows, lanes] * around[face][half]
            new_ref[rows, lanes] = (1.0 - OMEGA) * field[half] + coef_ref[SCALE, rows, lanes] * total
        return carry

    lax.fori_loop(0, BRK, step, 0)
    for message, out in enumerate((o0, o1, o2, o3)):
        pack(new_ref, table, message, out, 0)


def restricted(*parts):
    rows = BRK * SIDE // 2
    paired = jnp.concatenate(
        [part[pl.ds(0, rows, stride=2), :] + part[pl.ds(1, rows, stride=2), :] for part in parts], axis=1
    )
    fine = lax.broadcasted_iota(I32, (PLANE, HALF), 0)
    target = lax.broadcasted_iota(I32, (PLANE, HALF), 1)
    same = (fine // (2 * SIDE) == target // SIDE) & ((fine % SIDE) // 2 == target % SIDE)
    table = jnp.where(same, 0.125, 0.0).astype(jnp.bfloat16)
    total = jnp.zeros((rows, HALF), F32)
    rest = paired
    for _ in range(3):
        part = rest.astype(jnp.bfloat16)
        total = total + jnp.dot(part, table, preferred_element_type=F32)
        rest = rest - part.astype(F32)
    return total


def coarse_tiles(values):
    depth = SIDE // 2
    for coarse in range(COARSE_DEV):
        cz, cy, cx = coarse // 4, coarse // 2 % 2, coarse % 2
        for pz in range(2):
            for py in range(2):
                fine = ((2 * cz + pz) * EDGE + 2 * cy + py) * EDGE + 2 * cx
                left = values[fine * depth : (fine + 1) * depth, :]
                right = values[(fine + 1) * depth : (fine + 2) * depth, :]
                yield coarse, pz, py, left + pltpu.roll(right, depth, 1)


def write_coarse(values, out_ref, base):
    for coarse, pz, py, tile in coarse_tiles(values):
        top = base + pz * (SIDE // 2)
        out_ref[coarse, top : top + SIDE // 2, py * HALF : (py + 1) * HALF] = tile


def coefficient_kernel(kappa_ref, decay_ref, out_ref, low, high):
    for ref, base in ((kappa_ref, 0), (decay_ref, SIDE)):
        low[...] = ref[:, 0:HALF]
        high[...] = ref[:, HALF:PLANE]
        write_coarse(restricted(low, high), out_ref, base)


def residual_kernel(table, wanted, field_ref, source_ref, coef_ref, coarse_ref, m0, m1, m2, m3, send_ref, ext, left_low, left_high, coarse_left):
    fill_extended(ext, field_ref, (m0, m1, m2, m3), 0, table)

    def step(brick, carry):
        rows = brick_rows(brick)
        field = [ext[rows, lanes] for lanes in LANES]
        around = beside(ext, table, brick, *field)
        for half, lanes in enumerate(LANES):
            total = source_ref[rows, lanes] - coef_ref[DIAGONAL, rows, lanes] * field[half]
            for face in range(6):
                total = total + coef_ref[face, rows, lanes] * around[face][half]
            (left_low, left_high)[half][rows, :] = total
        return carry

    lax.fori_loop(0, BRK, step, 0)
    write_coarse(restricted(left_low, left_high), coarse_left, 0)

    def hand_over(target, carry):
        chosen = jnp.maximum(wanted[target], 0)
        send_ref[target, 0:SIDE, :] = coarse_left[chosen]
        send_ref[target, SIDE : 3 * SIDE, :] = coarse_ref[chosen]
        return carry

    lax.fori_loop(0, send_ref.shape[0], hand_over, 0)


def place_kernel(per_row, coarse_source, arrived, out_ref, sem):
    copies = [
        pltpu.make_async_copy(arrived.at[coarse_source[slot] // per_row], out_ref.at[slot], sem.at[slot])
        for slot in range(COARSE_DEV)
    ]
    for copy in copies:
        copy.start()
    for copy in copies:
        copy.wait()


def paired(block, axis, offset):
    size = lax.axis_size(axis)
    route = []
    for first in range(offset, size + offset, 2):
        one, two = first % size, (first + 1) % size
        route += [(one, two), (two, one)]
    return lax.ppermute(block, axis, route)


def exchanged(outgoing):
    return [
        paired(outgoing[0], "brick", 0),
        paired(outgoing[1], "brick", 1),
        paired(outgoing[2], "sub", 0),
        paired(outgoing[3], "sub", 1),
    ]


VMEM_SPEC = pl.BlockSpec(memory_space=pltpu.VMEM)
SMEM_SPEC = pl.BlockSpec(memory_space=pltpu.SMEM)
ANY_SPEC = pl.BlockSpec(memory_space=pl.ANY)


def in_vmem(*shape):
    return pltpu.VMEM(shape, F32)


def kernel_call(kernel, name, ins, outs, out_specs=None, scratch=()):
    return pl.pallas_call(
        kernel,
        out_shape=outs,
        in_specs=ins,
        out_specs=out_specs if out_specs is not None else tuple(VMEM_SPEC for _ in outs),
        scratch_shapes=list(scratch),
        compiler_params=pltpu.CompilerParams(vmem_limit_bytes=VMEM_LIMIT),
        name=name,
    )


def body(field_start, source, diffusion, decay_rate, neighbour, coarse_source):
    subs = lax.axis_size("sub")
    rows = BRK * SIDE
    field_start, source, diffusion, decay_rate = (
        array.reshape(rows, PLANE) for array in (field_start, source, diffusion, decay_rate)
    )
    table = kernel_call(
        functools.partial(route_kernel, subs),
        "route",
        [VMEM_SPEC],
        jax.ShapeDtypeStruct((8, 128), I32),
        out_specs=SMEM_SPEC,
        scratch=[pltpu.VMEM((8, 128), I32), pltpu.SemaphoreType.DMA(())],
    )(neighbour.T)
    message = in_vmem(SIDE, PLANE)
    double = in_vmem(2 * SIDE, PLANE)
    extended = pltpu.VMEM((EXT_BRICKS * SIDE, PLANE), F32)

    outgoing = kernel_call(
        pack_kernel, "pack", [SMEM_SPEC] + [VMEM_SPEC] * 2, (double,) * PEERS
    )(table, field_start, diffusion)
    incoming = exchanged(outgoing)

    me = lax.axis_index("brick") * subs + lax.axis_index("sub")
    orders = lax.all_gather(coarse_source, "brick")
    mine = orders - me * COARSE_DEV
    mine = jnp.where((mine >= 0) & (mine < COARSE_DEV), mine, -1)
    wanted = jnp.max(mine, axis=1)
    coarse_coefs = kernel_call(
        coefficient_kernel, "coarse_coefficients", [VMEM_SPEC] * 2, (in_vmem(COARSE_DEV, 2 * SIDE, PLANE),),
        scratch=[pltpu.VMEM((rows, HALF), F32), pltpu.VMEM((rows, HALF), F32)],
    )(diffusion, decay_rate)[0]

    field, coefs, *outgoing = kernel_call(
        first_kernel,
        "first_sweep",
        [SMEM_SPEC] + [VMEM_SPEC] * 8,
        (in_vmem(rows, PLANE), in_vmem(8, rows, PLANE)) + (message,) * PEERS,
        scratch=[extended, extended],
    )(table, field_start, diffusion, source, decay_rate, *incoming)
    incoming = exchanged(outgoing)
    for _ in range(SWEEPS - 1):
        field, *outgoing = kernel_call(
            sweep_kernel,
            "next_sweep",
            [SMEM_SPEC] + [VMEM_SPEC] * 7,
            (in_vmem(rows, PLANE),) + (message,) * PEERS,
            scratch=[extended],
        )(table, field, source, coefs, *incoming)
        incoming = exchanged(outgoing)
    brick_count = lax.axis_size("brick")
    send = kernel_call(
        residual_kernel,
        "residual",
        [SMEM_SPEC] * 2 + [VMEM_SPEC] * 8,
        (in_vmem(brick_count, 3 * SIDE, PLANE),),
        scratch=[extended, pltpu.VMEM((rows, HALF), F32), pltpu.VMEM((rows, HALF), F32), pltpu.VMEM((COARSE_DEV, SIDE, PLANE), F32)],
    )(table, wanted, field, source, coefs, coarse_coefs, *incoming)[0]
    arrived = lax.all_to_all(send, "brick", split_axis=0, concat_axis=0, tiled=True)
    moved = kernel_call(
        functools.partial(place_kernel, subs * COARSE_DEV),
        "place",
        [SMEM_SPEC, ANY_SPEC],
        jax.ShapeDtypeStruct((COARSE_DEV, 3 * SIDE, PLANE), F32),
        out_specs=ANY_SPEC,
        scratch=[pltpu.SemaphoreType.DMA((COARSE_DEV,))],
    )(coarse_source, arrived)
    return field.reshape(BRK, SIDE, PLANE), moved.reshape(COARSE_DEV, 3, SIDE, PLANE)


def solution(mesh):
    placed = (
        P(("brick", "sub"), None, None),
        P(("brick", "sub"), None, None),
        P(("brick", "sub"), None, None),
        P(("brick", "sub"), None, None),
        P(("brick", "sub"), None),
        P(("brick", "sub")),
    )
    return jax.shard_map(
        body,
        mesh=mesh,
        in_specs=placed,
        out_specs=(P(("brick", "sub"), None, None), P(("brick", "sub"), None, None, None)),
        check_vma=False,
    )
```

profile of v0, /device:TPU:0, one launch (start us, length us, event | category | flops | bytes accessed | tf_op | source)
XLA Modules:
  0.0 110.4 jit_solution(535581824452302265)
XLA Ops:
  0.6 0.7 copy-done.16
  1.3 2.0 %route.1.table = s32[8,128]{1,0:T(8,128)S(1)} custom-call(s32[6,64]{1,0:T(8,128)S(1)} %bitcast.19), custom_call_target="tpu_custom_call" | custom-call | tf_op jit(solution)/shard_map/route/pallas_call | solution.py:518
  3.3 0.0 copy-start.3
  3.4 1.2 %copy-done.3 = f32[64,16,256]{2,1,0:T(8,128)S(1)} copy-done((f32[64,16,256]{2,1,0:T(8,128)S(1)}, f32[64,16,256]{2,1,0:T(8,128)}, u32[]{:S(2)}) %copy-start.3) | copy-done | bytes 1048600
  4.6 1.2 %copy-done.9 = f32[64,16,256]{2,1,0:T(8,128)S(1)} copy-done((f32[64,16,256]{2,1,0:T(8,128)S(1)}, f32[64,16,256]{2,1,0:T(8,128)}, u32[]{:S(2)}) %copy-start.9) | copy-done | bytes 1048600
  5.8 1.4 %pack.1 = (f32[32,256]{1,0:T(8,128)S(1)}, f32[32,256]{1,0:T(8,128)S(1)}, f32[32,256]{1,0:T(8,128)S(1)}, f32[32,256]{1,0:T(8,128)S(1)}) custom-call(s32[8,128]{1,0:T(8,128)S(1)} %route.1.table, f32[1024,256]{1,0:T(8,128)S(1)} %bitcast.15, f32[1024,256]{1,0:T(8,128)S(1)} %bitcast.9), custom_call_target="tpu_custom_call" | custom-call | tf_op jit(solution)/shard_map/pack/pallas_call | solution.py:530
  7.2 1.7 %collective-permute-start = (f32[32,256]{1,0:T(8,128)S(1)}, f32[32,256]{1,0:T(8,128)S(1)}, u32[]{:S(2)}, u32[]{:S(2)}) collective-permute-start(f32[32,256]{1,0:T(8,128)S(1)} %get-tuple-element.17), channel_id=1, source_target_pairs={{0,8},{8,0},{16,24},{24,16},{32,40},{40,32},{48,56},{56,48},{64,72... | collective-permute-start | bytes 98312 | tf_op jit(solution)/shard_map/ppermute | solution.py:479
  8.9 4.5 %collective-permute-start.1 = (f32[32,256]{1,0:T(8,128)S(1)}, f32[32,256]{1,0:T(8,128)S(1)}, u32[]{:S(2)}, u32[]{:S(2)}) collective-permute-start(f32[32,256]{1,0:T(8,128)S(1)} %get-tuple-element.18), channel_id=1, source_target_pairs={{8,16},{16,8},{24,32},{32,24},{40,48},{48,40},{56,64},{64,56},{72,... | collective-permute-start | bytes 98312 | tf_op jit(solution)/shard_map/ppermute | solution.py:479
  13.4 4.1 %collective-permute-start.3 = (f32[32,256]{1,0:T(8,128)S(1)}, f32[32,256]{1,0:T(8,128)S(1)}, u32[]{:S(2)}, u32[]{:S(2)}) collective-permute-start(f32[32,256]{1,0:T(8,128)S(1)} %get-tuple-element.20), channel_id=1, source_target_pairs={{1,2},{2,1},{3,4},{4,3},{5,6},{6,5},{7,0},{0,7},{9,10},{10,9},{11,... | collective-permute-start | bytes 98312 | tf_op jit(solution)/shard_map/ppermute | solution.py:479
  17.6 1.2 %dynamic-slice = u32[1]{0:T(128)} dynamic-slice(u32[128]{0:T(128)} %constant.26, u32[]{:T(128)S(6)} %add.4), dynamic_slice_sizes={1} | dynamic-slice | bytes 12
  19.5 0.9 dynamic-update-slice
  20.3 11.7 %all-reduce = s32[128]{0:T(128)S(1)} all-reduce(s32[128]{0:T(128)S(1)} %dynamic-update-slice), channel_id=2, replica_groups=mesh['brick'=16,'sub'=8] {'brick'}, use_global_device_ids=true, to_apply=%add | all-reduce | flops 128 | bytes 1024
  32.0 0.0 collective-permute-done.m0
  32.0 0.0 collective-permute-done.1.m1
  32.0 0.0 collective-permute-done.2.m2
  32.0 0.0 collective-permute-done.3.m3
  32.0 0.0 copy-start.4
  32.1 1.2 %copy-done.4 = f32[64,16,256]{2,1,0:T(8,128)S(1)} copy-done((f32[64,16,256]{2,1,0:T(8,128)S(1)}, f32[64,16,256]{2,1,0:T(8,128)}, u32[]{:S(2)}) %copy-start.4) | copy-done | bytes 1048600
  33.3 1.2 %copy-done.6 = f32[64,16,256]{2,1,0:T(8,128)S(1)} copy-done((f32[64,16,256]{2,1,0:T(8,128)S(1)}, f32[64,16,256]{2,1,0:T(8,128)}, u32[]{:S(2)}) %copy-start.6) | copy-done | bytes 1048600
  34.5 1.2 %copy-done.10 = f32[64,16,256]{2,1,0:T(8,128)S(1)} copy-done((f32[64,16,256]{2,1,0:T(8,128)S(1)}, f32[64,16,256]{2,1,0:T(8,128)}, u32[]{:S(2)}) %copy-start.10) | copy-done | bytes 1048600
  35.7 1.2 %copy-done.11 = f32[64,16,256]{2,1,0:T(8,128)S(1)} copy-done((f32[64,16,256]{2,1,0:T(8,128)S(1)}, f32[64,16,256]{2,1,0:T(8,128)}, u32[]{:S(2)}) %copy-start.11) | copy-done | bytes 1048600
  36.9 9.9 %first_sweep.1 = (f32[1024,256]{1,0:T(8,128)S(1)}, f32[8,1024,256]{2,1,0:T(8,128)S(1)}, f32[16,256]{1,0:T(8,128)S(1)}, f32[16,256]{1,0:T(8,128)S(1)}, f32[16,256]{1,0:T(8,128)S(1)}, /*index=5*/f32[16,256]{1,0:T(8,128)S(1)}) custom-call(s32[8,128]{1,0:T(8,128)S(1)} %route.1.table, f32[1024,256]{1,0:T(8,128)S(1)} %bitcast.16, f32[1024,256]{1,0:T(8,128)S(1)} %bitcast.10, ...), custom_call_target="tpu_custom_call" | custom-call | tf_op jit(solution)/shard_map/first_sweep/pallas_call | solution.py:545
  46.8 3.3 %copy-done = f32[8,1024,256]{2,1,0:T(8,128)} copy-done((f32[8,1024,256]{2,1,0:T(8,128)}, f32[8,1024,256]{2,1,0:T(8,128)S(1)}, u32[]{:S(2)}) %copy-start) | copy-done | bytes 8388632
  50.1 1.0 copy-done.14
  51.1 1.0 collective-permute-start.4
  52.1 4.5 %collective-permute-start.5 = (f32[16,256]{1,0:T(8,128)S(1)}, f32[16,256]{1,0:T(8,128)S(1)}, u32[]{:S(2)}, u32[]{:S(2)}) collective-permute-start(f32[16,256]{1,0:T(8,128)S(1)} %get-tuple-element.24), channel_id=1, source_target_pairs={{8,16},{16,8},{24,32},{32,24},{40,48},{48,40},{56,64},{64,56},{72,... | collective-permute-start | bytes 49160 | tf_op jit(solution)/shard_map/ppermute | solution.py:479
  56.6 0.5 collective-permute-start.7
  57.1 0.1 reshape.30
  57.2 1.9 %collective-permute-done.5.m1 = f32[16,256]{1,0:T(8,128)S(1)} collective-permute-done((f32[16,256]{1,0:T(8,128)S(1)}, f32[16,256]{1,0:T(8,128)S(1)}, u32[]{:S(2)}, u32[]{:S(2)}) %collective-permute-start.5) | collective-permute-done | bytes 16416 | tf_op jit(solution)/shard_map/ppermute | solution.py:479
  59.1 1.9 %collective-permute-done.7.m3 = f32[16,256]{1,0:T(8,128)S(1)} collective-permute-done((f32[16,256]{1,0:T(8,128)S(1)}, f32[16,256]{1,0:T(8,128)S(1)}, u32[]{:S(2)}, u32[]{:S(2)}) %collective-permute-start.7) | collective-permute-done | bytes 16416 | tf_op jit(solution)/shard_map/ppermute | solution.py:479
  61.0 3.4 %copy-done.1 = f32[8,1024,256]{2,1,0:T(8,128)S(1)} copy-done((f32[8,1024,256]{2,1,0:T(8,128)S(1)}, f32[8,1024,256]{2,1,0:T(8,128)}, u32[]{:S(2)}) %copy-start.1) | copy-done | bytes 8388632
  64.4 1.2 %copy-done.7 = f32[64,16,256]{2,1,0:T(8,128)S(1)} copy-done((f32[64,16,256]{2,1,0:T(8,128)S(1)}, f32[64,16,256]{2,1,0:T(8,128)}, u32[]{:S(2)}) %copy-start.7) | copy-done | bytes 1048600
  65.6 1.2 %copy-done.15 = f32[1024,256]{1,0:T(8,128)S(1)} copy-done((f32[1024,256]{1,0:T(8,128)S(1)}, f32[1024,256]{1,0:T(8,128)}, u32[]{:S(2)}) %copy-start.15) | copy-done | bytes 1048600
  66.8 8.0 %next_sweep.1 = (f32[1024,256]{1,0:T(8,128)S(1)}, f32[16,256]{1,0:T(8,128)S(1)}, f32[16,256]{1,0:T(8,128)S(1)}, f32[16,256]{1,0:T(8,128)S(1)}, f32[16,256]{1,0:T(8,128)S(1)}) custom-call(s32[8,128]{1,0:T(8,128)S(1)} %route.1.table, f32[1024,256]{1,0:T(8,128)S(1)} %copy-done.15, f32[1024,256]{1,0:T(8,128)S(1)} %bitcast.13, f32[8,1024,256]{2,1,0:T(8,128)S(1)} %copy-done.1, ...), custom_call_target="tpu_custom_call" | custom-call | tf_op jit(solution)/shard_map/next_sweep/pallas_call | solution.py:554
  74.9 0.1 collective-permute-start.10
  75.0 0.6 collective-permute-start.11
  75.6 2.6 %collective-permute-start.9 = (f32[16,256]{1,0:T(8,128)S(1)}, f32[16,256]{1,0:T(8,128)S(1)}, u32[]{:S(2)}, u32[]{:S(2)}) collective-permute-start(f32[16,256]{1,0:T(8,128)S(1)} %get-tuple-element.29), channel_id=1, source_target_pairs={{8,16},{16,8},{24,32},{32,24},{40,48},{48,40},{56,64},{64,56},{72,... | collective-permute-start | bytes 49160 | tf_op jit(solution)/shard_map/ppermute | solution.py:479
  78.2 0.1 select_reduce_fusion.wanted
  78.3 0.0 copy-start.12
  78.3 1.2 %copy-done.12 = f32[64,16,256]{2,1,0:T(8,128)S(1)} copy-done((f32[64,16,256]{2,1,0:T(8,128)S(1)}, f32[64,16,256]{2,1,0:T(8,128)}, u32[]{:S(2)}) %copy-start.12) | copy-done | bytes 1048600
  79.5 0.8 coarse_coefficients.1.coarse_ref
  80.3 2.3 %collective-permute-done.9.m1 = f32[16,256]{1,0:T(8,128)S(1)} collective-permute-done((f32[16,256]{1,0:T(8,128)S(1)}, f32[16,256]{1,0:T(8,128)S(1)}, u32[]{:S(2)}, u32[]{:S(2)}) %collective-permute-start.9) | collective-permute-done | bytes 16416 | tf_op jit(solution)/shard_map/ppermute | solution.py:479
  82.6 7.9 %residual.1 = f32[16,48,256]{2,1,0:T(8,128)S(1)} custom-call(s32[8,128]{1,0:T(8,128)S(1)} %route.1.table, s32[16]{0:T(128)S(1)} %select_reduce_fusion.wanted, f32[1024,256]{1,0:T(8,128)S(1)} %get-tuple-element.27.field_ref, f32[1024,256]{1,0:T(8,128)S(1)} %bitcast.14, f32[8,1024,256]{2,1,0:T(8,128)S(1)} %copy-done.2, ...), custom_call_target="tpu_custom_call" | custom-call | tf_op jit(solution)/shard_map/residual/pallas_call | solution.py:563
  90.6 0.9 copy-done.13
  91.5 4.0 %all-to-all-start = ((f32[16,48,256]{2,1,0:T(8,128)}), f32[16,48,256]{2,1,0:T(8,128)S(1)}, u32[]{:S(2)}, u32[]{:S(2)}) async-start(f32[16,48,256]{2,1,0:T(8,128)} %copy-done.13), calls=%async_computation | async-start | bytes 1572864 | tf_op jit(solution)/shard_map/all_to_all | solution.py:570
  95.5 1.0 copy.9
  96.4 12.4 %all-to-all-done.arrived = f32[16,48,256]{2,1,0:T(8,128)S(1)} async-done(((f32[16,48,256]{2,1,0:T(8,128)}), f32[16,48,256]{2,1,0:T(8,128)S(1)}, u32[]{:S(2)}, u32[]{:S(2)}) %all-to-all-start) | async-done | bytes 786464 | tf_op jit(solution)/shard_map/all_to_all | solution.py:570
  108.9 1.4 %place.1 = f32[8,48,256]{2,1,0:T(8,128)} custom-call(s32[8]{0:T(128)S(1)} %copy-done.17, f32[16,48,256]{2,1,0:T(8,128)S(1)} %all-to-all-done.arrived), custom_call_target="tpu_custom_call" | custom-call | tf_op jit(solution)/shard_map/place/pallas_call | solution.py:571
  (29 shorter events, 0.1 us)
Async XLA Ops:
  0.6 0.7 copy-start.16
  3.3 1.2 %copy-start.3 = (f32[64,16,256]{2,1,0:T(8,128)S(1)}, f32[64,16,256]{2,1,0:T(8,128)}, u32[]{:S(2)}) copy-start(f32[64,16,256]{2,1,0:T(8,128)} %param.8) | copy-start | bytes 3145732
  4.6 1.2 %copy-start.9 = (f32[64,16,256]{2,1,0:T(8,128)S(1)}, f32[64,16,256]{2,1,0:T(8,128)}, u32[]{:S(2)}) copy-start(f32[64,16,256]{2,1,0:T(8,128)} %param.6) | copy-start | bytes 3145732
  5.8 72.5 %copy-start.5 = (f32[64,16,256]{2,1,0:T(8,128)S(1)}, f32[64,16,256]{2,1,0:T(8,128)}, u32[]{:S(2)}) copy-start(f32[64,16,256]{2,1,0:T(8,128)} %param.8) | copy-start | bytes 3145732
  7.2 24.8 %collective-permute-start = (f32[32,256]{1,0:T(8,128)S(1)}, f32[32,256]{1,0:T(8,128)S(1)}, u32[]{:S(2)}, u32[]{:S(2)}) collective-permute-start(f32[32,256]{1,0:T(8,128)S(1)} %get-tuple-element.17), channel_id=1, source_target_pairs={{0,8},{8,0},{16,24},{24,16},{32,40},{40,32},{48,56},{56,48},{64,72... | collective-permute-start | bytes 98312 | tf_op jit(solution)/shard_map/ppermute | solution.py:479
  8.9 23.2 %collective-permute-start.1 = (f32[32,256]{1,0:T(8,128)S(1)}, f32[32,256]{1,0:T(8,128)S(1)}, u32[]{:S(2)}, u32[]{:S(2)}) collective-permute-start(f32[32,256]{1,0:T(8,128)S(1)} %get-tuple-element.18), channel_id=1, source_target_pairs={{8,16},{16,8},{24,32},{32,24},{40,48},{48,40},{56,64},{64,56},{72,... | collective-permute-start | bytes 98312 | tf_op jit(solution)/shard_map/ppermute | solution.py:479
  13.4 18.6 %collective-permute-start.2 = (f32[32,256]{1,0:T(8,128)S(1)}, f32[32,256]{1,0:T(8,128)S(1)}, u32[]{:S(2)}, u32[]{:S(2)}) collective-permute-start(f32[32,256]{1,0:T(8,128)S(1)} %get-tuple-element.19), channel_id=1, source_target_pairs={{0,1},{1,0},{2,3},{3,2},{4,5},{5,4},{6,7},{7,6},{8,9},{9,8},{10,11... | collective-permute-start | bytes 98312 | tf_op jit(solution)/shard_map/ppermute | solution.py:479
  13.4 18.6 %collective-permute-start.3 = (f32[32,256]{1,0:T(8,128)S(1)}, f32[32,256]{1,0:T(8,128)S(1)}, u32[]{:S(2)}, u32[]{:S(2)}) collective-permute-start(f32[32,256]{1,0:T(8,128)S(1)} %get-tuple-element.20), channel_id=1, source_target_pairs={{1,2},{2,1},{3,4},{4,3},{5,6},{6,5},{7,0},{0,7},{9,10},{10,9},{11,... | collective-permute-start | bytes 98312 | tf_op jit(solution)/shard_map/ppermute | solution.py:479
  32.0 1.2 %copy-start.4 = (f32[64,16,256]{2,1,0:T(8,128)S(1)}, f32[64,16,256]{2,1,0:T(8,128)}, u32[]{:S(2)}) copy-start(f32[64,16,256]{2,1,0:T(8,128)} %param.8) | copy-start | bytes 3145732
  33.3 1.2 %copy-start.6 = (f32[64,16,256]{2,1,0:T(8,128)S(1)}, f32[64,16,256]{2,1,0:T(8,128)}, u32[]{:S(2)}) copy-start(f32[64,16,256]{2,1,0:T(8,128)} %param.7) | copy-start | bytes 3145732
  34.5 1.2 %copy-start.10 = (f32[64,16,256]{2,1,0:T(8,128)S(1)}, f32[64,16,256]{2,1,0:T(8,128)}, u32[]{:S(2)}) copy-start(f32[64,16,256]{2,1,0:T(8,128)} %param.6) | copy-start | bytes 3145732
  35.7 1.2 %copy-start.11 = (f32[64,16,256]{2,1,0:T(8,128)S(1)}, f32[64,16,256]{2,1,0:T(8,128)}, u32[]{:S(2)}) copy-start(f32[64,16,256]{2,1,0:T(8,128)} %param.9) | copy-start | bytes 3145732
  36.9 45.7 %copy-start.8 = (f32[64,16,256]{2,1,0:T(8,128)S(1)}, f32[64,16,256]{2,1,0:T(8,128)}, u32[]{:S(2)}) copy-start(f32[64,16,256]{2,1,0:T(8,128)} %param.7) | copy-start | bytes 3145732
  46.8 3.3 %copy-start = (f32[8,1024,256]{2,1,0:T(8,128)}, f32[8,1024,256]{2,1,0:T(8,128)S(1)}, u32[]{:S(2)}) copy-start(f32[8,1024,256]{2,1,0:T(8,128)S(1)} %get-tuple-element.22.coef_ref) | copy-start | bytes 25165828
  50.1 1.0 copy-start.14
  51.1 6.2 %collective-permute-start.4 = (f32[16,256]{1,0:T(8,128)S(1)}, f32[16,256]{1,0:T(8,128)S(1)}, u32[]{:S(2)}, u32[]{:S(2)}) collective-permute-start(f32[16,256]{1,0:T(8,128)S(1)} %get-tuple-element.23), channel_id=1, source_target_pairs={{0,8},{8,0},{16,24},{24,16},{32,40},{40,32},{48,56},{56,48},{64,72... | collective-permute-start | bytes 49160 | tf_op jit(solution)/shard_map/ppermute | solution.py:479
  52.1 7.1 %collective-permute-start.5 = (f32[16,256]{1,0:T(8,128)S(1)}, f32[16,256]{1,0:T(8,128)S(1)}, u32[]{:S(2)}, u32[]{:S(2)}) collective-permute-start(f32[16,256]{1,0:T(8,128)S(1)} %get-tuple-element.24), channel_id=1, source_target_pairs={{8,16},{16,8},{24,32},{32,24},{40,48},{48,40},{56,64},{64,56},{72,... | collective-permute-start | bytes 49160 | tf_op jit(solution)/shard_map/ppermute | solution.py:479
  56.6 2.5 %collective-permute-start.6 = (f32[16,256]{1,0:T(8,128)S(1)}, f32[16,256]{1,0:T(8,128)S(1)}, u32[]{:S(2)}, u32[]{:S(2)}) collective-permute-start(f32[16,256]{1,0:T(8,128)S(1)} %get-tuple-element.25), channel_id=1, source_target_pairs={{0,1},{1,0},{2,3},{3,2},{4,5},{5,4},{6,7},{7,6},{8,9},{9,8},{10,11... | collective-permute-start | bytes 49160 | tf_op jit(solution)/shard_map/ppermute | solution.py:479
  56.6 4.4 %collective-permute-start.7 = (f32[16,256]{1,0:T(8,128)S(1)}, f32[16,256]{1,0:T(8,128)S(1)}, u32[]{:S(2)}, u32[]{:S(2)}) collective-permute-start(f32[16,256]{1,0:T(8,128)S(1)} %get-tuple-element.26), channel_id=1, source_target_pairs={{1,2},{2,1},{3,4},{4,3},{5,6},{6,5},{7,0},{0,7},{9,10},{10,9},{11,... | collective-permute-start | bytes 49160 | tf_op jit(solution)/shard_map/ppermute | solution.py:479
  61.0 3.4 %copy-start.1 = (f32[8,1024,256]{2,1,0:T(8,128)S(1)}, f32[8,1024,256]{2,1,0:T(8,128)}, u32[]{:S(2)}) copy-start(f32[8,1024,256]{2,1,0:T(8,128)} %copy-done) | copy-start | bytes 25165828
  64.4 1.2 %copy-start.7 = (f32[64,16,256]{2,1,0:T(8,128)S(1)}, f32[64,16,256]{2,1,0:T(8,128)}, u32[]{:S(2)}) copy-start(f32[64,16,256]{2,1,0:T(8,128)} %param.7) | copy-start | bytes 3145732
  65.6 1.2 %copy-start.15 = (f32[1024,256]{1,0:T(8,128)S(1)}, f32[1024,256]{1,0:T(8,128)}, u32[]{:S(2)}) copy-start(f32[1024,256]{1,0:T(8,128)} %copy-done.14) | copy-start | bytes 3145732
  66.8 15.8 %copy-start.2 = (f32[8,1024,256]{2,1,0:T(8,128)S(1)}, f32[8,1024,256]{2,1,0:T(8,128)}, u32[]{:S(2)}) copy-start(f32[8,1024,256]{2,1,0:T(8,128)} %copy-done) | copy-start | bytes 25165828
  74.9 5.4 %collective-permute-start.10 = (f32[16,256]{1,0:T(8,128)S(1)}, f32[16,256]{1,0:T(8,128)S(1)}, u32[]{:S(2)}, u32[]{:S(2)}) collective-permute-start(f32[16,256]{1,0:T(8,128)S(1)} %get-tuple-element.30), channel_id=1, source_target_pairs={{0,1},{1,0},{2,3},{3,2},{4,5},{5,4},{6,7},{7,6},{8,9},{9,8},{10,11... | collective-permute-start | bytes 49160 | tf_op jit(solution)/shard_map/ppermute | solution.py:479
  75.0 5.3 %collective-permute-start.11 = (f32[16,256]{1,0:T(8,128)S(1)}, f32[16,256]{1,0:T(8,128)S(1)}, u32[]{:S(2)}, u32[]{:S(2)}) collective-permute-start(f32[16,256]{1,0:T(8,128)S(1)} %get-tuple-element.31), channel_id=1, source_target_pairs={{1,2},{2,1},{3,4},{4,3},{5,6},{6,5},{7,0},{0,7},{9,10},{10,9},{11,... | collective-permute-start | bytes 49160 | tf_op jit(solution)/shard_map/ppermute | solution.py:479
  75.6 4.7 %collective-permute-start.8 = (f32[16,256]{1,0:T(8,128)S(1)}, f32[16,256]{1,0:T(8,128)S(1)}, u32[]{:S(2)}, u32[]{:S(2)}) collective-permute-start(f32[16,256]{1,0:T(8,128)S(1)} %get-tuple-element.28), channel_id=1, source_target_pairs={{0,8},{8,0},{16,24},{24,16},{32,40},{40,32},{48,56},{56,48},{64,72... | collective-permute-start | bytes 49160 | tf_op jit(solution)/shard_map/ppermute | solution.py:479
  75.6 7.1 %collective-permute-start.9 = (f32[16,256]{1,0:T(8,128)S(1)}, f32[16,256]{1,0:T(8,128)S(1)}, u32[]{:S(2)}, u32[]{:S(2)}) collective-permute-start(f32[16,256]{1,0:T(8,128)S(1)} %get-tuple-element.29), channel_id=1, source_target_pairs={{8,16},{16,8},{24,32},{32,24},{40,48},{48,40},{56,64},{64,56},{72,... | collective-permute-start | bytes 49160 | tf_op jit(solution)/shard_map/ppermute | solution.py:479
  78.3 1.2 %copy-start.12 = (f32[64,16,256]{2,1,0:T(8,128)S(1)}, f32[64,16,256]{2,1,0:T(8,128)}, u32[]{:S(2)}) copy-start(f32[64,16,256]{2,1,0:T(8,128)} %param.9) | copy-start | bytes 3145732
  79.5 29.3 %copy-start.17 = (s32[8]{0:T(128)S(1)}, s32[8]{0:T(128)}, u32[]{:S(2)}) copy-start(s32[8]{0:T(128)} %coarse_source.1) | copy-start | bytes 100
  90.6 0.9 copy-start.13
  91.5 17.4 %all-to-all-start = ((f32[16,48,256]{2,1,0:T(8,128)}), f32[16,48,256]{2,1,0:T(8,128)S(1)}, u32[]{:S(2)}, u32[]{:S(2)}) async-start(f32[16,48,256]{2,1,0:T(8,128)} %copy-done.13), calls=%async_computation | async-start | bytes 1572864 | tf_op jit(solution)/shard_map/all_to_all | solution.py:570
where the time goes:
time: 111 us; the launch traced here: 110 us
  Pallas kernels  31.4 us (28%)
  starting transfers between devices  23.7 us (21%)
  local copies, waits for them, and re-layouts  23.4 us (21%)
  waiting for transfers between devices  18.5 us (17%)
  blocking collectives  11.7 us (11%)
  between operations  1.62 us (1%)
    unnamed x40, local copies, waits for them, and re-layouts  23.3 us
    ppermute x12, starting transfers between devices, paired(): return lax.ppermute(block, axis, route)  19.7 us
    all_to_all x1, waiting for transfers between devices, body(): lax.all_to_all(send, 'brick', split_axis=0, concat_axis=0, tiled=True)  12.4 us
    unnamed x1, blocking collectives  11.7 us
    pallas_call x1, Pallas kernels, body(): kernel_call(first_kernel, 'first_sweep', [SMEM_SPEC] + [VMEM_SPEC] * 8, (...  9.86 us
    pallas_call x1, Pallas kernels, body(): kernel_call(sweep_kernel, 'next_sweep', [SMEM_SPEC] + [VMEM_SPEC] * 7, (i...  8.04 us
    pallas_call x1, Pallas kernels, body(): kernel_call(residual_kernel, 'residual', [SMEM_SPEC] * 2 + [VMEM_SPEC] *...  7.94 us
    ppermute x12, waiting for transfers between devices, paired(): return lax.ppermute(block, axis, route)  6.09 us
  transfers between devices with their start and end apart: 13, of which 4 were waited for; matrix products, arithmetic and copies ran while one was open for 3% of the time, Pallas kernels for 1%

commit v1 on v0

--- a/solution.py
+++ b/solution.py
@@ -11,6 +11,7 @@
 LZ = 4
 SWEEPS = 2
 OMEGA = 0.8
+UNROLL = 16
 
 SIDE = 16
 PLANE = SIDE * SIDE
@@ -19,16 +20,16 @@
 FACES = 6 * BRK
 COARSE_DEV = BRK // 8
 CAP = 16
+KNOWN_ROWS = 8
+CHUNKS = 4
 PEERS = 4
 ZERO_BRICK = BRK
-MESSAGE_BRICK = BRK + 1
-SLOT_BRICK = MESSAGE_BRICK + PEERS
-EXT_BRICKS = SLOT_BRICK + PEERS * CAP
+EXT_BRICKS = BRK + 1
 SEND_ROW = 6
 ODD_ROW = 7
 F32 = jnp.float32
 I32 = jnp.int32
-VMEM_LIMIT = 40 * 1024 * 1024
+VMEM_LIMIT = 16 * 1024 * 1024
 
 
 def native_place(face):
@@ -56,7 +57,7 @@
     return me, [me + brick_step, me - brick_step, me + sub_step, me - sub_step]
 
 
-def route_kernel(subs, links_ref, table_ref, staged, sem):
+def route(subs, links_ref, table_ref, staged, sem):
     me, peers = peers_of(subs)
     links_row = links_ref[...]
     eye = (row_iota((BRK, BRK)) == lane_iota((BRK, BRK))).astype(F32)
@@ -79,13 +80,13 @@
             floor = jnp.where(there, number * 65536, floor)
         return key, floor
 
-    key_row, floor_row = keyed(links_row, lane_iota((6, BRK)) * 6 + row_iota((6, BRK)))
+    key_row, _ = keyed(links_row, lane_iota((6, BRK)) * 6 + row_iota((6, BRK)))
     key_col, floor_col = keyed(links_col, row_iota((BRK, 6)) * 6 + lane_iota((BRK, 6)))
 
     slot_lane = lane_iota((BRK, BRK))
     brick_sub = row_iota((BRK, BRK))
     listed = jnp.zeros((BRK, BRK), F32)
-    odd = jnp.zeros((1, BRK), F32)
+    odd = jnp.zeros((BRK, 1), F32)
     for face in range(6):
         mine = key_col[:, face : face + 1]
         least = floor_col[:, face : face + 1]
@@ -96,39 +97,23 @@
         rank = jnp.sum(count, axis=1, keepdims=True).astype(I32)
         slot = jnp.where(mine >= 0, (least >> 16) * CAP + rank, -1)
         listed = listed + jnp.where(slot == slot_lane, (brick_sub + (face * BRK + 1)).astype(F32), 0.0)
-        mine = key_row[face : face + 1, :]
-        least = floor_row[face : face + 1, :]
-        count = jnp.zeros((BRK, BRK), F32)
-        for other in range(6):
-            theirs = key_col[:, other : other + 1]
-            count = count + ((theirs < mine) & (theirs >= least)).astype(F32)
-        rank = jnp.sum(count, axis=0, keepdims=True).astype(I32)
         message = least >> 16
-        place = native_place(face)
         if face // 2 == 0:
             plain = message < 2
         elif face // 2 == 2:
             plain = message >= 2
         else:
             plain = message < 0
-        far = mine >= 0
-        odd = odd + (far & jnp.logical_not(plain)).astype(F32)
+        odd = odd + ((mine >= 0) & jnp.logical_not(plain)).astype(F32)
         links = links_row[face : face + 1, :]
         local = links - me * FACES
         near = (links >= 0) & (local >= 0) & (local < FACES)
         near_brick = ((local - (face ^ 1)) * 10923) >> 16
-        far_code = jnp.where(
-            plain,
-            (MESSAGE_BRICK + message) * SIDE + rank,
-            (SLOT_BRICK + message * CAP + rank) * SIDE + place,
-        )
-        code = jnp.where(
-            near, near_brick * SIDE + place, jnp.where(far, far_code, ZERO_BRICK * SIDE)
-        )
+        code = jnp.where(near, near_brick * SIDE + native_place(face), ZERO_BRICK * SIDE)
         staged[face : face + 1, 0:BRK] = code
     staged[SEND_ROW : SEND_ROW + 1, 0:BRK] = jnp.sum(listed, axis=0, keepdims=True).astype(I32) - 1
     staged[ODD_ROW : ODD_ROW + 1, 0:BRK] = jnp.broadcast_to(
-        jnp.sum(odd, axis=1, keepdims=True).astype(I32), (1, BRK)
+        jnp.sum(odd, axis=0, keepdims=True).astype(I32), (1, BRK)
     )
     copy = pltpu.make_async_copy(staged, table_ref, sem)
     copy.start()
@@ -231,17 +216,42 @@
         lax.fori_loop(0, CAP, step, 0)
 
 
-def fill_extended(ext, field_ref, messages, base, table):
+def fill_extended(ext, field_ref):
     ext[0 : BRK * SIDE, :] = field_ref[...]
     ext[ZERO_BRICK * SIDE : (ZERO_BRICK + 1) * SIDE, :] = jnp.zeros((SIDE, PLANE), F32)
-    for message in range(PEERS):
-        at = (MESSAGE_BRICK + message) * SIDE
-        ext[at : at + SIDE, :] = messages[message][base : base + SIDE, :]
+
+
+def from_peers(table, messages, bases, apply):
+    column = lane_iota((SIDE, HALF)) % SIDE
+    for message in range(2):
+        cells = [[messages[message][base : base + SIDE, lanes] for lanes in LANES] for base in bases]
+        for slot in range(CAP):
+            entry = table[SEND_ROW, message * CAP + slot]
+            valid = (entry >= 0) & fits(entry >> 6, message)
+            entry = jnp.where(valid, entry, 0)
+            face = entry >> 6
+            place = face * (SIDE - 1)
+            here = column == jnp.where(valid, place, -1)
+            turn = (place - slot) & (HALF - 1)
+            rows = brick_rows(entry & (BRK - 1))
+            for half, lanes in enumerate(LANES):
+                ghosts = [jnp.where(here, pltpu.roll(part[half], turn, 1), 0.0) for part in cells]
+                apply(face, rows, lanes, ghosts)
+    for message in range(2, PEERS):
+        for slot in range(CAP):
+            entry = table[SEND_ROW, message * CAP + slot]
+            valid = (entry >= 0) & fits(entry >> 6, message)
+            entry = jnp.where(valid, entry, 4 * BRK)
+            face = entry >> 6
+            rows = pl.ds((entry & (BRK - 1)) * SIDE + (face & 1) * (SIDE - 1), 1)
+            ghosts = [
+                jnp.where(valid, messages[message][base + slot : base + slot + 1, :], 0.0) for base in bases
+            ]
+            apply(face, rows, slice(0, PLANE), ghosts)
 
     @pl.when(table[ODD_ROW, 0] > 0)
     def _():
         for message in range(PEERS):
-            at = (MESSAGE_BRICK + message) * SIDE
 
             def step(slot, carry):
                 entry = table[SEND_ROW, message * CAP + slot]
@@ -249,27 +259,32 @@
 
                 @pl.when((entry >= 0) & jnp.logical_not(fits(face, message)))
                 def _():
-                    cells = ext[at : at + SIDE, :]
-                    if message < 2:
-                        compact = compacted(cells, column_rule(slot))
-                    else:
-                        row = jnp.sum(
-                            jnp.where(row_iota((SIDE, PLANE)) == slot, cells, 0.0), axis=0, keepdims=True
-                        )
-                        compact = compacted(jnp.where(band_mask(), row, 0.0), fold_rule)
-                    place = (1 - (face & 1)) * (SIDE - 1)
-                    kind = face >> 1
-                    from_x = spread(compact, column_rule(place))
-                    from_y = spread(compact, lanes_rule(place))
-                    row = jnp.where(band_mask(), spread(compact, fold_rule), 0.0)
-                    from_z = jnp.broadcast_to(jnp.sum(row, axis=0, keepdims=True), (SIDE, PLANE))
-                    ext[brick_rows(SLOT_BRICK + message * CAP + slot), :] = jnp.where(
-                        kind == 0, from_x, jnp.where(kind == 1, from_y, from_z)
-                    )
+                    ghosts = [
+                        aligned(messages[message][base : base + SIDE, :], message, slot, face)
+                        for base in bases
+                    ]
+                    apply(face, brick_rows(entry & (BRK - 1)), slice(0, PLANE), ghosts)
 
                 return carry
 
             lax.fori_loop(0, CAP, step, 0)
+
+
+def aligned(cells, message, slot, face):
+    if message < 2:
+        compact = compacted(cells, column_rule(slot))
+    else:
+        row = jnp.sum(jnp.where(row_iota((SIDE, PLANE)) == slot, cells, 0.0), axis=0, keepdims=True)
+        compact = compacted(jnp.where(band_mask(), row, 0.0), fold_rule)
+    place = (face & 1) * (SIDE - 1)
+    kind = face >> 1
+    from_x = spread(compact, column_rule(place))
+    from_y = spread(compact, lanes_rule(place))
+    row = jnp.where(band_mask(), spread(compact, fold_rule), 0.0)
+    from_z = jnp.where(
+        row_iota((SIDE, PLANE)) == place, jnp.sum(row, axis=0, keepdims=True), 0.0
+    )
+    return jnp.where(kind == 0, from_x, jnp.where(kind == 1, from_y, from_z))
 
 
 def beside(ext, table, brick, low, high):
@@ -331,20 +346,52 @@
 
 
 LANES = (slice(0, HALF), slice(HALF, PLANE))
+
+
+def write_known(known, outs, base):
+    for out in outs[:2]:
+        out[base : base + KNOWN_ROWS, 0:HALF] = known
+        out[base : base + KNOWN_ROWS, HALF:PLANE] = jnp.zeros((KNOWN_ROWS, HALF), F32)
+
+
+def learned(known, messages, base):
+    for message in messages[:2]:
+        known = jnp.maximum(known, message[base : base + KNOWN_ROWS, 0:HALF])
+    return known
 DIAGONAL = 6
-SCALE = 7
-
-
-def pack_kernel(table, field_ref, kappa_ref, *outs):
+
+
+def start_kernel(subs, wishes, links_ref, *refs):
+    arrays, table, loaded, outs, known_ref = refs[:4], refs[4], refs[5:9], refs[9:13], refs[13]
+    staged, table_sem, sems = refs[14:]
+    part = BRK * SIDE // CHUNKS
+    copies = []
+    for number, (array, target) in enumerate(zip(arrays, loaded)):
+        for chunk in range(CHUNKS):
+            rows = pl.ds(chunk * part, part)
+            copies.append(
+                pltpu.make_async_copy(array.at[rows], target.at[rows], sems.at[number * CHUNKS + chunk])
+            )
+            copies[-1].start()
+    lane = lane_iota((KNOWN_ROWS, HALF)) - lax.axis_index("brick") * COARSE_DEV
+    known = jnp.full((KNOWN_ROWS, HALF), -1.0, F32)
+    for slot in range(COARSE_DEV):
+        known = jnp.where(lane == slot, wishes[slot].astype(F32), known)
+    known_ref[...] = known
+    write_known(known, outs, 2 * SIDE)
+    route(subs, links_ref, table, staged, table_sem)
+    for copy in copies[: 2 * CHUNKS]:
+        copy.wait()
     for message in range(PEERS):
-        pack(field_ref, table, message, outs[message], 0)
-        pack(kappa_ref, table, message, outs[message], SIDE)
-
-
-def first_kernel(table, field_ref, kappa_ref, source_ref, decay_ref, m0, m1, m2, m3, new_ref, coef_ref, o0, o1, o2, o3, ext, kappa_ext):
-    messages = (m0, m1, m2, m3)
-    fill_extended(ext, field_ref, messages, 0, table)
-    fill_extended(kappa_ext, kappa_ref, messages, SIDE, table)
+        pack(loaded[0], table, message, outs[message], 0)
+        pack(loaded[1], table, message, outs[message], SIDE)
+    for copy in copies[2 * CHUNKS :]:
+        copy.wait()
+
+
+def links_kernel(table, field_ref, kappa_ref, source_ref, decay_ref, coef_ref, total_ref, ext, kappa_ext):
+    fill_extended(ext, field_ref)
+    fill_extended(kappa_ext, kappa_ref)
 
     def step(brick, carry):
         rows = brick_rows(brick)
@@ -360,19 +407,44 @@
                 coef_ref[face, rows, lanes] = link
                 diagonal = diagonal + link
                 total = total + link * around[face][half]
-            scale = OMEGA / diagonal
             coef_ref[DIAGONAL, rows, lanes] = diagonal
-            coef_ref[SCALE, rows, lanes] = scale
-            new_ref[rows, lanes] = (1.0 - OMEGA) * field[half] + scale * total
+            total_ref[rows, lanes] = total
         return carry
 
-    lax.fori_loop(0, BRK, step, 0)
+    lax.fori_loop(0, BRK, step, 0, unroll=UNROLL)
+
+
+def first_kernel(table, coef_in, total_in, field_ref, known_ref, m0, m1, m2, m3, coef_ref, new_ref, scale_ref, now_known_ref, o0, o1, o2, o3):
+    del coef_in, total_in
+    messages = (m0, m1, m2, m3)
+    known = learned(known_ref[...], messages, 2 * SIDE)
+    now_known_ref[...] = known
+    write_known(known, (o0, o1), SIDE)
+
+    def apply(face, rows, lanes, ghosts):
+        field, kappa = ghosts
+        more = 0.5 * kappa
+        link = coef_ref[face, rows, lanes] + more
+        coef_ref[face, rows, lanes] = link
+        coef_ref[DIAGONAL, rows, lanes] += more
+        new_ref[rows, lanes] += link * field
+
+    from_peers(table, messages, (0, SIDE), apply)
+
+    def step(brick, carry):
+        rows = brick_rows(brick)
+        scale = OMEGA / coef_ref[DIAGONAL, rows, :]
+        scale_ref[rows, :] = scale
+        new_ref[rows, :] = (1.0 - OMEGA) * field_ref[rows, :] + scale * new_ref[rows, :]
+        return carry
+
+    lax.fori_loop(0, BRK, step, 0, unroll=UNROLL)
     for message, out in enumerate((o0, o1, o2, o3)):
         pack(new_ref, table, message, out, 0)
 
 
-def sweep_kernel(table, field_ref, source_ref, coef_ref, m0, m1, m2, m3, new_ref, o0, o1, o2, o3, ext):
-    fill_extended(ext, field_ref, (m0, m1, m2, m3), 0, table)
+def sweep_kernel(table, field_ref, source_ref, coef_ref, scale_ref, new_ref, ext):
+    fill_extended(ext, field_ref)
 
     def step(brick, carry):
         rows = brick_rows(brick)
@@ -382,12 +454,59 @@
             total = source_ref[rows, lanes]
             for face in range(6):
                 total = total + coef_ref[face, rows, lanes] * around[face][half]
-            new_ref[rows, lanes] = (1.0 - OMEGA) * field[half] + coef_ref[SCALE, rows, lanes] * total
+            new_ref[rows, lanes] = (1.0 - OMEGA) * field[half] + scale_ref[rows, lanes] * total
         return carry
 
-    lax.fori_loop(0, BRK, step, 0)
+    lax.fori_loop(0, BRK, step, 0, unroll=UNROLL)
+
+
+def sweep_rest_kernel(table, new_in, coef_ref, scale_ref, known_ref, m0, m1, m2, m3, new_ref, now_known_ref, o0, o1, o2, o3):
+    del new_in
+    messages = (m0, m1, m2, m3)
+    known = learned(known_ref[...], messages, SIDE)
+    now_known_ref[...] = known
+    write_known(known, (o0, o1), SIDE)
+
+    def apply(face, rows, lanes, ghosts):
+        new_ref[rows, lanes] += scale_ref[rows, lanes] * (coef_ref[face, rows, lanes] * ghosts[0])
+
+    from_peers(table, messages, (0,), apply)
     for message, out in enumerate((o0, o1, o2, o3)):
         pack(new_ref, table, message, out, 0)
+
+
+def residual_kernel(table, field_ref, source_ref, coef_ref, left_low, left_high, field_out, ext, sem):
+    copy = pltpu.make_async_copy(field_ref, field_out, sem)
+    copy.start()
+    fill_extended(ext, field_ref)
+
+    def step(brick, carry):
+        rows = brick_rows(brick)
+        field = [ext[rows, lanes] for lanes in LANES]
+        around = beside(ext, table, brick, *field)
+        for half, lanes in enumerate(LANES):
+            total = source_ref[rows, lanes] - coef_ref[DIAGONAL, rows, lanes] * field[half]
+            for face in range(6):
+                total = total + coef_ref[face, rows, lanes] * around[face][half]
+            (left_low, left_high)[half][rows, :] = total
+        return carry
+
+    lax.fori_loop(0, BRK, step, 0, unroll=UNROLL)
+    copy.wait()
+
+
+def residual_rest_kernel(table, low_in, high_in, coef_ref, m0, m1, m2, m3, left_low, left_high, coarse_left):
+    del low_in, high_in
+
+    def apply(face, rows, lanes, ghosts):
+        more = coef_ref[face, rows, lanes] * ghosts[0]
+        if lanes != LANES[1]:
+            left_low[rows, :] += more[:, 0:HALF]
+        if lanes != LANES[0]:
+            left_high[rows, :] += more[:, more.shape[1] - HALF :]
+
+    from_peers(table, (m0, m1, m2, m3), (0,), apply)
+    write_coarse(restricted(left_low, left_high), coarse_left, 0)
 
 
 def restricted(*parts):
@@ -433,30 +552,20 @@
         write_coarse(restricted(low, high), out_ref, base)
 
 
-def residual_kernel(table, wanted, field_ref, source_ref, coef_ref, coarse_ref, m0, m1, m2, m3, send_ref, ext, left_low, left_high, coarse_left):
-    fill_extended(ext, field_ref, (m0, m1, m2, m3), 0, table)
-
-    def step(brick, carry):
-        rows = brick_rows(brick)
-        field = [ext[rows, lanes] for lanes in LANES]
-        around = beside(ext, table, brick, *field)
-        for half, lanes in enumerate(LANES):
-            total = source_ref[rows, lanes] - coef_ref[DIAGONAL, rows, lanes] * field[half]
-            for face in range(6):
-                total = total + coef_ref[face, rows, lanes] * around[face][half]
-            (left_low, left_high)[half][rows, :] = total
-        return carry
-
-    lax.fori_loop(0, BRK, step, 0)
-    write_coarse(restricted(left_low, left_high), coarse_left, 0)
-
-    def hand_over(target, carry):
-        chosen = jnp.maximum(wanted[target], 0)
+def hand_over_kernel(subs, known_ref, e0, e1, m0, m1, coarse_left, coarse_coefs, send_ref, held, wanted, sem):
+    known = learned(jnp.maximum(known_ref[...], jnp.maximum(e0[...], e1[...])), (m0, m1), SIDE)
+    mine = known.astype(I32) - (lax.axis_index("brick") * subs + lax.axis_index("sub")) * COARSE_DEV
+    mine = jnp.where((mine >= 0) & (mine < COARSE_DEV), mine + 1, 0)
+    for reach in (1, 2, 4):
+        mine = mine + pltpu.roll(mine, HALF - reach, 1)
+    held[...] = mine
+    copy = pltpu.make_async_copy(held, wanted, sem)
+    copy.start()
+    copy.wait()
+    for target in range(send_ref.shape[0]):
+        chosen = jnp.maximum(wanted[0, target * COARSE_DEV] - 1, 0)
         send_ref[target, 0:SIDE, :] = coarse_left[chosen]
-        send_ref[target, SIDE : 3 * SIDE, :] = coarse_ref[chosen]
-        return carry
-
-    lax.fori_loop(0, send_ref.shape[0], hand_over, 0)
+        send_ref[target, SIDE : 3 * SIDE, :] = coarse_coefs[chosen]
 
 
 def place_kernel(per_row, coarse_source, arrived, out_ref, sem):
@@ -479,6 +588,11 @@
     return lax.ppermute(block, axis, route)
 
 
+def shifted(block, axis, distance):
+    size = lax.axis_size(axis)
+    return lax.ppermute(block, axis, [(place, (place + distance) % size) for place in range(size)])
+
+
 def exchanged(outgoing):
     return [
         paired(outgoing[0], "brick", 0),
@@ -490,20 +604,21 @@
 
 VMEM_SPEC = pl.BlockSpec(memory_space=pltpu.VMEM)
 SMEM_SPEC = pl.BlockSpec(memory_space=pltpu.SMEM)
-ANY_SPEC = pl.BlockSpec(memory_space=pl.ANY)
+HBM_SPEC = pl.BlockSpec(memory_space=pltpu.HBM)
 
 
 def in_vmem(*shape):
     return pltpu.VMEM(shape, F32)
 
 
-def kernel_call(kernel, name, ins, outs, out_specs=None, scratch=()):
+def kernel_call(kernel, name, ins, outs, out_specs=None, scratch=(), aliases=None):
     return pl.pallas_call(
         kernel,
         out_shape=outs,
         in_specs=ins,
         out_specs=out_specs if out_specs is not None else tuple(VMEM_SPEC for _ in outs),
         scratch_shapes=list(scratch),
+        input_output_aliases=aliases or {},
         compiler_params=pltpu.CompilerParams(vmem_limit_bytes=VMEM_LIMIT),
         name=name,
     )
@@ -515,65 +630,97 @@
     field_start, source, diffusion, decay_rate = (
         array.reshape(rows, PLANE) for array in (field_start, source, diffusion, decay_rate)
     )
-    table = kernel_call(
-        functools.partial(route_kernel, subs),
-        "route",
-        [VMEM_SPEC],
-        jax.ShapeDtypeStruct((8, 128), I32),
-        out_specs=SMEM_SPEC,
-        scratch=[pltpu.VMEM((8, 128), I32), pltpu.SemaphoreType.DMA(())],
-    )(neighbour.T)
-    message = in_vmem(SIDE, PLANE)
-    double = in_vmem(2 * SIDE, PLANE)
+    known_shape = in_vmem(KNOWN_ROWS, HALF)
+    whole = in_vmem(rows, PLANE)
+    message = (in_vmem(SIDE + KNOWN_ROWS, PLANE),) * 2 + (in_vmem(SIDE, PLANE),) * 2
+    double = (in_vmem(2 * SIDE + KNOWN_ROWS, PLANE),) * 2 + (in_vmem(2 * SIDE, PLANE),) * 2
     extended = pltpu.VMEM((EXT_BRICKS * SIDE, PLANE), F32)
 
-    outgoing = kernel_call(
-        pack_kernel, "pack", [SMEM_SPEC] + [VMEM_SPEC] * 2, (double,) * PEERS
-    )(table, field_start, diffusion)
+    table, field_start, diffusion, source, decay_rate, *outgoing, known = kernel_call(
+        functools.partial(start_kernel, subs),
+        "route_and_pack",
+        [SMEM_SPEC, VMEM_SPEC] + [HBM_SPEC] * 4,
+        (jax.ShapeDtypeStruct((8, 128), I32),) + (in_vmem(rows, PLANE),) * 4 + double + (known_shape,),
+        out_specs=(SMEM_SPEC,) + (VMEM_SPEC,) * 9,
+        scratch=[
+            pltpu.VMEM((8, 128), I32),
+            pltpu.SemaphoreType.DMA(()),
+            pltpu.SemaphoreType.DMA((4 * CHUNKS,)),
+        ],
+    )(coarse_source, neighbour.T, *(pltpu.with_memory_space_constraint(a, pltpu.HBM) for a in (field_start, diffusion, source, decay_rate)))
     incoming = exchanged(outgoing)
 
-    me = lax.axis_index("brick") * subs + lax.axis_index("sub")
-    orders = lax.all_gather(coarse_source, "brick")
-    mine = orders - me * COARSE_DEV
-    mine = jnp.where((mine >= 0) & (mine < COARSE_DEV), mine, -1)
-    wanted = jnp.max(mine, axis=1)
     coarse_coefs = kernel_call(
         coefficient_kernel, "coarse_coefficients", [VMEM_SPEC] * 2, (in_vmem(COARSE_DEV, 2 * SIDE, PLANE),),
         scratch=[pltpu.VMEM((rows, HALF), F32), pltpu.VMEM((rows, HALF), F32)],
     )(diffusion, decay_rate)[0]
 
-    field, coefs, *outgoing = kernel_call(
+    coefs, total = kernel_call(
+        links_kernel,
+        "links",
+        [SMEM_SPEC] + [VMEM_SPEC] * 4,
+        (in_vmem(7, rows, PLANE), whole),
+        scratch=[extended, extended],
+    )(table, field_start, diffusion, source, decay_rate)
+    coefs, field, scale, known, *outgoing = kernel_call(
         first_kernel,
         "first_sweep",
         [SMEM_SPEC] + [VMEM_SPEC] * 8,
-        (in_vmem(rows, PLANE), in_vmem(8, rows, PLANE)) + (message,) * PEERS,
-        scratch=[extended, extended],
-    )(table, field_start, diffusion, source, decay_rate, *incoming)
+        (in_vmem(7, rows, PLANE), whole, whole, known_shape) + message,
+        aliases={1: 0, 2: 1},
+    )(table, coefs, total, field_start, known, *incoming)
     incoming = exchanged(outgoing)
     for _ in range(SWEEPS - 1):
-        field, *outgoing = kernel_call(
+        field = kernel_call(
             sweep_kernel,
             "next_sweep",
-            [SMEM_SPEC] + [VMEM_SPEC] * 7,
-            (in_vmem(rows, PLANE),) + (message,) * PEERS,
+            [SMEM_SPEC] + [VMEM_SPEC] * 4,
+            (whole,),
             scratch=[extended],
-        )(table, field, source, coefs, *incoming)
+        )(table, field, source, coefs, scale)[0]
+        field, known, *outgoing = kernel_call(
+            sweep_rest_kernel,
+            "next_sweep_rest",
+            [SMEM_SPEC] + [VMEM_SPEC] * 8,
+            (whole, known_shape) + message,
+            aliases={1: 0},
+        )(table, field, coefs, scale, known, *incoming)
         incoming = exchanged(outgoing)
-    brick_count = lax.axis_size("brick")
-    send = kernel_call(
+    others = [shifted(known, "brick", 6), shifted(known, "brick", -5)]
+    left = in_vmem(rows, HALF)
+    left_low, left_high, field = kernel_call(
         residual_kernel,
         "residual",
-        [SMEM_SPEC] * 2 + [VMEM_SPEC] * 8,
-        (in_vmem(brick_count, 3 * SIDE, PLANE),),
-        scratch=[extended, pltpu.VMEM((rows, HALF), F32), pltpu.VMEM((rows, HALF), F32), pltpu.VMEM((COARSE_DEV, SIDE, PLANE), F32)],
-    )(table, wanted, field, source, coefs, coarse_coefs, *incoming)[0]
+        [SMEM_SPEC] + [VMEM_SPEC] * 3,
+        (left, left, jax.ShapeDtypeStruct((rows, PLANE), F32)),
+        out_specs=(VMEM_SPEC, VMEM_SPEC, HBM_SPEC),
+        scratch=[extended, pltpu.SemaphoreType.DMA(())],
+    )(table, field, source, coefs)
+    _, _, coarse_left = kernel_call(
+        residual_rest_kernel,
+        "residual_rest",
+        [SMEM_SPEC] + [VMEM_SPEC] * 7,
+        (left, left, in_vmem(COARSE_DEV, SIDE, PLANE)),
+        aliases={1: 0, 2: 1},
+    )(table, left_low, left_high, coefs, *incoming)
+    send = kernel_call(
+        functools.partial(hand_over_kernel, subs),
+        "hand_over",
+        [VMEM_SPEC] * 7,
+        (in_vmem(lax.axis_size("brick"), 3 * SIDE, PLANE),),
+        scratch=[
+            pltpu.VMEM((KNOWN_ROWS, HALF), I32),
+            pltpu.SMEM((KNOWN_ROWS, HALF), I32),
+            pltpu.SemaphoreType.DMA(()),
+        ],
+    )(known, *others, *incoming[:2], coarse_left, coarse_coefs)[0]
     arrived = lax.all_to_all(send, "brick", split_axis=0, concat_axis=0, tiled=True)
     moved = kernel_call(
         functools.partial(place_kernel, subs * COARSE_DEV),
         "place",
-        [SMEM_SPEC, ANY_SPEC],
+        [SMEM_SPEC, HBM_SPEC],
         jax.ShapeDtypeStruct((COARSE_DEV, 3 * SIDE, PLANE), F32),
-        out_specs=ANY_SPEC,
+        out_specs=HBM_SPEC,
         scratch=[pltpu.SemaphoreType.DMA((COARSE_DEV,))],
     )(coarse_source, arrived)
     return field.reshape(BRK, SIDE, PLANE), moved.reshape(COARSE_DEV, 3, SIDE, PLANE)

time: 111 us -> 68.1 us (0.61)
  local copies, waits for them, and re-layouts: 23.4 us -> 1.33 us
  waiting for transfers between devices: 18.5 us -> 3.14 us
  blocking collectives: 11.7 us -> 20.2 us
  Pallas kernels: 31.4 us -> 23.9 us
  starting transfers between devices: 23.7 us -> 18.4 us
    unnamed x40 -> x4, local copies, waits for them, and re-layouts: 23.3 us -> 1.33 us
    all_to_all x0 -> x1, blocking collectives: none -> 20.2 us  [body(): lax.all_to_all(send, 'brick', split_axis=0, concat_axis=0, tiled=True)]
    all_to_all x1 -> x0, waiting for transfers between devices: 12.4 us -> none  [body(): lax.all_to_all(send, 'brick', split_axis=0, concat_axis=0, tiled=True)]
    unnamed x1 -> x0, blocking collectives: 11.7 us -> none
    pallas_call x1, Pallas kernels: 9.86 us -> 2.41 us  [body(): kernel_call(first_kernel, 'first_sweep', [SMEM_SPEC] + [VMEM_SPEC] * 8, (...]
    ppermute x12, waiting for transfers between devices: 6.09 us -> 1.93 us  [paired(): return lax.ppermute(block, axis, route)]
    all_to_all x1 -> x0, starting transfers between devices: 3.98 us -> none  [body(): lax.all_to_all(send, 'brick', split_axis=0, concat_axis=0, tiled=True)]
    ppermute x12, starting transfers between devices: 19.7 us -> 16.8 us  [paired(): return lax.ppermute(block, axis, route)]
  transfers between devices with their start and end apart: 13 -> 14, of which waited for: 4 -> 3; matrix products, arithmetic and copies ran while one was open for 3% -> 0% of each run, Pallas kernels for 1% -> 20%
where the time goes in v1:
time: 68.1 us; the launch traced here: 67.9 us
  Pallas kernels  23.9 us (35%)
  blocking collectives  20.2 us (30%)
  starting transfers between devices  18.4 us (27%)
  waiting for transfers between devices  3.14 us (5%)
  local copies, waits for them, and re-layouts  1.33 us (2%)
  between operations  0.95 us (1%)
    all_to_all x1, blocking collectives, body(): lax.all_to_all(send, 'brick', split_axis=0, concat_axis=0, tiled=True)  20.2 us
    ppermute x12, starting transfers between devices, paired(): return lax.ppermute(block, axis, route)  16.8 us
    pallas_call x1, Pallas kernels, body(): kernel_call(links_kernel, 'links', [SMEM_SPEC] + [VMEM_SPEC] * 4, (in_vme...  5.04 us
    pallas_call x1, Pallas kernels, body(): kernel_call(functools.partial(start_kernel, subs), 'route_and_pack', [SME...  4 us
    pallas_call x1, Pallas kernels, body(): kernel_call(residual_kernel, 'residual', [SMEM_SPEC] + [VMEM_SPEC] * 3, (...  3.04 us
    pallas_call x1, Pallas kernels, body(): kernel_call(sweep_kernel, 'next_sweep', [SMEM_SPEC] + [VMEM_SPEC] * 4, (w...  3.01 us
    pallas_call x1, Pallas kernels, body(): kernel_call(first_kernel, 'first_sweep', [SMEM_SPEC] + [VMEM_SPEC] * 8, (...  2.41 us
    ppermute x12, waiting for transfers between devices, paired(): return lax.ppermute(block, axis, route)  1.93 us
  transfers between devices with their start and end apart: 14, of which 3 were waited for; matrix products, arithmetic and copies ran while one was open for 0% of the time, Pallas kernels for 20%

profile of v1, /device:TPU:0, one launch (start us, length us, event | category | flops | bytes accessed | tf_op | source)
XLA Modules:
  0.0 67.9 jit_solution(8957358787180136778)
XLA Ops:
  0.6 0.0 copy-start
  0.6 0.7 copy-done
  1.3 0.0 copy-start.1
  1.3 0.7 copy-done.1
  2.0 4.0 %route_and_pack.1 = (s32[8,128]{1,0:T(8,128)S(1)}, f32[1024,256]{1,0:T(8,128)S(1)}, f32[1024,256]{1,0:T(8,128)S(1)}, f32[1024,256]{1,0:T(8,128)S(1)}, f32[1024,2...) custom-call(s32[8]{0:T(128)S(1)} %copy-done.1, ...), custom_call_target="tpu_custom_call" | custom-call | tf_op jit(solution)/shard_map/route_and_pack/pallas_call | solution.py:639
  6.0 1.7 %collective-permute-start = (f32[40,256]{1,0:T(8,128)S(1)}, f32[40,256]{1,0:T(8,128)S(1)}, u32[]{:S(2)}, u32[]{:S(2)}) collective-permute-start(f32[40,256]{1,0:T(8,128)S(1)} %get-tuple-element.40), channel_id=1, source_target_pairs={{0,8},{8,0},{16,24},{24,16},{32,40},{40,32},{48,56},{56,48},{64,72... | collective-permute-start | bytes 122888 | tf_op jit(solution)/shard_map/ppermute | solution.py:588
  7.6 4.5 %collective-permute-start.1 = (f32[40,256]{1,0:T(8,128)S(1)}, f32[40,256]{1,0:T(8,128)S(1)}, u32[]{:S(2)}, u32[]{:S(2)}) collective-permute-start(f32[40,256]{1,0:T(8,128)S(1)} %get-tuple-element.41), channel_id=1, source_target_pairs={{8,16},{16,8},{24,32},{32,24},{40,48},{48,40},{56,64},{64,56},{72,... | collective-permute-start | bytes 122888 | tf_op jit(solution)/shard_map/ppermute | solution.py:588
  12.2 0.0 collective-permute-start.2
  12.2 4.1 %collective-permute-start.3 = (f32[32,256]{1,0:T(8,128)S(1)}, f32[32,256]{1,0:T(8,128)S(1)}, u32[]{:S(2)}, u32[]{:S(2)}) collective-permute-start(f32[32,256]{1,0:T(8,128)S(1)} %get-tuple-element.43), channel_id=1, source_target_pairs={{1,2},{2,1},{3,4},{4,3},{5,6},{6,5},{7,0},{0,7},{9,10},{10,9},{11,... | collective-permute-start | bytes 98312 | tf_op jit(solution)/shard_map/ppermute | solution.py:588
  16.3 5.0 %links.1 = (f32[7,1024,256]{2,1,0:T(8,128)S(1)}, f32[1024,256]{1,0:T(8,128)S(1)}) custom-call(s32[8,128]{1,0:T(8,128)S(1)} %get-tuple-element.32.table, f32[1024,256]{1,0:T(8,128)S(1)} %get-tuple-element.33.field_ref, f32[1024,256]{1,0:T(8,128)S(1)} %get-tuple-element.34.kappa_ref, f32[1024,256]{1,0:T(8,128)S(1)} %get-tuple-element.35.source_ref, ...), custom_call_target="tpu_custom_call" | custom-call | tf_op jit(solution)/shard_map/links/pallas_call | solution.py:658
  21.4 0.0 collective-permute-done.2.m2
  21.4 0.0 collective-permute-done.3.m3
  21.4 0.0 collective-permute-done.m0
  21.4 0.0 collective-permute-done.1.m1
  21.4 2.4 %first_sweep.1 = (f32[7,1024,256]{2,1,0:T(8,128)S(1)}, f32[1024,256]{1,0:T(8,128)S(1)}, f32[1024,256]{1,0:T(8,128)S(1)}, f32[8,128]{1,0:T(8,128)S(1)}, f32[24,25...) custom-call(s32[8,128]{1,0:T(8,128)S(1)} %get-tuple-element.32.table, ...), custom_call_target="tpu_custom_call", output_to_operand_aliasing={{0}: (1, {}), {1}: (2, {})} | custom-call | tf_op jit(solution)/shard_map/first_sweep/pallas_call | solution.py:665
  23.8 0.1 collective-permute-start.4
  23.9 1.1 %collective-permute-start.5 = (f32[24,256]{1,0:T(8,128)S(1)}, f32[24,256]{1,0:T(8,128)S(1)}, u32[]{:S(2)}, u32[]{:S(2)}) collective-permute-start(f32[24,256]{1,0:T(8,128)S(1)} %get-tuple-element.49), channel_id=1, source_target_pairs={{8,16},{16,8},{24,32},{32,24},{40,48},{48,40},{56,64},{64,56},{72,... | collective-permute-start | bytes 73736 | tf_op jit(solution)/shard_map/ppermute | solution.py:588
  25.1 0.0 collective-permute-start.6
  25.1 1.1 %collective-permute-start.7 = (f32[16,256]{1,0:T(8,128)S(1)}, f32[16,256]{1,0:T(8,128)S(1)}, u32[]{:S(2)}, u32[]{:S(2)}) collective-permute-start(f32[16,256]{1,0:T(8,128)S(1)} %get-tuple-element.51), channel_id=1, source_target_pairs={{1,2},{2,1},{3,4},{4,3},{5,6},{6,5},{7,0},{0,7},{9,10},{10,9},{11,... | collective-permute-start | bytes 49160 | tf_op jit(solution)/shard_map/ppermute | solution.py:588
  26.2 3.0 %next_sweep.1.new_in = f32[1024,256]{1,0:T(8,128)S(1)} custom-call(s32[8,128]{1,0:T(8,128)S(1)} %get-tuple-element.32.table, f32[1024,256]{1,0:T(8,128)S(1)} %get-tuple-element.44.field_ref, f32[1024,256]{1,0:T(8,128)S(1)} %get-tuple-element.35.source_ref, f32[7,1024,256]{2,1,0:T(8,128)S(1)} %get-tuple-element.45.coef_ref, ...), custom_call_target="tpu_custom_call" | custom-call | tf_op jit(solution)/shard_map/next_sweep/pallas_call | solution.py:674
  29.2 0.0 collective-permute-done.6.m2
  29.2 0.2 collective-permute-done.7.m3
  29.5 0.0 collective-permute-done.4.m0
  29.5 1.7 %collective-permute-done.5.m1 = f32[24,256]{1,0:T(8,128)S(1)} collective-permute-done((f32[24,256]{1,0:T(8,128)S(1)}, f32[24,256]{1,0:T(8,128)S(1)}, u32[]{:S(2)}, u32[]{:S(2)}) %collective-permute-start.5) | collective-permute-done | bytes 24608 | tf_op jit(solution)/shard_map/ppermute | solution.py:588
  31.2 1.7 %next_sweep_rest.1 = (f32[1024,256]{1,0:T(8,128)S(1)}, f32[8,128]{1,0:T(8,128)S(1)}, f32[24,256]{1,0:T(8,128)S(1)}, f32[24,256]{1,0:T(8,128)S(1)}, f32[16,256]{1,0:T(8,128)S(1)}, /*index=5*/f32[16,256]{1,0:T(8,128)S(1)}) custom-call(s32[8,128]{1,0:T(8,128)S(1)} %get-tuple-element.32.table, ...), custom_call_target="tpu_custom_call", output_to_operand_aliasing={{0}: (1, {})} | custom-call | tf_op jit(solution)/shard_map/next_sweep_rest/pallas_call | solution.py:681
  32.9 0.1 collective-permute-start.10
  33.0 2.7 %collective-permute-start.11 = (f32[24,256]{1,0:T(8,128)S(1)}, f32[24,256]{1,0:T(8,128)S(1)}, u32[]{:S(2)}, u32[]{:S(2)}) collective-permute-start(f32[24,256]{1,0:T(8,128)S(1)} %get-tuple-element.56), channel_id=1, source_target_pairs={{8,16},{16,8},{24,32},{32,24},{40,48},{48,40},{56,64},{64,56},{72,... | collective-permute-start | bytes 73736 | tf_op jit(solution)/shard_map/ppermute | solution.py:588
  35.6 0.0 collective-permute-start.12
  35.6 1.4 %collective-permute-start.13 = (f32[16,256]{1,0:T(8,128)S(1)}, f32[16,256]{1,0:T(8,128)S(1)}, u32[]{:S(2)}, u32[]{:S(2)}) collective-permute-start(f32[16,256]{1,0:T(8,128)S(1)} %get-tuple-element.60), channel_id=1, source_target_pairs={{1,2},{2,1},{3,4},{4,3},{5,6},{6,5},{7,0},{0,7},{9,10},{10,9},{11,... | collective-permute-start | bytes 49160 | tf_op jit(solution)/shard_map/ppermute | solution.py:588
  37.0 0.8 %collective-permute-start.9 = (f32[8,128]{1,0:T(8,128)S(1)}, f32[8,128]{1,0:T(8,128)S(1)}, u32[]{:S(2)}, u32[]{:S(2)}) collective-permute-start(f32[8,128]{1,0:T(8,128)S(1)} %get-tuple-element.54.known_ref), channel_id=1, source_target_pairs={{0,88},{8,96},{16,104},{24,112},{32,120},{40,0},{48,8},{56,16},{64... | collective-permute-start | bytes 12296 | tf_op jit(solution)/shard_map/ppermute | solution.py:593
  37.8 0.0 collective-permute-done.12.m2
  37.8 0.8 %collective-permute-start.8 = (f32[8,128]{1,0:T(8,128)S(1)}, f32[8,128]{1,0:T(8,128)S(1)}, u32[]{:S(2)}, u32[]{:S(2)}) collective-permute-start(f32[8,128]{1,0:T(8,128)S(1)} %get-tuple-element.54.known_ref), channel_id=1, source_target_pairs={{0,48},{8,56},{16,64},{24,72},{32,80},{40,88},{48,96},{56,104},{64... | collective-permute-start | bytes 12296 | tf_op jit(solution)/shard_map/ppermute | solution.py:593
  38.6 0.8 %coarse_coefficients.1.coarse_coefs = f32[8,32,256]{2,1,0:T(8,128)S(1)} custom-call(f32[1024,256]{1,0:T(8,128)S(1)} %get-tuple-element.34.kappa_ref, f32[1024,256]{1,0:T(8,128)S(1)} %get-tuple-element.36.decay_ref), custom_call_target="tpu_custom_call" | custom-call | tf_op jit(solution)/shard_map/coarse_coefficients/pallas_call | solution.py:653
  39.4 3.0 %residual.1 = (f32[1024,128]{1,0:T(8,128)S(1)}, f32[1024,128]{1,0:T(8,128)S(1)}, f32[1024,256]{1,0:T(8,128)}) custom-call(s32[8,128]{1,0:T(8,128)S(1)} %get-tuple-element.32.table, f32[1024,256]{1,0:T(8,128)S(1)} %get-tuple-element.52.field_ref, f32[1024,256]{1,0:T(8,128)S(1)} %get-tuple-element.35.source_ref, f32[7,1024,256]{2,1,0:T(8,128)S(1)} %get-tuple-element.45.coef_ref), custom_call_target="tpu_custom_call" | custom-call | tf_op jit(solution)/shard_map/residual/pallas_call | solution.py:691
  42.4 0.0 collective-permute-done.13.m3
  42.4 0.0 collective-permute-done.10.m0
  42.4 0.0 collective-permute-done.11.m1
  42.5 1.6 %residual_rest.1 = (f32[1024,128]{1,0:T(8,128)S(1)}, f32[1024,128]{1,0:T(8,128)S(1)}, f32[8,16,256]{2,1,0:T(8,128)S(1)}) custom-call(s32[8,128]{1,0:T(8,128)S(1)} %get-tuple-element.32.table, f32[1024,128]{1,0:T(8,128)S(1)} %get-tuple-element.57.low_in, f32[1024,128]{1,0:T(8,128)S(1)} %get-tuple-element.58.high_in, ...), custom_call_target="tpu_custom_call", output_to_operand_aliasing={{0}: (1, {}), {1}: (2, {})} | custom-call | tf_op jit(solution)/shard_map/residual_rest/pallas_call | solution.py:699
  44.1 0.0 collective-permute-done.9.e1
  44.1 1.2 %collective-permute-done.8.e0 = f32[8,128]{1,0:T(8,128)S(1)} collective-permute-done((f32[8,128]{1,0:T(8,128)S(1)}, f32[8,128]{1,0:T(8,128)S(1)}, u32[]{:S(2)}, u32[]{:S(2)}) %collective-permute-start.8) | collective-permute-done | bytes 4128 | tf_op jit(solution)/shard_map/ppermute | solution.py:593
  45.3 0.9 %hand_over.1 = f32[16,48,256]{2,1,0:T(8,128)S(1)} custom-call(f32[8,128]{1,0:T(8,128)S(1)} %get-tuple-element.54.known_ref, f32[8,128]{1,0:T(8,128)S(1)} %collective-permute-done.8.e0, f32[8,128]{1,0:T(8,128)S(1)} %collective-permute-done.9.e1, f32[24,256]{1,0:T(8,128)S(1)} %collective-permute-done.10.m0, f32[24,256]{1,0:T(8,128)S(1)} %collective-permute-done.11.m1, ...), custom_call_target="tpu_custom_call" | custom-call | tf_op jit(solution)/shard_map/hand_over/pallas_call | solution.py:706
  46.2 20.2 %all_to_all.5.arrived = f32[16,48,256]{2,1,0:T(8,128)S(1)} all-to-all(f32[16,48,256]{2,1,0:T(8,128)S(1)} %hand_over.1), channel_id=1, replica_groups=mesh['brick'=16,'sub'=8] {'brick'}, dimensions={0} | all-to-all | bytes 1572864 | tf_op jit(solution)/shard_map/all_to_all | solution.py:717
  66.4 1.4 %place.1 = f32[8,48,256]{2,1,0:T(8,128)} custom-call(s32[8]{0:T(128)S(1)} %copy-done.1, f32[16,48,256]{2,1,0:T(8,128)S(1)} %all_to_all.5.arrived), custom_call_target="tpu_custom_call" | custom-call | tf_op jit(solution)/shard_map/place/pallas_call | solution.py:718
Async XLA Ops:
  0.6 0.7 %copy-start = (s32[64,6]{0,1:T(8,128)S(1)}, s32[64,6]{0,1:T(8,128)}, u32[]{:S(2)}) copy-start(s32[64,6]{0,1:T(8,128)} %param.10) | copy-start | bytes 4612
  1.3 0.7 copy-start.1
  6.0 15.4 %collective-permute-start = (f32[40,256]{1,0:T(8,128)S(1)}, f32[40,256]{1,0:T(8,128)S(1)}, u32[]{:S(2)}, u32[]{:S(2)}) collective-permute-start(f32[40,256]{1,0:T(8,128)S(1)} %get-tuple-element.40), channel_id=1, source_target_pairs={{0,8},{8,0},{16,24},{24,16},{32,40},{40,32},{48,56},{56,48},{64,72... | collective-permute-start | bytes 122888 | tf_op jit(solution)/shard_map/ppermute | solution.py:588
  7.6 13.8 %collective-permute-start.1 = (f32[40,256]{1,0:T(8,128)S(1)}, f32[40,256]{1,0:T(8,128)S(1)}, u32[]{:S(2)}, u32[]{:S(2)}) collective-permute-start(f32[40,256]{1,0:T(8,128)S(1)} %get-tuple-element.41), channel_id=1, source_target_pairs={{8,16},{16,8},{24,32},{32,24},{40,48},{48,40},{56,64},{64,56},{72,... | collective-permute-start | bytes 122888 | tf_op jit(solution)/shard_map/ppermute | solution.py:588
  12.2 9.2 %collective-permute-start.2 = (f32[32,256]{1,0:T(8,128)S(1)}, f32[32,256]{1,0:T(8,128)S(1)}, u32[]{:S(2)}, u32[]{:S(2)}) collective-permute-start(f32[32,256]{1,0:T(8,128)S(1)} %get-tuple-element.42), channel_id=1, source_target_pairs={{0,1},{1,0},{2,3},{3,2},{4,5},{5,4},{6,7},{7,6},{8,9},{9,8},{10,11... | collective-permute-start | bytes 98312 | tf_op jit(solution)/shard_map/ppermute | solution.py:588
  12.2 9.2 %collective-permute-start.3 = (f32[32,256]{1,0:T(8,128)S(1)}, f32[32,256]{1,0:T(8,128)S(1)}, u32[]{:S(2)}, u32[]{:S(2)}) collective-permute-start(f32[32,256]{1,0:T(8,128)S(1)} %get-tuple-element.43), channel_id=1, source_target_pairs={{1,2},{2,1},{3,4},{4,3},{5,6},{6,5},{7,0},{0,7},{9,10},{10,9},{11,... | collective-permute-start | bytes 98312 | tf_op jit(solution)/shard_map/ppermute | solution.py:588
  23.8 5.6 %collective-permute-start.4 = (f32[24,256]{1,0:T(8,128)S(1)}, f32[24,256]{1,0:T(8,128)S(1)}, u32[]{:S(2)}, u32[]{:S(2)}) collective-permute-start(f32[24,256]{1,0:T(8,128)S(1)} %get-tuple-element.48), channel_id=1, source_target_pairs={{0,8},{8,0},{16,24},{24,16},{32,40},{40,32},{48,56},{56,48},{64,72... | collective-permute-start | bytes 73736 | tf_op jit(solution)/shard_map/ppermute | solution.py:588
  23.9 7.2 %collective-permute-start.5 = (f32[24,256]{1,0:T(8,128)S(1)}, f32[24,256]{1,0:T(8,128)S(1)}, u32[]{:S(2)}, u32[]{:S(2)}) collective-permute-start(f32[24,256]{1,0:T(8,128)S(1)} %get-tuple-element.49), channel_id=1, source_target_pairs={{8,16},{16,8},{24,32},{32,24},{40,48},{48,40},{56,64},{64,56},{72,... | collective-permute-start | bytes 73736 | tf_op jit(solution)/shard_map/ppermute | solution.py:588
  25.1 4.2 %collective-permute-start.6 = (f32[16,256]{1,0:T(8,128)S(1)}, f32[16,256]{1,0:T(8,128)S(1)}, u32[]{:S(2)}, u32[]{:S(2)}) collective-permute-start(f32[16,256]{1,0:T(8,128)S(1)} %get-tuple-element.50), channel_id=1, source_target_pairs={{0,1},{1,0},{2,3},{3,2},{4,5},{5,4},{6,7},{7,6},{8,9},{9,8},{10,11... | collective-permute-start | bytes 49160 | tf_op jit(solution)/shard_map/ppermute | solution.py:588
  25.1 4.4 %collective-permute-start.7 = (f32[16,256]{1,0:T(8,128)S(1)}, f32[16,256]{1,0:T(8,128)S(1)}, u32[]{:S(2)}, u32[]{:S(2)}) collective-permute-start(f32[16,256]{1,0:T(8,128)S(1)} %get-tuple-element.51), channel_id=1, source_target_pairs={{1,2},{2,1},{3,4},{4,3},{5,6},{6,5},{7,0},{0,7},{9,10},{10,9},{11,... | collective-permute-start | bytes 49160 | tf_op jit(solution)/shard_map/ppermute | solution.py:588
  32.9 9.6 %collective-permute-start.10 = (f32[24,256]{1,0:T(8,128)S(1)}, f32[24,256]{1,0:T(8,128)S(1)}, u32[]{:S(2)}, u32[]{:S(2)}) collective-permute-start(f32[24,256]{1,0:T(8,128)S(1)} %get-tuple-element.55), channel_id=1, source_target_pairs={{0,8},{8,0},{16,24},{24,16},{32,40},{40,32},{48,56},{56,48},{64,72... | collective-permute-start | bytes 73736 | tf_op jit(solution)/shard_map/ppermute | solution.py:588
  33.0 9.5 %collective-permute-start.11 = (f32[24,256]{1,0:T(8,128)S(1)}, f32[24,256]{1,0:T(8,128)S(1)}, u32[]{:S(2)}, u32[]{:S(2)}) collective-permute-start(f32[24,256]{1,0:T(8,128)S(1)} %get-tuple-element.56), channel_id=1, source_target_pairs={{8,16},{16,8},{24,32},{32,24},{40,48},{48,40},{56,64},{64,56},{72,... | collective-permute-start | bytes 73736 | tf_op jit(solution)/shard_map/ppermute | solution.py:588
  35.6 2.2 %collective-permute-start.12 = (f32[16,256]{1,0:T(8,128)S(1)}, f32[16,256]{1,0:T(8,128)S(1)}, u32[]{:S(2)}, u32[]{:S(2)}) collective-permute-start(f32[16,256]{1,0:T(8,128)S(1)} %get-tuple-element.59), channel_id=1, source_target_pairs={{0,1},{1,0},{2,3},{3,2},{4,5},{5,4},{6,7},{7,6},{8,9},{9,8},{10,11... | collective-permute-start | bytes 49160 | tf_op jit(solution)/shard_map/ppermute | solution.py:588
  35.6 6.8 %collective-permute-start.13 = (f32[16,256]{1,0:T(8,128)S(1)}, f32[16,256]{1,0:T(8,128)S(1)}, u32[]{:S(2)}, u32[]{:S(2)}) collective-permute-start(f32[16,256]{1,0:T(8,128)S(1)} %get-tuple-element.60), channel_id=1, source_target_pairs={{1,2},{2,1},{3,4},{4,3},{5,6},{6,5},{7,0},{0,7},{9,10},{10,9},{11,... | collective-permute-start | bytes 49160 | tf_op jit(solution)/shard_map/ppermute | solution.py:588
  37.0 7.1 %collective-permute-start.9 = (f32[8,128]{1,0:T(8,128)S(1)}, f32[8,128]{1,0:T(8,128)S(1)}, u32[]{:S(2)}, u32[]{:S(2)}) collective-permute-start(f32[8,128]{1,0:T(8,128)S(1)} %get-tuple-element.54.known_ref), channel_id=1, source_target_pairs={{0,88},{8,96},{16,104},{24,112},{32,120},{40,0},{48,8},{56,16},{64... | collective-permute-start | bytes 12296 | tf_op jit(solution)/shard_map/ppermute | solution.py:593
  37.8 7.5 %collective-permute-start.8 = (f32[8,128]{1,0:T(8,128)S(1)}, f32[8,128]{1,0:T(8,128)S(1)}, u32[]{:S(2)}, u32[]{:S(2)}) collective-permute-start(f32[8,128]{1,0:T(8,128)S(1)} %get-tuple-element.54.known_ref), channel_id=1, source_target_pairs={{0,48},{8,56},{16,64},{24,72},{32,80},{40,88},{48,96},{56,104},{64... | collective-permute-start | bytes 12296 | tf_op jit(solution)/shard_map/ppermute | solution.py:593

commit v2 on v1

--- a/solution.py
+++ b/solution.py
@@ -16,6 +16,7 @@
 SIDE = 16
 PLANE = SIDE * SIDE
 HALF = PLANE // 2
+DEEP = SIDE // 2
 BRK = EDGE * EDGE * LZ
 FACES = 6 * BRK
 COARSE_DEV = BRK // 8
@@ -25,15 +26,12 @@
 PEERS = 4
 ZERO_BRICK = BRK
 EXT_BRICKS = BRK + 1
+LANES = (slice(0, HALF), slice(HALF, PLANE))
 SEND_ROW = 6
 ODD_ROW = 7
 F32 = jnp.float32
 I32 = jnp.int32
 VMEM_LIMIT = 16 * 1024 * 1024
-
-
-def native_place(face):
-    return SIDE - 1 if face % 2 == 0 else 0
 
 
 def lane_iota(shape):
@@ -109,7 +107,7 @@
         local = links - me * FACES
         near = (links >= 0) & (local >= 0) & (local < FACES)
         near_brick = ((local - (face ^ 1)) * 10923) >> 16
-        code = jnp.where(near, near_brick * SIDE + native_place(face), ZERO_BRICK * SIDE)
+        code = jnp.where(near, near_brick, ZERO_BRICK)
         staged[face : face + 1, 0:BRK] = code
     staged[SEND_ROW : SEND_ROW + 1, 0:BRK] = jnp.sum(listed, axis=0, keepdims=True).astype(I32) - 1
     staged[ODD_ROW : ODD_ROW + 1, 0:BRK] = jnp.broadcast_to(
@@ -117,7 +115,7 @@
     )
     copy = pltpu.make_async_copy(staged, table_ref, sem)
     copy.start()
-    copy.wait()
+    return copy
 
 
 def picker(shape, lane_axis, make):
@@ -169,26 +167,35 @@
     return face < 2 if message < 2 else face >= 4
 
 
-def pack(ref, table, message, out_ref, base):
+def pack(fields, table, message, out_ref):
+    entries = [jnp.maximum(table[SEND_ROW, message * CAP + slot], 0) for slot in range(CAP)]
     if message < 2:
         column = lane_iota((SIDE, HALF)) % SIDE
-        low = jnp.zeros((SIDE, HALF), F32)
-        high = jnp.zeros((SIDE, HALF), F32)
-        for slot in range(CAP):
-            entry = jnp.maximum(table[SEND_ROW, message * CAP + slot], 0)
+        parts = [[jnp.zeros((SIDE, HALF), F32)] * 2 for _ in fields]
+        for slot, entry in enumerate(entries):
             rows = brick_rows(entry & (BRK - 1))
             turn = (slot - ((entry >> 6) & 1) * (SIDE - 1)) & (HALF - 1)
             here = column == slot
-            low = jnp.where(here, pltpu.roll(ref[rows, 0:HALF], turn, 1), low)
-            high = jnp.where(here, pltpu.roll(ref[rows, HALF:PLANE], turn, 1), high)
-        out_ref[base : base + SIDE, 0:HALF] = low
-        out_ref[base : base + SIDE, HALF:PLANE] = high
+            for ref, halves in zip(fields, parts):
+                for half, lanes in enumerate(LANES):
+                    halves[half] = jnp.where(here, pltpu.roll(ref[rows, lanes], turn, 1), halves[half])
+        for number, halves in enumerate(parts):
+            for half, lanes in enumerate(LANES):
+                out_ref[number * SIDE : (number + 1) * SIDE, lanes] = halves[half]
     else:
-        for slot in range(CAP):
-            entry = jnp.maximum(table[SEND_ROW, message * CAP + slot], 0)
-            row = (entry & (BRK - 1)) * SIDE + ((entry >> 6) & 1) * (SIDE - 1)
-            out_ref[base + slot : base + slot + 1, :] = ref[pl.ds(row, 1), :]
-
+        found = []
+        for ref in fields:
+            for entry in entries:
+                row = (entry & (BRK - 1)) * SIDE + ((entry >> 6) & 1) * (SIDE - 1)
+                found.append(ref[pl.ds(row, 1), :])
+        for number, row in enumerate(found):
+            out_ref[number : number + 1, :] = row
+
+    for number, ref in enumerate(fields):
+        pack_odd(ref, table, message, out_ref, number * SIDE)
+
+
+def pack_odd(ref, table, message, out_ref, base):
     @pl.when(table[ODD_ROW, 0] > 0)
     def _():
         def step(slot, carry):
@@ -221,33 +228,29 @@
     ext[ZERO_BRICK * SIDE : (ZERO_BRICK + 1) * SIDE, :] = jnp.zeros((SIDE, PLANE), F32)
 
 
-def from_peers(table, messages, bases, apply):
+def from_peers(table, given, apply):
     column = lane_iota((SIDE, HALF)) % SIDE
     for message in range(2):
-        cells = [[messages[message][base : base + SIDE, lanes] for lanes in LANES] for base in bases]
+        cells = [[array[:, lanes] for lanes in LANES] for array in given[message]]
         for slot in range(CAP):
             entry = table[SEND_ROW, message * CAP + slot]
             valid = (entry >= 0) & fits(entry >> 6, message)
             entry = jnp.where(valid, entry, 0)
-            face = entry >> 6
-            place = face * (SIDE - 1)
+            place = (entry >> 6) * (SIDE - 1)
             here = column == jnp.where(valid, place, -1)
             turn = (place - slot) & (HALF - 1)
             rows = brick_rows(entry & (BRK - 1))
             for half, lanes in enumerate(LANES):
-                ghosts = [jnp.where(here, pltpu.roll(part[half], turn, 1), 0.0) for part in cells]
-                apply(face, rows, lanes, ghosts)
+                values = [jnp.where(here, pltpu.roll(part[half], turn, 1), 0.0) for part in cells]
+                apply(rows, lanes, values)
     for message in range(2, PEERS):
         for slot in range(CAP):
             entry = table[SEND_ROW, message * CAP + slot]
             valid = (entry >= 0) & fits(entry >> 6, message)
-            entry = jnp.where(valid, entry, 4 * BRK)
-            face = entry >> 6
-            rows = pl.ds((entry & (BRK - 1)) * SIDE + (face & 1) * (SIDE - 1), 1)
-            ghosts = [
-                jnp.where(valid, messages[message][base + slot : base + slot + 1, :], 0.0) for base in bases
-            ]
-            apply(face, rows, slice(0, PLANE), ghosts)
+            entry = jnp.where(valid, entry, 0)
+            rows = pl.ds((entry & (BRK - 1)) * SIDE + ((entry >> 6) & 1) * (SIDE - 1), 1)
+            values = [jnp.where(valid, array[slot : slot + 1, :], 0.0) for array in given[message]]
+            apply(rows, slice(0, PLANE), values)
 
     @pl.when(table[ODD_ROW, 0] > 0)
     def _():
@@ -259,11 +262,8 @@
 
                 @pl.when((entry >= 0) & jnp.logical_not(fits(face, message)))
                 def _():
-                    ghosts = [
-                        aligned(messages[message][base : base + SIDE, :], message, slot, face)
-                        for base in bases
-                    ]
-                    apply(face, brick_rows(entry & (BRK - 1)), slice(0, PLANE), ghosts)
+                    values = [aligned(array, message, slot, face) for array in given[message]]
+                    apply(brick_rows(entry & (BRK - 1)), slice(0, PLANE), values)
 
                 return carry
 
@@ -290,62 +290,43 @@
 def beside(ext, table, brick, low, high):
     lane = lane_iota((SIDE, HALF))
     column = lane % SIDE
-    row = row_iota((SIDE, HALF))
-
-    def entry(face):
-        code = table[face, brick]
-        return code >> 4, code & (SIDE - 1)
-
-    source, place = entry(0)
-    rows = brick_rows(source)
-    turn = (HALF - place) & (HALF - 1)
+    row = row_iota((DEEP, HALF))
+
+    def across(face):
+        rows = brick_rows(table[face, brick])
+        return ext[rows, 0:HALF], ext[rows, HALF:PLANE]
+
+    def taken(cells, lanes):
+        return jnp.take_along_axis(cells, lanes, axis=1)
+
+    here = column == SIDE - 1
+    lanes = jnp.where(column == 0, lane + (SIDE - 1), lane - 1)
+    x_lower = [taken(jnp.where(here, far, own), lanes) for far, own in zip(across(0), (low, high))]
     here = column == 0
-    x_lower = (
-        jnp.where(here, pltpu.roll(ext[rows, 0:HALF], turn, 1), pltpu.roll(low, 1, 1)),
-        jnp.where(here, pltpu.roll(ext[rows, HALF:PLANE], turn, 1), pltpu.roll(high, 1, 1)),
-    )
-    source, place = entry(1)
-    rows = brick_rows(source)
-    turn = SIDE - 1 - place
-    here = column == SIDE - 1
-    x_upper = (
-        jnp.where(here, pltpu.roll(ext[rows, 0:HALF], turn, 1), pltpu.roll(low, HALF - 1, 1)),
-        jnp.where(here, pltpu.roll(ext[rows, HALF:PLANE], turn, 1), pltpu.roll(high, HALF - 1, 1)),
-    )
-    source, place = entry(2)
-    part = pl.multiple_of((place >> 3) * HALF, HALF)
-    turn = (HALF - (place & 7) * SIDE) & (HALF - 1)
-    ghost = pltpu.roll(ext[brick_rows(source), pl.ds(part, HALF)], turn, 1)
-    turned_low = pltpu.roll(low, SIDE, 1)
-    turned_high = pltpu.roll(high, SIDE, 1)
+    lanes = jnp.where(column == SIDE - 1, lane - (SIDE - 1), lane + 1)
+    x_upper = [taken(jnp.where(here, far, own), lanes) for far, own in zip(across(1), (low, high))]
+    here = lane >= HALF - SIDE
+    y_lower = [
+        pltpu.roll(jnp.where(here, far, own), SIDE, 1)
+        for far, own in ((across(2)[1], low), (low, high))
+    ]
     here = lane < SIDE
-    y_lower = (jnp.where(here, ghost, turned_low), jnp.where(here, turned_low, turned_high))
-    source, place = entry(3)
-    part = pl.multiple_of((place >> 3) * HALF, HALF)
-    turn = HALF - SIDE - (place & 7) * SIDE
-    ghost = pltpu.roll(ext[brick_rows(source), pl.ds(part, HALF)], turn, 1)
-    turned_low = pltpu.roll(low, HALF - SIDE, 1)
-    turned_high = pltpu.roll(high, HALF - SIDE, 1)
-    here = lane >= HALF - SIDE
-    y_upper = (jnp.where(here, turned_high, turned_low), jnp.where(here, ghost, turned_high))
-    source, place = entry(4)
-    ghost = ext[pl.ds(source * SIDE + place, 1), :]
-    here = row == 0
-    z_lower = (
-        jnp.where(here, ghost[:, 0:HALF], pltpu.roll(low, 1, 0)),
-        jnp.where(here, ghost[:, HALF:PLANE], pltpu.roll(high, 1, 0)),
-    )
-    source, place = entry(5)
-    ghost = ext[pl.ds(source * SIDE + place, 1), :]
-    here = row == SIDE - 1
-    z_upper = (
-        jnp.where(here, ghost[:, 0:HALF], pltpu.roll(low, SIDE - 1, 0)),
-        jnp.where(here, ghost[:, HALF:PLANE], pltpu.roll(high, SIDE - 1, 0)),
-    )
+    y_upper = [
+        pltpu.roll(jnp.where(here, far, own), HALF - SIDE, 1)
+        for far, own in ((high, low), (across(3)[0], high))
+    ]
+    below = pl.ds(pl.multiple_of(table[4, brick] * SIDE + DEEP, DEEP), DEEP)
+    above = pl.ds(pl.multiple_of(table[5, brick] * SIDE, DEEP), DEEP)
+    last = row == DEEP - 1
+    first = row == 0
+    z_lower, z_upper = [], []
+    for own, lanes in zip((low, high), LANES):
+        top, bottom = own[0:DEEP], own[DEEP:SIDE]
+        z_lower.append(pltpu.roll(jnp.concatenate([top, jnp.where(last, ext[below, lanes], bottom)], axis=0), 1, 0))
+        z_upper.append(
+            pltpu.roll(jnp.concatenate([jnp.where(first, ext[above, lanes], top), bottom], axis=0), SIDE - 1, 0)
+        )
     return [x_lower, x_upper, y_lower, y_upper, z_lower, z_upper]
-
-
-LANES = (slice(0, HALF), slice(HALF, PLANE))
 
 
 def write_known(known, outs, base):
@@ -354,42 +335,53 @@
         out[base : base + KNOWN_ROWS, HALF:PLANE] = jnp.zeros((KNOWN_ROWS, HALF), F32)
 
 
-def learned(known, messages, base):
+def learned(known, messages, base, others=()):
+    for other in others:
+        known = jnp.maximum(known, other[...])
     for message in messages[:2]:
         known = jnp.maximum(known, message[base : base + KNOWN_ROWS, 0:HALF])
     return known
-DIAGONAL = 6
-
-
-def start_kernel(subs, wishes, links_ref, *refs):
-    arrays, table, loaded, outs, known_ref = refs[:4], refs[4], refs[5:9], refs[9:13], refs[13]
-    staged, table_sem, sems = refs[14:]
+
+
+def chunked_copies(pairs, sems):
     part = BRK * SIDE // CHUNKS
     copies = []
-    for number, (array, target) in enumerate(zip(arrays, loaded)):
-        for chunk in range(CHUNKS):
-            rows = pl.ds(chunk * part, part)
-            copies.append(
-                pltpu.make_async_copy(array.at[rows], target.at[rows], sems.at[number * CHUNKS + chunk])
-            )
-            copies[-1].start()
+    for chunk in range(CHUNKS):
+        rows = pl.ds(chunk * part, part)
+        for array, target in pairs:
+            copies.append(pltpu.make_async_copy(array.at[rows], target.at[rows], sems.at[len(copies)]))
+    return copies
+
+
+def start_kernel(subs, wishes_hbm, links_hbm, field_hbm, kappa_hbm, table, field, kappa, o0, o1, o2, o3, known_ref, staged, wishes, links, wish_sem, link_sem, table_sem, sems):
+    outs = (o0, o1, o2, o3)
+    link_copy = pltpu.make_async_copy(links_hbm, links, link_sem)
+    link_copy.start()
+    wish_copy = pltpu.make_async_copy(wishes_hbm, wishes, wish_sem)
+    wish_copy.start()
+    copies = chunked_copies(((field_hbm, field), (kappa_hbm, kappa)), sems)
+    for copy in copies:
+        copy.start()
+    link_copy.wait()
+    table_copy = route(subs, links, table, staged, table_sem)
+    wish_copy.wait()
     lane = lane_iota((KNOWN_ROWS, HALF)) - lax.axis_index("brick") * COARSE_DEV
     known = jnp.full((KNOWN_ROWS, HALF), -1.0, F32)
     for slot in range(COARSE_DEV):
         known = jnp.where(lane == slot, wishes[slot].astype(F32), known)
     known_ref[...] = known
     write_known(known, outs, 2 * SIDE)
-    route(subs, links_ref, table, staged, table_sem)
-    for copy in copies[: 2 * CHUNKS]:
+    table_copy.wait()
+    for copy in copies:
         copy.wait()
     for message in range(PEERS):
-        pack(loaded[0], table, message, outs[message], 0)
-        pack(loaded[1], table, message, outs[message], SIDE)
-    for copy in copies[2 * CHUNKS :]:
-        copy.wait()
-
-
-def links_kernel(table, field_ref, kappa_ref, source_ref, decay_ref, coef_ref, total_ref, ext, kappa_ext):
+        pack((field, kappa), table, message, outs[message])
+
+
+def links_kernel(table, field_ref, kappa_ref, source_hbm, decay_hbm, coef_ref, diagonal_ref, total_ref, source_ref, decay_ref, ext, kappa_ext, sems):
+    copies = chunked_copies(((source_hbm, source_ref), (decay_hbm, decay_ref)), sems)
+    for copy in copies:
+        copy.start()
     fill_extended(ext, field_ref)
     fill_extended(kappa_ext, kappa_ref)
 
@@ -407,40 +399,47 @@
                 coef_ref[face, rows, lanes] = link
                 diagonal = diagonal + link
                 total = total + link * around[face][half]
-            coef_ref[DIAGONAL, rows, lanes] = diagonal
+            diagonal_ref[rows, lanes] = diagonal
             total_ref[rows, lanes] = total
         return carry
 
-    lax.fori_loop(0, BRK, step, 0, unroll=UNROLL)
-
-
-def first_kernel(table, coef_in, total_in, field_ref, known_ref, m0, m1, m2, m3, coef_ref, new_ref, scale_ref, now_known_ref, o0, o1, o2, o3):
-    del coef_in, total_in
-    messages = (m0, m1, m2, m3)
-    known = learned(known_ref[...], messages, 2 * SIDE)
+    part = BRK // CHUNKS
+    for chunk in range(CHUNKS):
+        for copy in copies[2 * chunk : 2 * chunk + 2]:
+            copy.wait()
+        lax.fori_loop(chunk * part, (chunk + 1) * part, step, 0, unroll=UNROLL)
+
+
+def first_kernel(table, diagonal_in, total_in, field_ref, known_ref, other_ref, own0, own1, own2, own3, m0, m1, m2, m3, diagonal_ref, new_ref, scale_ref, now_known_ref, l0, l1, l2, l3, o0, o1, o2, o3):
+    messages, far_links = (m0, m1, m2, m3), (l0, l1, l2, l3)
+    known = learned(known_ref[...], messages, 2 * SIDE, (other_ref,))
     now_known_ref[...] = known
     write_known(known, (o0, o1), SIDE)
-
-    def apply(face, rows, lanes, ghosts):
-        field, kappa = ghosts
-        more = 0.5 * kappa
-        link = coef_ref[face, rows, lanes] + more
-        coef_ref[face, rows, lanes] = link
-        coef_ref[DIAGONAL, rows, lanes] += more
-        new_ref[rows, lanes] += link * field
-
-    from_peers(table, messages, (0, SIDE), apply)
+    diagonal_ref[...] = diagonal_in[...]
+    new_ref[...] = total_in[...]
+    given = []
+    for own, message, far_link in zip((own0, own1, own2, own3), messages, far_links):
+        kappa = message[SIDE : 2 * SIDE, :]
+        link = 0.5 * (own[SIDE : 2 * SIDE, :] + kappa)
+        far_link[...] = link
+        given.append((link * message[0:SIDE, :], 0.5 * kappa))
+
+    def apply(rows, lanes, more):
+        new_ref[rows, lanes] += more[0]
+        diagonal_ref[rows, lanes] += more[1]
+
+    from_peers(table, given, apply)
 
     def step(brick, carry):
         rows = brick_rows(brick)
-        scale = OMEGA / coef_ref[DIAGONAL, rows, :]
+        scale = OMEGA / diagonal_ref[rows, :]
         scale_ref[rows, :] = scale
         new_ref[rows, :] = (1.0 - OMEGA) * field_ref[rows, :] + scale * new_ref[rows, :]
         return carry
 
     lax.fori_loop(0, BRK, step, 0, unroll=UNROLL)
     for message, out in enumerate((o0, o1, o2, o3)):
-        pack(new_ref, table, message, out, 0)
+        pack((new_ref,), table, message, out)
 
 
 def sweep_kernel(table, field_ref, source_ref, coef_ref, scale_ref, new_ref, ext):
@@ -460,22 +459,23 @@
     lax.fori_loop(0, BRK, step, 0, unroll=UNROLL)
 
 
-def sweep_rest_kernel(table, new_in, coef_ref, scale_ref, known_ref, m0, m1, m2, m3, new_ref, now_known_ref, o0, o1, o2, o3):
-    del new_in
+def sweep_rest_kernel(table, new_in, scale_ref, known_ref, other_ref, l0, l1, l2, l3, m0, m1, m2, m3, new_ref, now_known_ref, o0, o1, o2, o3):
     messages = (m0, m1, m2, m3)
-    known = learned(known_ref[...], messages, SIDE)
+    known = learned(known_ref[...], messages, SIDE, (other_ref,))
     now_known_ref[...] = known
     write_known(known, (o0, o1), SIDE)
-
-    def apply(face, rows, lanes, ghosts):
-        new_ref[rows, lanes] += scale_ref[rows, lanes] * (coef_ref[face, rows, lanes] * ghosts[0])
-
-    from_peers(table, messages, (0,), apply)
+    new_ref[...] = new_in[...]
+    given = [(link[...] * message[0:SIDE, :],) for link, message in zip((l0, l1, l2, l3), messages)]
+
+    def apply(rows, lanes, more):
+        new_ref[rows, lanes] += scale_ref[rows, lanes] * more[0]
+
+    from_peers(table, given, apply)
     for message, out in enumerate((o0, o1, o2, o3)):
-        pack(new_ref, table, message, out, 0)
-
-
-def residual_kernel(table, field_ref, source_ref, coef_ref, left_low, left_high, field_out, ext, sem):
+        pack((new_ref,), table, message, out)
+
+
+def residual_kernel(table, field_ref, source_ref, coef_ref, diagonal_ref, left_low, left_high, field_out, ext, sem):
     copy = pltpu.make_async_copy(field_ref, field_out, sem)
     copy.start()
     fill_extended(ext, field_ref)
@@ -485,7 +485,7 @@
         field = [ext[rows, lanes] for lanes in LANES]
         around = beside(ext, table, brick, *field)
         for half, lanes in enumerate(LANES):
-            total = source_ref[rows, lanes] - coef_ref[DIAGONAL, rows, lanes] * field[half]
+            total = source_ref[rows, lanes] - diagonal_ref[rows, lanes] * field[half]
             for face in range(6):
                 total = total + coef_ref[face, rows, lanes] * around[face][half]
             (left_low, left_high)[half][rows, :] = total
@@ -495,18 +495,34 @@
     copy.wait()
 
 
-def residual_rest_kernel(table, low_in, high_in, coef_ref, m0, m1, m2, m3, left_low, left_high, coarse_left):
-    del low_in, high_in
-
-    def apply(face, rows, lanes, ghosts):
-        more = coef_ref[face, rows, lanes] * ghosts[0]
+def residual_rest_kernel(subs, table, low_in, high_in, known_ref, coarse_coefs, l0, l1, l2, l3, m0, m1, m2, m3, send_ref, left_low, left_high, coarse_left, held, wanted, sem):
+    known = learned(known_ref[...], (m0, m1), SIDE)
+    mine = known.astype(I32) - (lax.axis_index("brick") * subs + lax.axis_index("sub")) * COARSE_DEV
+    mine = jnp.where((mine >= 0) & (mine < COARSE_DEV), mine + 1, 0)
+    for reach in (1, 2, 4):
+        mine = mine + pltpu.roll(mine, HALF - reach, 1)
+    held[...] = mine
+    copy = pltpu.make_async_copy(held, wanted, sem)
+    copy.start()
+
+    left_low[...] = low_in[...]
+    left_high[...] = high_in[...]
+    messages = (m0, m1, m2, m3)
+    given = [(link[...] * message[0:SIDE, :],) for link, message in zip((l0, l1, l2, l3), messages)]
+
+    def apply(rows, lanes, more):
         if lanes != LANES[1]:
-            left_low[rows, :] += more[:, 0:HALF]
+            left_low[rows, :] += more[0][:, 0:HALF]
         if lanes != LANES[0]:
-            left_high[rows, :] += more[:, more.shape[1] - HALF :]
-
-    from_peers(table, (m0, m1, m2, m3), (0,), apply)
+            left_high[rows, :] += more[0][:, more[0].shape[1] - HALF :]
+
+    from_peers(table, given, apply)
     write_coarse(restricted(left_low, left_high), coarse_left, 0)
+    copy.wait()
+    for target in range(send_ref.shape[0]):
+        chosen = jnp.maximum(wanted[0, target * COARSE_DEV] - 1, 0)
+        send_ref[target, 0:SIDE, :] = coarse_left[chosen]
+        send_ref[target, SIDE : 3 * SIDE, :] = coarse_coefs[chosen]
 
 
 def restricted(*parts):
@@ -552,22 +568,6 @@
         write_coarse(restricted(low, high), out_ref, base)
 
 
-def hand_over_kernel(subs, known_ref, e0, e1, m0, m1, coarse_left, coarse_coefs, send_ref, held, wanted, sem):
-    known = learned(jnp.maximum(known_ref[...], jnp.maximum(e0[...], e1[...])), (m0, m1), SIDE)
-    mine = known.astype(I32) - (lax.axis_index("brick") * subs + lax.axis_index("sub")) * COARSE_DEV
-    mine = jnp.where((mine >= 0) & (mine < COARSE_DEV), mine + 1, 0)
-    for reach in (1, 2, 4):
-        mine = mine + pltpu.roll(mine, HALF - reach, 1)
-    held[...] = mine
-    copy = pltpu.make_async_copy(held, wanted, sem)
-    copy.start()
-    copy.wait()
-    for target in range(send_ref.shape[0]):
-        chosen = jnp.maximum(wanted[0, target * COARSE_DEV] - 1, 0)
-        send_ref[target, 0:SIDE, :] = coarse_left[chosen]
-        send_ref[target, SIDE : 3 * SIDE, :] = coarse_coefs[chosen]
-
-
 def place_kernel(per_row, coarse_source, arrived, out_ref, sem):
     copies = [
         pltpu.make_async_copy(arrived.at[coarse_source[slot] // per_row], out_ref.at[slot], sem.at[slot])
@@ -607,18 +607,21 @@
 HBM_SPEC = pl.BlockSpec(memory_space=pltpu.HBM)
 
 
+def in_hbm(array):
+    return pltpu.with_memory_space_constraint(array, pltpu.HBM)
+
+
 def in_vmem(*shape):
     return pltpu.VMEM(shape, F32)
 
 
-def kernel_call(kernel, name, ins, outs, out_specs=None, scratch=(), aliases=None):
+def kernel_call(kernel, name, ins, outs, out_specs=None, scratch=()):
     return pl.pallas_call(
         kernel,
         out_shape=outs,
         in_specs=ins,
         out_specs=out_specs if out_specs is not None else tuple(VMEM_SPEC for _ in outs),
         scratch_shapes=list(scratch),
-        input_output_aliases=aliases or {},
         compiler_params=pltpu.CompilerParams(vmem_limit_bytes=VMEM_LIMIT),
         name=name,
     )
@@ -636,40 +639,47 @@
     double = (in_vmem(2 * SIDE + KNOWN_ROWS, PLANE),) * 2 + (in_vmem(2 * SIDE, PLANE),) * 2
     extended = pltpu.VMEM((EXT_BRICKS * SIDE, PLANE), F32)
 
-    table, field_start, diffusion, source, decay_rate, *outgoing, known = kernel_call(
+    table, field_start, diffusion, *outgoing, known = kernel_call(
         functools.partial(start_kernel, subs),
         "route_and_pack",
-        [SMEM_SPEC, VMEM_SPEC] + [HBM_SPEC] * 4,
-        (jax.ShapeDtypeStruct((8, 128), I32),) + (in_vmem(rows, PLANE),) * 4 + double + (known_shape,),
-        out_specs=(SMEM_SPEC,) + (VMEM_SPEC,) * 9,
+        [HBM_SPEC] * 4,
+        (jax.ShapeDtypeStruct((8, 128), I32),) + (whole,) * 2 + double + (known_shape,),
+        out_specs=(SMEM_SPEC,) + (VMEM_SPEC,) * 7,
         scratch=[
             pltpu.VMEM((8, 128), I32),
+            pltpu.SMEM((COARSE_DEV,), I32),
+            pltpu.VMEM((6, BRK), I32),
             pltpu.SemaphoreType.DMA(()),
-            pltpu.SemaphoreType.DMA((4 * CHUNKS,)),
+            pltpu.SemaphoreType.DMA(()),
+            pltpu.SemaphoreType.DMA(()),
+            pltpu.SemaphoreType.DMA((2 * CHUNKS,)),
         ],
-    )(coarse_source, neighbour.T, *(pltpu.with_memory_space_constraint(a, pltpu.HBM) for a in (field_start, diffusion, source, decay_rate)))
+    )(*(in_hbm(array) for array in (coarse_source, neighbour.T, field_start, diffusion)))
+    own_faces = outgoing
     incoming = exchanged(outgoing)
-
+    bricks_along = lax.axis_size("brick")
+    other = shifted(known, "brick", bricks_along // 2)
+
+    coefs, diagonal, total, source, decay_rate = kernel_call(
+        links_kernel,
+        "links",
+        [SMEM_SPEC] + [VMEM_SPEC] * 2 + [HBM_SPEC] * 2,
+        (in_vmem(6, rows, PLANE),) + (whole,) * 4,
+        scratch=[extended, extended, pltpu.SemaphoreType.DMA((2 * CHUNKS,))],
+    )(table, field_start, diffusion, in_hbm(source), in_hbm(decay_rate))
     coarse_coefs = kernel_call(
         coefficient_kernel, "coarse_coefficients", [VMEM_SPEC] * 2, (in_vmem(COARSE_DEV, 2 * SIDE, PLANE),),
         scratch=[pltpu.VMEM((rows, HALF), F32), pltpu.VMEM((rows, HALF), F32)],
     )(diffusion, decay_rate)[0]
-
-    coefs, total = kernel_call(
-        links_kernel,
-        "links",
-        [SMEM_SPEC] + [VMEM_SPEC] * 4,
-        (in_vmem(7, rows, PLANE), whole),
-        scratch=[extended, extended],
-    )(table, field_start, diffusion, source, decay_rate)
-    coefs, field, scale, known, *outgoing = kernel_call(
+    diagonal, field, scale, known, *rest = kernel_call(
         first_kernel,
         "first_sweep",
-        [SMEM_SPEC] + [VMEM_SPEC] * 8,
-        (in_vmem(7, rows, PLANE), whole, whole, known_shape) + message,
-        aliases={1: 0, 2: 1},
-    )(table, coefs, total, field_start, known, *incoming)
+        [SMEM_SPEC] + [VMEM_SPEC] * 13,
+        (whole, whole, whole, known_shape) + (in_vmem(SIDE, PLANE),) * PEERS + message,
+    )(table, diagonal, total, field_start, known, other, *own_faces, *incoming)
+    far_links, outgoing = rest[:PEERS], rest[PEERS:]
     incoming = exchanged(outgoing)
+    other = shifted(known, "brick", bricks_along // 4)
     for _ in range(SWEEPS - 1):
         field = kernel_call(
             sweep_kernel,
@@ -681,39 +691,33 @@
         field, known, *outgoing = kernel_call(
             sweep_rest_kernel,
             "next_sweep_rest",
-            [SMEM_SPEC] + [VMEM_SPEC] * 8,
+            [SMEM_SPEC] + [VMEM_SPEC] * 12,
             (whole, known_shape) + message,
-            aliases={1: 0},
-        )(table, field, coefs, scale, known, *incoming)
+        )(table, field, scale, known, other, *far_links, *incoming)
         incoming = exchanged(outgoing)
-    others = [shifted(known, "brick", 6), shifted(known, "brick", -5)]
     left = in_vmem(rows, HALF)
     left_low, left_high, field = kernel_call(
         residual_kernel,
         "residual",
-        [SMEM_SPEC] + [VMEM_SPEC] * 3,
+        [SMEM_SPEC] + [VMEM_SPEC] * 4,
         (left, left, jax.ShapeDtypeStruct((rows, PLANE), F32)),
         out_specs=(VMEM_SPEC, VMEM_SPEC, HBM_SPEC),
         scratch=[extended, pltpu.SemaphoreType.DMA(())],
-    )(table, field, source, coefs)
-    _, _, coarse_left = kernel_call(
-        residual_rest_kernel,
+    )(table, field, source, coefs, diagonal)
+    send = kernel_call(
+        functools.partial(residual_rest_kernel, subs),
         "residual_rest",
-        [SMEM_SPEC] + [VMEM_SPEC] * 7,
-        (left, left, in_vmem(COARSE_DEV, SIDE, PLANE)),
-        aliases={1: 0, 2: 1},
-    )(table, left_low, left_high, coefs, *incoming)
-    send = kernel_call(
-        functools.partial(hand_over_kernel, subs),
-        "hand_over",
-        [VMEM_SPEC] * 7,
-        (in_vmem(lax.axis_size("brick"), 3 * SIDE, PLANE),),
+        [SMEM_SPEC] + [VMEM_SPEC] * 12,
+        (in_vmem(bricks_along, 3 * SIDE, PLANE),),
         scratch=[
+            pltpu.VMEM((rows, HALF), F32),
+            pltpu.VMEM((rows, HALF), F32),
+            pltpu.VMEM((COARSE_DEV, SIDE, PLANE), F32),
             pltpu.VMEM((KNOWN_ROWS, HALF), I32),
             pltpu.SMEM((KNOWN_ROWS, HALF), I32),
             pltpu.SemaphoreType.DMA(()),
         ],
-    )(known, *others, *incoming[:2], coarse_left, coarse_coefs)[0]
+    )(table, left_low, left_high, known, coarse_coefs, *far_links, *incoming)[0]
     arrived = lax.all_to_all(send, "brick", split_axis=0, concat_axis=0, tiled=True)
     moved = kernel_call(
         functools.partial(place_kernel, subs * COARSE_DEV),

time: 68.1 us -> 63.3 us (0.930)
  waiting for transfers between devices: 3.14 us -> 1.26 us
  Pallas kernels: 23.9 us -> 22.2 us
  local copies, waits for them, and re-layouts: 1.33 us -> 0.01 us
  blocking collectives: 20.2 us -> 19.1 us
  starting transfers between devices: 18.4 us -> 19.4 us
    ppermute x12, waiting for transfers between devices: 1.93 us -> 0.03 us  [paired(): return lax.ppermute(block, axis, route)]
    pallas_call x6 -> x5, Pallas kernels: 17 us -> 15.7 us  [the longest x1 5.28 us: body(): kernel_call(links_kernel, 'links', [SMEM_SPEC] + [VMEM_SPEC] * 2 + [HBM_S...]
    unnamed x4 -> x2, local copies, waits for them, and re-layouts: 1.33 us -> 0.01 us
    ppermute x12, starting transfers between devices: 16.8 us -> 18.1 us  [paired(): return lax.ppermute(block, axis, route)]
    all_to_all x1, blocking collectives: 20.2 us -> 19.1 us  [body(): lax.all_to_all(send, 'brick', split_axis=0, concat_axis=0, tiled=True)]
  transfers between devices with their start and end apart: 14 -> 14, of which waited for: 3 -> 1; matrix products, arithmetic and copies ran while one was open for 0% -> 0% of each run, Pallas kernels for 20% -> 19%
where the time goes in v2:
time: 63.3 us; the launch traced here: 62.9 us
  Pallas kernels  22.2 us (35%)
  starting transfers between devices  19.4 us (31%)
  blocking collectives  19.1 us (30%)
  waiting for transfers between devices  1.26 us (2%)
  between operations  0.94 us (1%)
    all_to_all x1, blocking collectives, body(): lax.all_to_all(send, 'brick', split_axis=0, concat_axis=0, tiled=True)  19.1 us
    ppermute x12, starting transfers between devices, paired(): return lax.ppermute(block, axis, route)  18.1 us
    pallas_call x1, Pallas kernels, body(): kernel_call(links_kernel, 'links', [SMEM_SPEC] + [VMEM_SPEC] * 2 + [HBM_S...  5.28 us
    pallas_call x1, Pallas kernels, body(): kernel_call(functools.partial(start_kernel, subs), 'route_and_pack', [HBM...  3.82 us
    pallas_call x1, Pallas kernels, body(): kernel_call(sweep_kernel, 'next_sweep', [SMEM_SPEC] + [VMEM_SPEC] * 4, (w...  2.92 us
    pallas_call x1, Pallas kernels, body(): kernel_call(residual_kernel, 'residual', [SMEM_SPEC] + [VMEM_SPEC] * 4, (...  2.85 us
    pallas_call x1, Pallas kernels, body(): kernel_call(first_kernel, 'first_sweep', [SMEM_SPEC] + [VMEM_SPEC] * 13,...  2.01 us
    pallas_call x1, Pallas kernels, body(): kernel_call(functools.partial(residual_rest_kernel, subs), 'residual_rest...  1.69 us
  transfers between devices with their start and end apart: 14, of which 1 were waited for; matrix products, arithmetic and copies ran while one was open for 0% of the time, Pallas kernels for 19%

profile of v2, /device:TPU:0, one launch (start us, length us, event | category | flops | bytes accessed | tf_op | source)
XLA Modules:
  0.0 62.9 jit_solution(6571051813388178265)
XLA Ops:
  0.6 3.8 %route_and_pack.1 = (s32[8,128]{1,0:T(8,128)S(1)}, f32[1024,256]{1,0:T(8,128)S(1)}, f32[1024,256]{1,0:T(8,128)S(1)}, f32[40,256]{1,0:T(8,128)S(1)}, f32[40,256]{...) custom-call(s32[8]{0:T(128)} %coarse_source.1, s32[6,64]{1,0:T(8,128)} %bitcast.12, ...), custom_call_target="tpu_custom_call" | custom-call | tf_op jit(solution)/shard_map/route_and_pack/pallas_call | solution.py:642
  4.5 1.7 %collective-permute-start.1 = (f32[40,256]{1,0:T(8,128)S(1)}, f32[40,256]{1,0:T(8,128)S(1)}, u32[]{:S(2)}, u32[]{:S(2)}) collective-permute-start(f32[40,256]{1,0:T(8,128)S(1)} %get-tuple-element.42.own0), channel_id=1, source_target_pairs={{0,8},{8,0},{16,24},{24,16},{32,40},{40,32},{48,56},{56,48},{64,72... | collective-permute-start | bytes 122888 | tf_op jit(solution)/shard_map/ppermute | solution.py:588
  6.1 4.5 %collective-permute-start.2 = (f32[40,256]{1,0:T(8,128)S(1)}, f32[40,256]{1,0:T(8,128)S(1)}, u32[]{:S(2)}, u32[]{:S(2)}) collective-permute-start(f32[40,256]{1,0:T(8,128)S(1)} %get-tuple-element.43.own1), channel_id=1, source_target_pairs={{8,16},{16,8},{24,32},{32,24},{40,48},{48,40},{56,64},{64,56},{72,... | collective-permute-start | bytes 122888 | tf_op jit(solution)/shard_map/ppermute | solution.py:588
  10.7 0.0 collective-permute-start.3
  10.7 4.1 %collective-permute-start.4 = (f32[32,256]{1,0:T(8,128)S(1)}, f32[32,256]{1,0:T(8,128)S(1)}, u32[]{:S(2)}, u32[]{:S(2)}) collective-permute-start(f32[32,256]{1,0:T(8,128)S(1)} %get-tuple-element.45.own3), channel_id=1, source_target_pairs={{1,2},{2,1},{3,4},{4,3},{5,6},{6,5},{7,0},{0,7},{9,10},{10,9},{11,... | collective-permute-start | bytes 98312 | tf_op jit(solution)/shard_map/ppermute | solution.py:588
  14.8 0.6 %collective-permute-start = (f32[8,128]{1,0:T(8,128)S(1)}, f32[8,128]{1,0:T(8,128)S(1)}, u32[]{:S(2)}, u32[]{:S(2)}) collective-permute-start(f32[8,128]{1,0:T(8,128)S(1)} %get-tuple-element.41.known_ref), channel_id=1, source_target_pairs={{0,64},{8,72},{16,80},{24,88},{32,96},{40,104},{48,112},{56,120},{... | collective-permute-start | bytes 12296 | tf_op jit(solution)/shard_map/ppermute | solution.py:593
  15.4 5.3 %links.1 = (f32[6,1024,256]{2,1,0:T(8,128)S(1)}, f32[1024,256]{1,0:T(8,128)S(1)}, f32[1024,256]{1,0:T(8,128)S(1)}, f32[1024,256]{1,0:T(8,128)S(1)}, f32[1024,256]{1,0:T(8,128)S(1)}) custom-call(s32[8,128]{1,0:T(8,128)S(1)} %get-tuple-element.36.table, f32[1024,256]{1,0:T(8,128)S(1)} %get-tuple-element.37.field_ref, ...), custom_call_target="tpu_custom_call" | custom-call | tf_op jit(solution)/shard_map/links/pallas_call | solution.py:663
  20.7 0.0 collective-permute-done.other_ref
  20.7 0.0 collective-permute-done.3.m2
  20.8 0.0 collective-permute-done.4.m3
  20.8 0.0 collective-permute-done.1.m0
  20.8 0.0 collective-permute-done.2.m1
  20.8 2.0 %first_sweep.1 = (f32[1024,256]{1,0:T(8,128)S(1)}, f32[1024,256]{1,0:T(8,128)S(1)}, f32[1024,256]{1,0:T(8,128)S(1)}, f32[8,128]{1,0:T(8,128)S(1)}, f32[16,256]{1...) custom-call(s32[8,128]{1,0:T(8,128)S(1)} %get-tuple-element.36.table, ...), custom_call_target="tpu_custom_call" | custom-call | tf_op jit(solution)/shard_map/first_sweep/pallas_call | solution.py:674
  22.8 0.8 %collective-permute-start.6 = (f32[24,256]{1,0:T(8,128)S(1)}, f32[24,256]{1,0:T(8,128)S(1)}, u32[]{:S(2)}, u32[]{:S(2)}) collective-permute-start(f32[24,256]{1,0:T(8,128)S(1)} %get-tuple-element.55), channel_id=1, source_target_pairs={{0,8},{8,0},{16,24},{24,16},{32,40},{40,32},{48,56},{56,48},{64,72... | collective-permute-start | bytes 73736 | tf_op jit(solution)/shard_map/ppermute | solution.py:588
  23.6 2.1 %collective-permute-start.7 = (f32[24,256]{1,0:T(8,128)S(1)}, f32[24,256]{1,0:T(8,128)S(1)}, u32[]{:S(2)}, u32[]{:S(2)}) collective-permute-start(f32[24,256]{1,0:T(8,128)S(1)} %get-tuple-element.56), channel_id=1, source_target_pairs={{8,16},{16,8},{24,32},{32,24},{40,48},{48,40},{56,64},{64,56},{72,... | collective-permute-start | bytes 73736 | tf_op jit(solution)/shard_map/ppermute | solution.py:588
  25.7 0.0 collective-permute-start.8
  25.7 0.5 collective-permute-start.9
  26.2 0.7 %collective-permute-start.5 = (f32[8,128]{1,0:T(8,128)S(1)}, f32[8,128]{1,0:T(8,128)S(1)}, u32[]{:S(2)}, u32[]{:S(2)}) collective-permute-start(f32[8,128]{1,0:T(8,128)S(1)} %get-tuple-element.50.known_ref), channel_id=1, source_target_pairs={{0,32},{8,40},{16,48},{24,56},{32,64},{40,72},{48,80},{56,88},{64,... | collective-permute-start | bytes 12296 | tf_op jit(solution)/shard_map/ppermute | solution.py:593
  26.9 2.9 %next_sweep.1.new_in = f32[1024,256]{1,0:T(8,128)S(1)} custom-call(s32[8,128]{1,0:T(8,128)S(1)} %get-tuple-element.36.table, f32[1024,256]{1,0:T(8,128)S(1)} %get-tuple-element.46.field_ref, f32[1024,256]{1,0:T(8,128)S(1)} %get-tuple-element.47.source_ref, f32[6,1024,256]{2,1,0:T(8,128)S(1)} %get-tuple-element.48.coef_ref, ...), custom_call_target="tpu_custom_call" | custom-call | tf_op jit(solution)/shard_map/next_sweep/pallas_call | solution.py:684
  29.8 1.2 %collective-permute-done.5.other_ref = f32[8,128]{1,0:T(8,128)S(1)} collective-permute-done((f32[8,128]{1,0:T(8,128)S(1)}, f32[8,128]{1,0:T(8,128)S(1)}, u32[]{:S(2)}, u32[]{:S(2)}) %collective-permute-start.5) | collective-permute-done | bytes 4128 | tf_op jit(solution)/shard_map/ppermute | solution.py:593
  31.1 0.0 collective-permute-done.8.m2
  31.1 0.0 collective-permute-done.9.m3
  31.1 0.0 collective-permute-done.6.m0
  31.1 0.0 collective-permute-done.7.m1
  31.1 1.5 %next_sweep_rest.1 = (f32[1024,256]{1,0:T(8,128)S(1)}, f32[8,128]{1,0:T(8,128)S(1)}, f32[24,256]{1,0:T(8,128)S(1)}, f32[24,256]{1,0:T(8,128)S(1)}, f32[16,256]{1,0:T(8,128)S(1)}, /*index=5*/f32[16,256]{1,0:T(8,128)S(1)}) custom-call(s32[8,128]{1,0:T(8,128)S(1)} %get-tuple-element.36.table, f32[1024,256]{1,0:T(8,128)S(1)} %next_sweep.1.new_in, ...), custom_call_target="tpu_custom_call" | custom-call | tf_op jit(solution)/shard_map/next_sweep_rest/pallas_call | solution.py:691
  32.6 0.6 collective-permute-start.10
  33.2 2.1 %collective-permute-start.11 = (f32[24,256]{1,0:T(8,128)S(1)}, f32[24,256]{1,0:T(8,128)S(1)}, u32[]{:S(2)}, u32[]{:S(2)}) collective-permute-start(f32[24,256]{1,0:T(8,128)S(1)} %get-tuple-element.67), channel_id=1, source_target_pairs={{8,16},{16,8},{24,32},{32,24},{40,48},{48,40},{56,64},{64,56},{72,... | collective-permute-start | bytes 73736 | tf_op jit(solution)/shard_map/ppermute | solution.py:588
  35.3 0.0 collective-permute-start.12
  35.3 1.6 %collective-permute-start.13 = (f32[16,256]{1,0:T(8,128)S(1)}, f32[16,256]{1,0:T(8,128)S(1)}, u32[]{:S(2)}, u32[]{:S(2)}) collective-permute-start(f32[16,256]{1,0:T(8,128)S(1)} %get-tuple-element.69), channel_id=1, source_target_pairs={{1,2},{2,1},{3,4},{4,3},{5,6},{6,5},{7,0},{0,7},{9,10},{10,9},{11,... | collective-permute-start | bytes 49160 | tf_op jit(solution)/shard_map/ppermute | solution.py:588
  36.9 0.8 %coarse_coefficients.1.coarse_coefs = f32[8,32,256]{2,1,0:T(8,128)S(1)} custom-call(f32[1024,256]{1,0:T(8,128)S(1)} %get-tuple-element.38.kappa_ref, f32[1024,256]{1,0:T(8,128)S(1)} %get-tuple-element.65.decay_ref), custom_call_target="tpu_custom_call" | custom-call | tf_op jit(solution)/shard_map/coarse_coefficients/pallas_call | solution.py:670
  37.7 0.0 copy-start
  37.7 2.9 %residual.1 = (f32[1024,128]{1,0:T(8,128)S(1)}, f32[1024,128]{1,0:T(8,128)S(1)}, f32[1024,256]{1,0:T(8,128)}) custom-call(s32[8,128]{1,0:T(8,128)S(1)} %get-tuple-element.36.table, f32[1024,256]{1,0:T(8,128)S(1)} %get-tuple-element.59.field_ref, f32[1024,256]{1,0:T(8,128)S(1)} %get-tuple-element.47.source_ref, ...), custom_call_target="tpu_custom_call" | custom-call | tf_op jit(solution)/shard_map/residual/pallas_call | solution.py:699
  40.6 0.0 collective-permute-done.12.m2
  40.6 0.0 collective-permute-done.13.m3
  40.6 0.0 collective-permute-done.10.m0
  40.6 0.0 collective-permute-done.11.m1
  40.6 1.7 %residual_rest.1 = f32[16,48,256]{2,1,0:T(8,128)S(1)} custom-call(s32[8,128]{1,0:T(8,128)S(1)} %get-tuple-element.36.table, f32[1024,128]{1,0:T(8,128)S(1)} %get-tuple-element.62.low_in, f32[1024,128]{1,0:T(8,128)S(1)} %get-tuple-element.63.high_in, f32[8,128]{1,0:T(8,128)S(1)} %get-tuple-element.64.known_ref, ...), custom_call_target="tpu_custom_call" | custom-call | tf_op jit(solution)/shard_map/residual_rest/pallas_call | solution.py:707
  42.3 19.1 %all_to_all.5.arrived = f32[16,48,256]{2,1,0:T(8,128)S(1)} all-to-all(f32[16,48,256]{2,1,0:T(8,128)S(1)} %residual_rest.1), channel_id=1, replica_groups=mesh['brick'=16,'sub'=8] {'brick'}, dimensions={0} | all-to-all | bytes 1572864 | tf_op jit(solution)/shard_map/all_to_all | solution.py:721
  61.4 0.0 copy-done
  61.4 1.4 %place.1 = f32[8,48,256]{2,1,0:T(8,128)} custom-call(s32[8]{0:T(128)S(1)} %copy-done, f32[16,48,256]{2,1,0:T(8,128)S(1)} %all_to_all.5.arrived), custom_call_target="tpu_custom_call" | custom-call | tf_op jit(solution)/shard_map/place/pallas_call | solution.py:722
Async XLA Ops:
  4.5 16.3 %collective-permute-start.1 = (f32[40,256]{1,0:T(8,128)S(1)}, f32[40,256]{1,0:T(8,128)S(1)}, u32[]{:S(2)}, u32[]{:S(2)}) collective-permute-start(f32[40,256]{1,0:T(8,128)S(1)} %get-tuple-element.42.own0), channel_id=1, source_target_pairs={{0,8},{8,0},{16,24},{24,16},{32,40},{40,32},{48,56},{56,48},{64,72... | collective-permute-start | bytes 122888 | tf_op jit(solution)/shard_map/ppermute | solution.py:588
  6.1 14.7 %collective-permute-start.2 = (f32[40,256]{1,0:T(8,128)S(1)}, f32[40,256]{1,0:T(8,128)S(1)}, u32[]{:S(2)}, u32[]{:S(2)}) collective-permute-start(f32[40,256]{1,0:T(8,128)S(1)} %get-tuple-element.43.own1), channel_id=1, source_target_pairs={{8,16},{16,8},{24,32},{32,24},{40,48},{48,40},{56,64},{64,56},{72,... | collective-permute-start | bytes 122888 | tf_op jit(solution)/shard_map/ppermute | solution.py:588
  10.7 10.1 %collective-permute-start.3 = (f32[32,256]{1,0:T(8,128)S(1)}, f32[32,256]{1,0:T(8,128)S(1)}, u32[]{:S(2)}, u32[]{:S(2)}) collective-permute-start(f32[32,256]{1,0:T(8,128)S(1)} %get-tuple-element.44.own2), channel_id=1, source_target_pairs={{0,1},{1,0},{2,3},{3,2},{4,5},{5,4},{6,7},{7,6},{8,9},{9,8},{10,11... | collective-permute-start | bytes 98312 | tf_op jit(solution)/shard_map/ppermute | solution.py:588
  10.7 10.1 %collective-permute-start.4 = (f32[32,256]{1,0:T(8,128)S(1)}, f32[32,256]{1,0:T(8,128)S(1)}, u32[]{:S(2)}, u32[]{:S(2)}) collective-permute-start(f32[32,256]{1,0:T(8,128)S(1)} %get-tuple-element.45.own3), channel_id=1, source_target_pairs={{1,2},{2,1},{3,4},{4,3},{5,6},{6,5},{7,0},{0,7},{9,10},{10,9},{11,... | collective-permute-start | bytes 98312 | tf_op jit(solution)/shard_map/ppermute | solution.py:588
  14.8 5.9 %collective-permute-start = (f32[8,128]{1,0:T(8,128)S(1)}, f32[8,128]{1,0:T(8,128)S(1)}, u32[]{:S(2)}, u32[]{:S(2)}) collective-permute-start(f32[8,128]{1,0:T(8,128)S(1)} %get-tuple-element.41.known_ref), channel_id=1, source_target_pairs={{0,64},{8,72},{16,80},{24,88},{32,96},{40,104},{48,112},{56,120},{... | collective-permute-start | bytes 12296 | tf_op jit(solution)/shard_map/ppermute | solution.py:593
  22.8 8.3 %collective-permute-start.6 = (f32[24,256]{1,0:T(8,128)S(1)}, f32[24,256]{1,0:T(8,128)S(1)}, u32[]{:S(2)}, u32[]{:S(2)}) collective-permute-start(f32[24,256]{1,0:T(8,128)S(1)} %get-tuple-element.55), channel_id=1, source_target_pairs={{0,8},{8,0},{16,24},{24,16},{32,40},{40,32},{48,56},{56,48},{64,72... | collective-permute-start | bytes 73736 | tf_op jit(solution)/shard_map/ppermute | solution.py:588
  23.6 7.5 %collective-permute-start.7 = (f32[24,256]{1,0:T(8,128)S(1)}, f32[24,256]{1,0:T(8,128)S(1)}, u32[]{:S(2)}, u32[]{:S(2)}) collective-permute-start(f32[24,256]{1,0:T(8,128)S(1)} %get-tuple-element.56), channel_id=1, source_target_pairs={{8,16},{16,8},{24,32},{32,24},{40,48},{48,40},{56,64},{64,56},{72,... | collective-permute-start | bytes 73736 | tf_op jit(solution)/shard_map/ppermute | solution.py:588
  25.7 5.3 %collective-permute-start.8 = (f32[16,256]{1,0:T(8,128)S(1)}, f32[16,256]{1,0:T(8,128)S(1)}, u32[]{:S(2)}, u32[]{:S(2)}) collective-permute-start(f32[16,256]{1,0:T(8,128)S(1)} %get-tuple-element.57), channel_id=1, source_target_pairs={{0,1},{1,0},{2,3},{3,2},{4,5},{5,4},{6,7},{7,6},{8,9},{9,8},{10,11... | collective-permute-start | bytes 49160 | tf_op jit(solution)/shard_map/ppermute | solution.py:588
  25.7 5.3 %collective-permute-start.9 = (f32[16,256]{1,0:T(8,128)S(1)}, f32[16,256]{1,0:T(8,128)S(1)}, u32[]{:S(2)}, u32[]{:S(2)}) collective-permute-start(f32[16,256]{1,0:T(8,128)S(1)} %get-tuple-element.58), channel_id=1, source_target_pairs={{1,2},{2,1},{3,4},{4,3},{5,6},{6,5},{7,0},{0,7},{9,10},{10,9},{11,... | collective-permute-start | bytes 49160 | tf_op jit(solution)/shard_map/ppermute | solution.py:588
  26.2 4.8 %collective-permute-start.5 = (f32[8,128]{1,0:T(8,128)S(1)}, f32[8,128]{1,0:T(8,128)S(1)}, u32[]{:S(2)}, u32[]{:S(2)}) collective-permute-start(f32[8,128]{1,0:T(8,128)S(1)} %get-tuple-element.50.known_ref), channel_id=1, source_target_pairs={{0,32},{8,40},{16,48},{24,56},{32,64},{40,72},{48,80},{56,88},{64,... | collective-permute-start | bytes 12296 | tf_op jit(solution)/shard_map/ppermute | solution.py:593
  32.6 8.0 %collective-permute-start.10 = (f32[24,256]{1,0:T(8,128)S(1)}, f32[24,256]{1,0:T(8,128)S(1)}, u32[]{:S(2)}, u32[]{:S(2)}) collective-permute-start(f32[24,256]{1,0:T(8,128)S(1)} %get-tuple-element.66), channel_id=1, source_target_pairs={{0,8},{8,0},{16,24},{24,16},{32,40},{40,32},{48,56},{56,48},{64,72... | collective-permute-start | bytes 73736 | tf_op jit(solution)/shard_map/ppermute | solution.py:588
  33.2 7.4 %collective-permute-start.11 = (f32[24,256]{1,0:T(8,128)S(1)}, f32[24,256]{1,0:T(8,128)S(1)}, u32[]{:S(2)}, u32[]{:S(2)}) collective-permute-start(f32[24,256]{1,0:T(8,128)S(1)} %get-tuple-element.67), channel_id=1, source_target_pairs={{8,16},{16,8},{24,32},{32,24},{40,48},{48,40},{56,64},{64,56},{72,... | collective-permute-start | bytes 73736 | tf_op jit(solution)/shard_map/ppermute | solution.py:588
  35.3 5.3 %collective-permute-start.12 = (f32[16,256]{1,0:T(8,128)S(1)}, f32[16,256]{1,0:T(8,128)S(1)}, u32[]{:S(2)}, u32[]{:S(2)}) collective-permute-start(f32[16,256]{1,0:T(8,128)S(1)} %get-tuple-element.68), channel_id=1, source_target_pairs={{0,1},{1,0},{2,3},{3,2},{4,5},{5,4},{6,7},{7,6},{8,9},{9,8},{10,11... | collective-permute-start | bytes 49160 | tf_op jit(solution)/shard_map/ppermute | solution.py:588
  35.3 5.3 %collective-permute-start.13 = (f32[16,256]{1,0:T(8,128)S(1)}, f32[16,256]{1,0:T(8,128)S(1)}, u32[]{:S(2)}, u32[]{:S(2)}) collective-permute-start(f32[16,256]{1,0:T(8,128)S(1)} %get-tuple-element.69), channel_id=1, source_target_pairs={{1,2},{2,1},{3,4},{4,3},{5,6},{6,5},{7,0},{0,7},{9,10},{10,9},{11,... | collective-permute-start | bytes 49160 | tf_op jit(solution)/shard_map/ppermute | solution.py:588
  37.7 23.7 %copy-start = (s32[8]{0:T(128)S(1)}, s32[8]{0:T(128)}, u32[]{:S(2)}) copy-start(s32[8]{0:T(128)} %coarse_source.1) | copy-start | bytes 100

commit v3 on v2

--- a/solution.py
+++ b/solution.py
@@ -55,7 +55,7 @@
     return me, [me + brick_step, me - brick_step, me + sub_step, me - sub_step]
 
 
-def route(subs, links_ref, table_ref, staged, sem):
+def route(subs, links_ref, table_ref, staged, bricks, sem, bricks_sem):
     me, peers = peers_of(subs)
     links_row = links_ref[...]
     eye = (row_iota((BRK, BRK)) == lane_iota((BRK, BRK))).astype(F32)
@@ -103,19 +103,19 @@
         else:
             plain = message < 0
         odd = odd + ((mine >= 0) & jnp.logical_not(plain)).astype(F32)
+    staged[0:1, 0:BRK] = jnp.sum(listed, axis=0, keepdims=True).astype(I32) - 1
+    staged[1:2, 0:BRK] = jnp.broadcast_to(jnp.sum(odd, axis=0, keepdims=True).astype(I32), (1, BRK))
+    copy = pltpu.make_async_copy(staged, table_ref.at[SEND_ROW : SEND_ROW + 2], sem)
+    copy.start()
+    for face in range(6):
         links = links_row[face : face + 1, :]
         local = links - me * FACES
         near = (links >= 0) & (local >= 0) & (local < FACES)
         near_brick = ((local - (face ^ 1)) * 10923) >> 16
-        code = jnp.where(near, near_brick, ZERO_BRICK)
-        staged[face : face + 1, 0:BRK] = code
-    staged[SEND_ROW : SEND_ROW + 1, 0:BRK] = jnp.sum(listed, axis=0, keepdims=True).astype(I32) - 1
-    staged[ODD_ROW : ODD_ROW + 1, 0:BRK] = jnp.broadcast_to(
-        jnp.sum(odd, axis=0, keepdims=True).astype(I32), (1, BRK)
-    )
-    copy = pltpu.make_async_copy(staged, table_ref, sem)
-    copy.start()
-    return copy
+        bricks[face : face + 1, 0:BRK] = jnp.where(near, near_brick, ZERO_BRICK)
+    bricks_copy = pltpu.make_async_copy(bricks, table_ref.at[0:SEND_ROW], bricks_sem)
+    bricks_copy.start()
+    return copy, bricks_copy
 
 
 def picker(shape, lane_axis, make):
@@ -223,9 +223,8 @@
         lax.fori_loop(0, CAP, step, 0)
 
 
-def fill_extended(ext, field_ref):
-    ext[0 : BRK * SIDE, :] = field_ref[...]
-    ext[ZERO_BRICK * SIDE : (ZERO_BRICK + 1) * SIDE, :] = jnp.zeros((SIDE, PLANE), F32)
+def end_extended(ref):
+    ref[BRK * SIDE : EXT_BRICKS * SIDE, :] = jnp.zeros((SIDE, PLANE), F32)
 
 
 def from_peers(table, given, apply):
@@ -301,10 +300,10 @@
 
     here = column == SIDE - 1
     lanes = jnp.where(column == 0, lane + (SIDE - 1), lane - 1)
-    x_lower = [taken(jnp.where(here, far, own), lanes) for far, own in zip(across(0), (low, high))]
+    x_lower = [jnp.where(column == 0, pltpu.roll(far, HALF - SIDE + 1, 1), pltpu.roll(own, 1, 1)) for far, own in zip(across(0), (low, high))]
     here = column == 0
     lanes = jnp.where(column == SIDE - 1, lane - (SIDE - 1), lane + 1)
-    x_upper = [taken(jnp.where(here, far, own), lanes) for far, own in zip(across(1), (low, high))]
+    x_upper = [jnp.where(column == SIDE - 1, pltpu.roll(far, SIDE - 1, 1), pltpu.roll(own, HALF - 1, 1)) for far, own in zip(across(1), (low, high))]
     here = lane >= HALF - SIDE
     y_lower = [
         pltpu.roll(jnp.where(here, far, own), SIDE, 1)
@@ -353,7 +352,7 @@
     return copies
 
 
-def start_kernel(subs, wishes_hbm, links_hbm, field_hbm, kappa_hbm, table, field, kappa, o0, o1, o2, o3, known_ref, staged, wishes, links, wish_sem, link_sem, table_sem, sems):
+def start_kernel(subs, wishes_hbm, links_hbm, field_hbm, kappa_hbm, table, field, kappa, o0, o1, o2, o3, known_ref, staged, bricks, wishes, links, wish_sem, link_sem, table_sem, bricks_sem, sems):
     outs = (o0, o1, o2, o3)
     link_copy = pltpu.make_async_copy(links_hbm, links, link_sem)
     link_copy.start()
@@ -362,8 +361,10 @@
     copies = chunked_copies(((field_hbm, field), (kappa_hbm, kappa)), sems)
     for copy in copies:
         copy.start()
+    end_extended(field)
+    end_extended(kappa)
     link_copy.wait()
-    table_copy = route(subs, links, table, staged, table_sem)
+    table_copy, bricks_copy = route(subs, links, table, staged, bricks, table_sem, bricks_sem)
     wish_copy.wait()
     lane = lane_iota((KNOWN_ROWS, HALF)) - lax.axis_index("brick") * COARSE_DEV
     known = jnp.full((KNOWN_ROWS, HALF), -1.0, F32)
@@ -376,14 +377,13 @@
         copy.wait()
     for message in range(PEERS):
         pack((field, kappa), table, message, outs[message])
-
-
-def links_kernel(table, field_ref, kappa_ref, source_hbm, decay_hbm, coef_ref, diagonal_ref, total_ref, source_ref, decay_ref, ext, kappa_ext, sems):
+    bricks_copy.wait()
+
+
+def links_kernel(table, ext, kappa_ext, source_hbm, decay_hbm, coef_ref, diagonal_ref, total_ref, source_ref, decay_ref, sems):
     copies = chunked_copies(((source_hbm, source_ref), (decay_hbm, decay_ref)), sems)
     for copy in copies:
         copy.start()
-    fill_extended(ext, field_ref)
-    fill_extended(kappa_ext, kappa_ref)
 
     def step(brick, carry):
         rows = brick_rows(brick)
@@ -392,8 +392,7 @@
         around = beside(ext, table, brick, *field)
         kappa_around = beside(kappa_ext, table, brick, *kappa)
         for half, lanes in enumerate(LANES):
-            diagonal = decay_ref[rows, lanes]
-            total = source_ref[rows, lanes]
+            diagonal, total = 0.0, 0.0
             for face in range(6):
                 link = 0.5 * (kappa[half] + kappa_around[face][half])
                 coef_ref[face, rows, lanes] = link
@@ -403,20 +402,19 @@
             total_ref[rows, lanes] = total
         return carry
 
-    part = BRK // CHUNKS
-    for chunk in range(CHUNKS):
-        for copy in copies[2 * chunk : 2 * chunk + 2]:
-            copy.wait()
-        lax.fori_loop(chunk * part, (chunk + 1) * part, step, 0, unroll=UNROLL)
-
-
-def first_kernel(table, diagonal_in, total_in, field_ref, known_ref, other_ref, own0, own1, own2, own3, m0, m1, m2, m3, diagonal_ref, new_ref, scale_ref, now_known_ref, l0, l1, l2, l3, o0, o1, o2, o3):
+    lax.fori_loop(0, BRK, step, 0, unroll=UNROLL)
+    for copy in copies:
+        copy.wait()
+
+
+def first_kernel(table, diagonal_in, total_in, source_ref, decay_ref, field_ref, known_ref, other_ref, own0, own1, own2, own3, m0, m1, m2, m3, diagonal_ref, new_ref, scale_ref, now_known_ref, l0, l1, l2, l3, o0, o1, o2, o3):
     messages, far_links = (m0, m1, m2, m3), (l0, l1, l2, l3)
     known = learned(known_ref[...], messages, 2 * SIDE, (other_ref,))
     now_known_ref[...] = known
     write_known(known, (o0, o1), SIDE)
-    diagonal_ref[...] = diagonal_in[...]
-    new_ref[...] = total_in[...]
+    diagonal_ref[...] = diagonal_in[...] + decay_ref[...]
+    new_ref[0 : BRK * SIDE, :] = total_in[...] + source_ref[...]
+    end_extended(new_ref)
     given = []
     for own, message, far_link in zip((own0, own1, own2, own3), messages, far_links):
         kappa = message[SIDE : 2 * SIDE, :]
@@ -442,9 +440,7 @@
         pack((new_ref,), table, message, out)
 
 
-def sweep_kernel(table, field_ref, source_ref, coef_ref, scale_ref, new_ref, ext):
-    fill_extended(ext, field_ref)
-
+def sweep_kernel(table, ext, source_ref, coef_ref, scale_ref, new_ref):
     def step(brick, carry):
         rows = brick_rows(brick)
         field = [ext[rows, lanes] for lanes in LANES]
@@ -464,7 +460,8 @@
     known = learned(known_ref[...], messages, SIDE, (other_ref,))
     now_known_ref[...] = known
     write_known(known, (o0, o1), SIDE)
-    new_ref[...] = new_in[...]
+    new_ref[0 : BRK * SIDE, :] = new_in[...]
+    end_extended(new_ref)
     given = [(link[...] * message[0:SIDE, :],) for link, message in zip((l0, l1, l2, l3), messages)]
 
     def apply(rows, lanes, more):
@@ -475,10 +472,9 @@
         pack((new_ref,), table, message, out)
 
 
-def residual_kernel(table, field_ref, source_ref, coef_ref, diagonal_ref, left_low, left_high, field_out, ext, sem):
-    copy = pltpu.make_async_copy(field_ref, field_out, sem)
+def residual_kernel(table, ext, source_ref, coef_ref, diagonal_ref, left_low, left_high, field_out, sem):
+    copy = pltpu.make_async_copy(ext.at[0 : BRK * SIDE], field_out, sem)
     copy.start()
-    fill_extended(ext, field_ref)
 
     def step(brick, carry):
         rows = brick_rows(brick)
@@ -563,8 +559,8 @@
 
 def coefficient_kernel(kappa_ref, decay_ref, out_ref, low, high):
     for ref, base in ((kappa_ref, 0), (decay_ref, SIDE)):
-        low[...] = ref[:, 0:HALF]
-        high[...] = ref[:, HALF:PLANE]
+        low[...] = ref[0 : BRK * SIDE, 0:HALF]
+        high[...] = ref[0 : BRK * SIDE, HALF:PLANE]
         write_coarse(restricted(low, high), out_ref, base)
 
 
@@ -635,20 +631,22 @@
     )
     known_shape = in_vmem(KNOWN_ROWS, HALF)
     whole = in_vmem(rows, PLANE)
+    extended = in_vmem(EXT_BRICKS * SIDE, PLANE)
     message = (in_vmem(SIDE + KNOWN_ROWS, PLANE),) * 2 + (in_vmem(SIDE, PLANE),) * 2
     double = (in_vmem(2 * SIDE + KNOWN_ROWS, PLANE),) * 2 + (in_vmem(2 * SIDE, PLANE),) * 2
-    extended = pltpu.VMEM((EXT_BRICKS * SIDE, PLANE), F32)
 
     table, field_start, diffusion, *outgoing, known = kernel_call(
         functools.partial(start_kernel, subs),
         "route_and_pack",
         [HBM_SPEC] * 4,
-        (jax.ShapeDtypeStruct((8, 128), I32),) + (whole,) * 2 + double + (known_shape,),
+        (jax.ShapeDtypeStruct((8, 128), I32),) + (extended,) * 2 + double + (known_shape,),
         out_specs=(SMEM_SPEC,) + (VMEM_SPEC,) * 7,
         scratch=[
-            pltpu.VMEM((8, 128), I32),
+            pltpu.VMEM((2, HALF), I32),
+            pltpu.VMEM((SEND_ROW, HALF), I32),
             pltpu.SMEM((COARSE_DEV,), I32),
             pltpu.VMEM((6, BRK), I32),
+            pltpu.SemaphoreType.DMA(()),
             pltpu.SemaphoreType.DMA(()),
             pltpu.SemaphoreType.DMA(()),
             pltpu.SemaphoreType.DMA(()),
@@ -665,7 +663,7 @@
         "links",
         [SMEM_SPEC] + [VMEM_SPEC] * 2 + [HBM_SPEC] * 2,
         (in_vmem(6, rows, PLANE),) + (whole,) * 4,
-        scratch=[extended, extended, pltpu.SemaphoreType.DMA((2 * CHUNKS,))],
+        scratch=[pltpu.SemaphoreType.DMA((2 * CHUNKS,))],
     )(table, field_start, diffusion, in_hbm(source), in_hbm(decay_rate))
     coarse_coefs = kernel_call(
         coefficient_kernel, "coarse_coefficients", [VMEM_SPEC] * 2, (in_vmem(COARSE_DEV, 2 * SIDE, PLANE),),
@@ -674,9 +672,9 @@
     diagonal, field, scale, known, *rest = kernel_call(
         first_kernel,
         "first_sweep",
-        [SMEM_SPEC] + [VMEM_SPEC] * 13,
-        (whole, whole, whole, known_shape) + (in_vmem(SIDE, PLANE),) * PEERS + message,
-    )(table, diagonal, total, field_start, known, other, *own_faces, *incoming)
+        [SMEM_SPEC] + [VMEM_SPEC] * 15,
+        (whole, extended, whole, known_shape) + (in_vmem(SIDE, PLANE),) * PEERS + message,
+    )(table, diagonal, total, source, decay_rate, field_start, known, other, *own_faces, *incoming)
     far_links, outgoing = rest[:PEERS], rest[PEERS:]
     incoming = exchanged(outgoing)
     other = shifted(known, "brick", bricks_along // 4)
@@ -686,13 +684,12 @@
             "next_sweep",
             [SMEM_SPEC] + [VMEM_SPEC] * 4,
             (whole,),
-            scratch=[extended],
         )(table, field, source, coefs, scale)[0]
         field, known, *outgoing = kernel_call(
             sweep_rest_kernel,
             "next_sweep_rest",
             [SMEM_SPEC] + [VMEM_SPEC] * 12,
-            (whole, known_shape) + message,
+            (extended, known_shape) + message,
         )(table, field, scale, known, other, *far_links, *incoming)
         incoming = exchanged(outgoing)
     left = in_vmem(rows, HALF)
@@ -702,7 +699,7 @@
         [SMEM_SPEC] + [VMEM_SPEC] * 4,
         (left, left, jax.ShapeDtypeStruct((rows, PLANE), F32)),
         out_specs=(VMEM_SPEC, VMEM_SPEC, HBM_SPEC),
-        scratch=[extended, pltpu.SemaphoreType.DMA(())],
+        scratch=[pltpu.SemaphoreType.DMA(())],
     )(table, field, source, coefs, diagonal)
     send = kernel_call(
         functools.partial(residual_rest_kernel, subs),

time: 63.3 us -> 62.7 us (level)
  Pallas kernels: 22.2 us -> 21.2 us
  waiting for transfers between devices: 1.26 us -> 1.9 us
    pallas_call x1, Pallas kernels: 5.28 us -> 4.45 us  [body(): kernel_call(links_kernel, 'links', [SMEM_SPEC] + [VMEM_SPEC] * 2 + [HBM_S...]
  transfers between devices with their start and end apart: 14 -> 14, of which waited for: 1 -> 2; matrix products, arithmetic and copies ran while one was open for 0% -> 0% of each run, Pallas kernels for 19% -> 17%
where the time goes in v3:
time: 62.7 us; the launch traced here: 62.2 us
  Pallas kernels  21.2 us (34%)
  starting transfers between devices  19.1 us (30%)
  blocking collectives  19.1 us (30%)
  waiting for transfers between devices  1.9 us (3%)
  between operations  0.92 us (1%)
    all_to_all x1, blocking collectives, body(): lax.all_to_all(send, 'brick', split_axis=0, concat_axis=0, tiled=True)  19.1 us
    ppermute x12, starting transfers between devices, paired(): return lax.ppermute(block, axis, route)  17.8 us
    pallas_call x1, Pallas kernels, body(): kernel_call(links_kernel, 'links', [SMEM_SPEC] + [VMEM_SPEC] * 2 + [HBM_S...  4.45 us
    pallas_call x1, Pallas kernels, body(): kernel_call(functools.partial(start_kernel, subs), 'route_and_pack', [HBM...  3.87 us
    pallas_call x1, Pallas kernels, body(): kernel_call(residual_kernel, 'residual', [SMEM_SPEC] + [VMEM_SPEC] * 4, (...  2.61 us
    pallas_call x1, Pallas kernels, body(): kernel_call(sweep_kernel, 'next_sweep', [SMEM_SPEC] + [VMEM_SPEC] * 4, (w...  2.61 us
    pallas_call x1, Pallas kernels, body(): kernel_call(first_kernel, 'first_sweep', [SMEM_SPEC] + [VMEM_SPEC] * 15,...  2.12 us
    pallas_call x1, Pallas kernels, body(): kernel_call(functools.partial(residual_rest_kernel, subs), 'residual_rest...  1.67 us
  transfers between devices with their start and end apart: 14, of which 2 were waited for; matrix products, arithmetic and copies ran while one was open for 0% of the time, Pallas kernels for 17%

profile of v3, /device:TPU:0, one launch (start us, length us, event | category | flops | bytes accessed | tf_op | source)
XLA Modules:
  0.0 62.2 jit_solution(17372055356996945042)
XLA Ops:
  0.6 3.9 %route_and_pack.1 = (s32[8,128]{1,0:T(8,128)S(1)}, f32[1040,256]{1,0:T(8,128)S(1)}, f32[1040,256]{1,0:T(8,128)S(1)}, f32[40,256]{1,0:T(8,128)S(1)}, f32[40,256]{...) custom-call(s32[8]{0:T(128)} %coarse_source.1, s32[6,64]{1,0:T(8,128)} %bitcast.12, ...), custom_call_target="tpu_custom_call" | custom-call | tf_op jit(solution)/shard_map/route_and_pack/pallas_call | solution.py:638
  4.5 1.7 %collective-permute-start.1 = (f32[40,256]{1,0:T(8,128)S(1)}, f32[40,256]{1,0:T(8,128)S(1)}, u32[]{:S(2)}, u32[]{:S(2)}) collective-permute-start(f32[40,256]{1,0:T(8,128)S(1)} %get-tuple-element.44.own0), channel_id=1, source_target_pairs={{0,8},{8,0},{16,24},{24,16},{32,40},{40,32},{48,56},{56,48},{64,72... | collective-permute-start | bytes 122888 | tf_op jit(solution)/shard_map/ppermute | solution.py:584
  6.2 4.5 %collective-permute-start.2 = (f32[40,256]{1,0:T(8,128)S(1)}, f32[40,256]{1,0:T(8,128)S(1)}, u32[]{:S(2)}, u32[]{:S(2)}) collective-permute-start(f32[40,256]{1,0:T(8,128)S(1)} %get-tuple-element.45.own1), channel_id=1, source_target_pairs={{8,16},{16,8},{24,32},{32,24},{40,48},{48,40},{56,64},{64,56},{72,... | collective-permute-start | bytes 122888 | tf_op jit(solution)/shard_map/ppermute | solution.py:584
  10.7 0.0 collective-permute-start.3
  10.7 4.1 %collective-permute-start.4 = (f32[32,256]{1,0:T(8,128)S(1)}, f32[32,256]{1,0:T(8,128)S(1)}, u32[]{:S(2)}, u32[]{:S(2)}) collective-permute-start(f32[32,256]{1,0:T(8,128)S(1)} %get-tuple-element.47.own3), channel_id=1, source_target_pairs={{1,2},{2,1},{3,4},{4,3},{5,6},{6,5},{7,0},{0,7},{9,10},{10,9},{11,... | collective-permute-start | bytes 98312 | tf_op jit(solution)/shard_map/ppermute | solution.py:584
  14.9 0.6 %collective-permute-start = (f32[8,128]{1,0:T(8,128)S(1)}, f32[8,128]{1,0:T(8,128)S(1)}, u32[]{:S(2)}, u32[]{:S(2)}) collective-permute-start(f32[8,128]{1,0:T(8,128)S(1)} %get-tuple-element.43.known_ref), channel_id=1, source_target_pairs={{0,64},{8,72},{16,80},{24,88},{32,96},{40,104},{48,112},{56,120},{... | collective-permute-start | bytes 12296 | tf_op jit(solution)/shard_map/ppermute | solution.py:589
  15.5 4.5 %links.1 = (f32[6,1024,256]{2,1,0:T(8,128)S(1)}, f32[1024,256]{1,0:T(8,128)S(1)}, f32[1024,256]{1,0:T(8,128)S(1)}, f32[1024,256]{1,0:T(8,128)S(1)}, f32[1024,256]{1,0:T(8,128)S(1)}) custom-call(s32[8,128]{1,0:T(8,128)S(1)} %get-tuple-element.36.table, f32[1040,256]{1,0:T(8,128)S(1)} %get-tuple-element.37.ext.field_ref, ...), custom_call_target="tpu_custom_call" | custom-call | tf_op jit(solution)/shard_map/links/pallas_call | solution.py:661
  20.0 0.0 collective-permute-done.other_ref
  20.0 0.0 collective-permute-done.3.m2
  20.0 0.0 collective-permute-done.4.m3
  20.0 0.0 collective-permute-done.1.m0
  20.0 0.0 collective-permute-done.2.m1
  20.0 2.1 %first_sweep.1 = (f32[1024,256]{1,0:T(8,128)S(1)}, f32[1040,256]{1,0:T(8,128)S(1)}, f32[1024,256]{1,0:T(8,128)S(1)}, f32[8,128]{1,0:T(8,128)S(1)}, f32[16,256]{1...) custom-call(s32[8,128]{1,0:T(8,128)S(1)} %get-tuple-element.36.table, ...), custom_call_target="tpu_custom_call" | custom-call | tf_op jit(solution)/shard_map/first_sweep/pallas_call | solution.py:672
  22.1 0.8 %collective-permute-start.6 = (f32[24,256]{1,0:T(8,128)S(1)}, f32[24,256]{1,0:T(8,128)S(1)}, u32[]{:S(2)}, u32[]{:S(2)}) collective-permute-start(f32[24,256]{1,0:T(8,128)S(1)} %get-tuple-element.56), channel_id=1, source_target_pairs={{0,8},{8,0},{16,24},{24,16},{32,40},{40,32},{48,56},{56,48},{64,72... | collective-permute-start | bytes 73736 | tf_op jit(solution)/shard_map/ppermute | solution.py:584
  22.9 2.2 %collective-permute-start.7 = (f32[24,256]{1,0:T(8,128)S(1)}, f32[24,256]{1,0:T(8,128)S(1)}, u32[]{:S(2)}, u32[]{:S(2)}) collective-permute-start(f32[24,256]{1,0:T(8,128)S(1)} %get-tuple-element.57), channel_id=1, source_target_pairs={{8,16},{16,8},{24,32},{32,24},{40,48},{48,40},{56,64},{64,56},{72,... | collective-permute-start | bytes 73736 | tf_op jit(solution)/shard_map/ppermute | solution.py:584
  25.1 0.0 collective-permute-start.8
  25.1 0.5 collective-permute-start.9
  25.6 0.7 %collective-permute-start.5 = (f32[8,128]{1,0:T(8,128)S(1)}, f32[8,128]{1,0:T(8,128)S(1)}, u32[]{:S(2)}, u32[]{:S(2)}) collective-permute-start(f32[8,128]{1,0:T(8,128)S(1)} %get-tuple-element.51.known_ref), channel_id=1, source_target_pairs={{0,32},{8,40},{16,48},{24,56},{32,64},{40,72},{48,80},{56,88},{64,... | collective-permute-start | bytes 12296 | tf_op jit(solution)/shard_map/ppermute | solution.py:589
  26.2 2.6 %next_sweep.1.new_in = f32[1024,256]{1,0:T(8,128)S(1)} custom-call(s32[8,128]{1,0:T(8,128)S(1)} %get-tuple-element.36.table, f32[1040,256]{1,0:T(8,128)S(1)} %get-tuple-element.48.ext, f32[1024,256]{1,0:T(8,128)S(1)} %get-tuple-element.41.source_ref, f32[6,1024,256]{2,1,0:T(8,128)S(1)} %get-tuple-element.49.coef_ref, f32[1024,256]{1,0:T(8,128)S(1)} %get-tuple-element.50.scale_ref), custom_call_target="tpu_custom_call" | custom-call | tf_op jit(solution)/shard_map/next_sweep/pallas_call | solution.py:682
  28.8 1.5 %collective-permute-done.5.other_ref = f32[8,128]{1,0:T(8,128)S(1)} collective-permute-done((f32[8,128]{1,0:T(8,128)S(1)}, f32[8,128]{1,0:T(8,128)S(1)}, u32[]{:S(2)}, u32[]{:S(2)}) %collective-permute-start.5) | collective-permute-done | bytes 4128 | tf_op jit(solution)/shard_map/ppermute | solution.py:589
  30.4 0.0 collective-permute-done.8.m2
  30.4 0.0 collective-permute-done.9.m3
  30.4 0.0 collective-permute-done.6.m0
  30.4 0.0 collective-permute-done.7.m1
  30.4 1.7 %next_sweep_rest.1 = (f32[1040,256]{1,0:T(8,128)S(1)}, f32[8,128]{1,0:T(8,128)S(1)}, f32[24,256]{1,0:T(8,128)S(1)}, f32[24,256]{1,0:T(8,128)S(1)}, f32[16,256]{1,0:T(8,128)S(1)}, /*index=5*/f32[16,256]{1,0:T(8,128)S(1)}) custom-call(s32[8,128]{1,0:T(8,128)S(1)} %get-tuple-element.36.table, f32[1024,256]{1,0:T(8,128)S(1)} %next_sweep.1.new_in, ...), custom_call_target="tpu_custom_call" | custom-call | tf_op jit(solution)/shard_map/next_sweep_rest/pallas_call | solution.py:688
  32.1 0.6 collective-permute-start.10
  32.7 1.8 %collective-permute-start.11 = (f32[24,256]{1,0:T(8,128)S(1)}, f32[24,256]{1,0:T(8,128)S(1)}, u32[]{:S(2)}, u32[]{:S(2)}) collective-permute-start(f32[24,256]{1,0:T(8,128)S(1)} %get-tuple-element.67), channel_id=1, source_target_pairs={{8,16},{16,8},{24,32},{32,24},{40,48},{48,40},{56,64},{64,56},{72,... | collective-permute-start | bytes 73736 | tf_op jit(solution)/shard_map/ppermute | solution.py:584
  34.5 0.0 collective-permute-start.12
  34.5 1.6 %collective-permute-start.13 = (f32[16,256]{1,0:T(8,128)S(1)}, f32[16,256]{1,0:T(8,128)S(1)}, u32[]{:S(2)}, u32[]{:S(2)}) collective-permute-start(f32[16,256]{1,0:T(8,128)S(1)} %get-tuple-element.69), channel_id=1, source_target_pairs={{1,2},{2,1},{3,4},{4,3},{5,6},{6,5},{7,0},{0,7},{9,10},{10,9},{11,... | collective-permute-start | bytes 49160 | tf_op jit(solution)/shard_map/ppermute | solution.py:584
  36.1 0.8 %coarse_coefficients.1.coarse_coefs = f32[8,32,256]{2,1,0:T(8,128)S(1)} custom-call(f32[1040,256]{1,0:T(8,128)S(1)} %get-tuple-element.38.kappa_ext.kappa_ref, f32[1024,256]{1,0:T(8,128)S(1)} %get-tuple-element.42.decay_ref), custom_call_target="tpu_custom_call" | custom-call | tf_op jit(solution)/shard_map/coarse_coefficients/pallas_call | solution.py:668
  36.9 2.6 %residual.1 = (f32[1024,128]{1,0:T(8,128)S(1)}, f32[1024,128]{1,0:T(8,128)S(1)}, f32[1024,256]{1,0:T(8,128)}) custom-call(s32[8,128]{1,0:T(8,128)S(1)} %get-tuple-element.36.table, f32[1040,256]{1,0:T(8,128)S(1)} %get-tuple-element.60.ext, f32[1024,256]{1,0:T(8,128)S(1)} %get-tuple-element.41.source_ref, f32[6,1024,256]{2,1,0:T(8,128)S(1)} %get-tuple-element.49.coef_ref, ...), custom_call_target="tpu_custom_call" | custom-call | tf_op jit(solution)/shard_map/residual/pallas_call | solution.py:696
  39.5 0.0 collective-permute-done.12.m2
  39.5 0.0 collective-permute-done.13.m3
  39.5 0.0 collective-permute-done.10.m0
  39.5 0.3 collective-permute-done.11.m1
  39.8 1.7 %residual_rest.1 = f32[16,48,256]{2,1,0:T(8,128)S(1)} custom-call(s32[8,128]{1,0:T(8,128)S(1)} %get-tuple-element.36.table, f32[1024,128]{1,0:T(8,128)S(1)} %get-tuple-element.63.low_in, f32[1024,128]{1,0:T(8,128)S(1)} %get-tuple-element.64.high_in, f32[8,128]{1,0:T(8,128)S(1)} %get-tuple-element.65.known_ref, ...), custom_call_target="tpu_custom_call" | custom-call | tf_op jit(solution)/shard_map/residual_rest/pallas_call | solution.py:704
  41.5 0.0 copy-start
  41.5 19.1 %all_to_all.5.arrived = f32[16,48,256]{2,1,0:T(8,128)S(1)} all-to-all(f32[16,48,256]{2,1,0:T(8,128)S(1)} %residual_rest.1), channel_id=1, replica_groups=mesh['brick'=16,'sub'=8] {'brick'}, dimensions={0} | all-to-all | bytes 1572864 | tf_op jit(solution)/shard_map/all_to_all | solution.py:718
  60.6 0.0 copy-done
  60.6 1.4 %place.1 = f32[8,48,256]{2,1,0:T(8,128)} custom-call(s32[8]{0:T(128)S(1)} %copy-done, f32[16,48,256]{2,1,0:T(8,128)S(1)} %all_to_all.5.arrived), custom_call_target="tpu_custom_call" | custom-call | tf_op jit(solution)/shard_map/place/pallas_call | solution.py:719
Async XLA Ops:
  4.5 15.5 %collective-permute-start.1 = (f32[40,256]{1,0:T(8,128)S(1)}, f32[40,256]{1,0:T(8,128)S(1)}, u32[]{:S(2)}, u32[]{:S(2)}) collective-permute-start(f32[40,256]{1,0:T(8,128)S(1)} %get-tuple-element.44.own0), channel_id=1, source_target_pairs={{0,8},{8,0},{16,24},{24,16},{32,40},{40,32},{48,56},{56,48},{64,72... | collective-permute-start | bytes 122888 | tf_op jit(solution)/shard_map/ppermute | solution.py:584
  6.2 13.8 %collective-permute-start.2 = (f32[40,256]{1,0:T(8,128)S(1)}, f32[40,256]{1,0:T(8,128)S(1)}, u32[]{:S(2)}, u32[]{:S(2)}) collective-permute-start(f32[40,256]{1,0:T(8,128)S(1)} %get-tuple-element.45.own1), channel_id=1, source_target_pairs={{8,16},{16,8},{24,32},{32,24},{40,48},{48,40},{56,64},{64,56},{72,... | collective-permute-start | bytes 122888 | tf_op jit(solution)/shard_map/ppermute | solution.py:584
  10.7 9.3 %collective-permute-start.3 = (f32[32,256]{1,0:T(8,128)S(1)}, f32[32,256]{1,0:T(8,128)S(1)}, u32[]{:S(2)}, u32[]{:S(2)}) collective-permute-start(f32[32,256]{1,0:T(8,128)S(1)} %get-tuple-element.46.own2), channel_id=1, source_target_pairs={{0,1},{1,0},{2,3},{3,2},{4,5},{5,4},{6,7},{7,6},{8,9},{9,8},{10,11... | collective-permute-start | bytes 98312 | tf_op jit(solution)/shard_map/ppermute | solution.py:584
  10.7 9.3 %collective-permute-start.4 = (f32[32,256]{1,0:T(8,128)S(1)}, f32[32,256]{1,0:T(8,128)S(1)}, u32[]{:S(2)}, u32[]{:S(2)}) collective-permute-start(f32[32,256]{1,0:T(8,128)S(1)} %get-tuple-element.47.own3), channel_id=1, source_target_pairs={{1,2},{2,1},{3,4},{4,3},{5,6},{6,5},{7,0},{0,7},{9,10},{10,9},{11,... | collective-permute-start | bytes 98312 | tf_op jit(solution)/shard_map/ppermute | solution.py:584
  14.9 5.1 %collective-permute-start = (f32[8,128]{1,0:T(8,128)S(1)}, f32[8,128]{1,0:T(8,128)S(1)}, u32[]{:S(2)}, u32[]{:S(2)}) collective-permute-start(f32[8,128]{1,0:T(8,128)S(1)} %get-tuple-element.43.known_ref), channel_id=1, source_target_pairs={{0,64},{8,72},{16,80},{24,88},{32,96},{40,104},{48,112},{56,120},{... | collective-permute-start | bytes 12296 | tf_op jit(solution)/shard_map/ppermute | solution.py:589
  22.1 8.3 %collective-permute-start.6 = (f32[24,256]{1,0:T(8,128)S(1)}, f32[24,256]{1,0:T(8,128)S(1)}, u32[]{:S(2)}, u32[]{:S(2)}) collective-permute-start(f32[24,256]{1,0:T(8,128)S(1)} %get-tuple-element.56), channel_id=1, source_target_pairs={{0,8},{8,0},{16,24},{24,16},{32,40},{40,32},{48,56},{56,48},{64,72... | collective-permute-start | bytes 73736 | tf_op jit(solution)/shard_map/ppermute | solution.py:584
  22.9 7.5 %collective-permute-start.7 = (f32[24,256]{1,0:T(8,128)S(1)}, f32[24,256]{1,0:T(8,128)S(1)}, u32[]{:S(2)}, u32[]{:S(2)}) collective-permute-start(f32[24,256]{1,0:T(8,128)S(1)} %get-tuple-element.57), channel_id=1, source_target_pairs={{8,16},{16,8},{24,32},{32,24},{40,48},{48,40},{56,64},{64,56},{72,... | collective-permute-start | bytes 73736 | tf_op jit(solution)/shard_map/ppermute | solution.py:584
  25.1 5.3 %collective-permute-start.8 = (f32[16,256]{1,0:T(8,128)S(1)}, f32[16,256]{1,0:T(8,128)S(1)}, u32[]{:S(2)}, u32[]{:S(2)}) collective-permute-start(f32[16,256]{1,0:T(8,128)S(1)} %get-tuple-element.58), channel_id=1, source_target_pairs={{0,1},{1,0},{2,3},{3,2},{4,5},{5,4},{6,7},{7,6},{8,9},{9,8},{10,11... | collective-permute-start | bytes 49160 | tf_op jit(solution)/shard_map/ppermute | solution.py:584
  25.1 5.3 %collective-permute-start.9 = (f32[16,256]{1,0:T(8,128)S(1)}, f32[16,256]{1,0:T(8,128)S(1)}, u32[]{:S(2)}, u32[]{:S(2)}) collective-permute-start(f32[16,256]{1,0:T(8,128)S(1)} %get-tuple-element.59), channel_id=1, source_target_pairs={{1,2},{2,1},{3,4},{4,3},{5,6},{6,5},{7,0},{0,7},{9,10},{10,9},{11,... | collective-permute-start | bytes 49160 | tf_op jit(solution)/shard_map/ppermute | solution.py:584
  25.6 4.8 %collective-permute-start.5 = (f32[8,128]{1,0:T(8,128)S(1)}, f32[8,128]{1,0:T(8,128)S(1)}, u32[]{:S(2)}, u32[]{:S(2)}) collective-permute-start(f32[8,128]{1,0:T(8,128)S(1)} %get-tuple-element.51.known_ref), channel_id=1, source_target_pairs={{0,32},{8,40},{16,48},{24,56},{32,64},{40,72},{48,80},{56,88},{64,... | collective-permute-start | bytes 12296 | tf_op jit(solution)/shard_map/ppermute | solution.py:589
  32.1 7.4 %collective-permute-start.10 = (f32[24,256]{1,0:T(8,128)S(1)}, f32[24,256]{1,0:T(8,128)S(1)}, u32[]{:S(2)}, u32[]{:S(2)}) collective-permute-start(f32[24,256]{1,0:T(8,128)S(1)} %get-tuple-element.66), channel_id=1, source_target_pairs={{0,8},{8,0},{16,24},{24,16},{32,40},{40,32},{48,56},{56,48},{64,72... | collective-permute-start | bytes 73736 | tf_op jit(solution)/shard_map/ppermute | solution.py:584
  32.7 7.1 %collective-permute-start.11 = (f32[24,256]{1,0:T(8,128)S(1)}, f32[24,256]{1,0:T(8,128)S(1)}, u32[]{:S(2)}, u32[]{:S(2)}) collective-permute-start(f32[24,256]{1,0:T(8,128)S(1)} %get-tuple-element.67), channel_id=1, source_target_pairs={{8,16},{16,8},{24,32},{32,24},{40,48},{48,40},{56,64},{64,56},{72,... | collective-permute-start | bytes 73736 | tf_op jit(solution)/shard_map/ppermute | solution.py:584
  34.5 5.0 %collective-permute-start.12 = (f32[16,256]{1,0:T(8,128)S(1)}, f32[16,256]{1,0:T(8,128)S(1)}, u32[]{:S(2)}, u32[]{:S(2)}) collective-permute-start(f32[16,256]{1,0:T(8,128)S(1)} %get-tuple-element.68), channel_id=1, source_target_pairs={{0,1},{1,0},{2,3},{3,2},{4,5},{5,4},{6,7},{7,6},{8,9},{9,8},{10,11... | collective-permute-start | bytes 49160 | tf_op jit(solution)/shard_map/ppermute | solution.py:584
  34.5 5.0 %collective-permute-start.13 = (f32[16,256]{1,0:T(8,128)S(1)}, f32[16,256]{1,0:T(8,128)S(1)}, u32[]{:S(2)}, u32[]{:S(2)}) collective-permute-start(f32[16,256]{1,0:T(8,128)S(1)} %get-tuple-element.69), channel_id=1, source_target_pairs={{1,2},{2,1},{3,4},{4,3},{5,6},{6,5},{7,0},{0,7},{9,10},{10,9},{11,... | collective-permute-start | bytes 49160 | tf_op jit(solution)/shard_map/ppermute | solution.py:584
  41.5 19.1 %copy-start = (s32[8]{0:T(128)S(1)}, s32[8]{0:T(128)}, u32[]{:S(2)}) copy-start(s32[8]{0:T(128)} %coarse_source.1) | copy-start | bytes 100

commit v4 on v3

--- a/solution.py
+++ b/solution.py
@@ -656,7 +656,7 @@
     own_faces = outgoing
     incoming = exchanged(outgoing)
     bricks_along = lax.axis_size("brick")
-    other = shifted(known, "brick", bricks_along // 2)
+    other = shifted(known, "brick", bricks_along // 4)
 
     coefs, diagonal, total, source, decay_rate = kernel_call(
         links_kernel,
@@ -677,7 +677,7 @@
     )(table, diagonal, total, source, decay_rate, field_start, known, other, *own_faces, *incoming)
     far_links, outgoing = rest[:PEERS], rest[PEERS:]
     incoming = exchanged(outgoing)
-    other = shifted(known, "brick", bricks_along // 4)
+    other = shifted(known, "brick", bricks_along // 2)
     for _ in range(SWEEPS - 1):
         field = kernel_call(
             sweep_kernel,

time: 62.7 us -> 62.3 us (level)
  starting transfers between devices: 19.1 us -> 20.4 us
  blocking collectives: 19.1 us -> 18.3 us
    ppermute x12, starting transfers between devices: 17.8 us -> 18.7 us  [paired(): return lax.ppermute(block, axis, route)]
    all_to_all x1, blocking collectives: 19.1 us -> 18.3 us  [body(): lax.all_to_all(send, 'brick', split_axis=0, concat_axis=0, tiled=True)]
  transfers between devices with their start and end apart: 14 -> 14, of which waited for: 2 -> 3; matrix products, arithmetic and copies ran while one was open for 0% -> 0% of each run, Pallas kernels for 17% -> 17%
where the time goes in v4:
time: 62.3 us; the launch traced here: 62.1 us
  Pallas kernels  21.2 us (34%)
  starting transfers between devices  20.4 us (33%)
  blocking collectives  18.3 us (29%)
  waiting for transfers between devices  1.38 us (2%)
  between operations  0.91 us (1%)
    ppermute x12, starting transfers between devices, paired(): return lax.ppermute(block, axis, route)  18.7 us
    all_to_all x1, blocking collectives, body(): lax.all_to_all(send, 'brick', split_axis=0, concat_axis=0, tiled=True)  18.3 us
    pallas_call x1, Pallas kernels, body(): kernel_call(links_kernel, 'links', [SMEM_SPEC] + [VMEM_SPEC] * 2 + [HBM_S...  4.46 us
    pallas_call x1, Pallas kernels, body(): kernel_call(functools.partial(start_kernel, subs), 'route_and_pack', [HBM...  3.87 us
    pallas_call x1, Pallas kernels, body(): kernel_call(residual_kernel, 'residual', [SMEM_SPEC] + [VMEM_SPEC] * 4, (...  2.61 us
    pallas_call x1, Pallas kernels, body(): kernel_call(sweep_kernel, 'next_sweep', [SMEM_SPEC] + [VMEM_SPEC] * 4, (w...  2.61 us
    pallas_call x1, Pallas kernels, body(): kernel_call(first_kernel, 'first_sweep', [SMEM_SPEC] + [VMEM_SPEC] * 15,...  2.13 us
    pallas_call x1, Pallas kernels, body(): kernel_call(functools.partial(residual_rest_kernel, subs), 'residual_rest...  1.68 us
  transfers between devices with their start and end apart: 14, of which 3 were waited for; matrix products, arithmetic and copies ran while one was open for 0% of the time, Pallas kernels for 17%

profile of v4, /device:TPU:0, one launch (start us, length us, event | category | flops | bytes accessed | tf_op | source)
XLA Modules:
  0.0 62.1 jit_solution(11490467349351535195)
XLA Ops:
  0.6 3.9 %route_and_pack.1 = (s32[8,128]{1,0:T(8,128)S(1)}, f32[1040,256]{1,0:T(8,128)S(1)}, f32[1040,256]{1,0:T(8,128)S(1)}, f32[40,256]{1,0:T(8,128)S(1)}, f32[40,256]{...) custom-call(s32[8]{0:T(128)} %coarse_source.1, s32[6,64]{1,0:T(8,128)} %bitcast.12, ...), custom_call_target="tpu_custom_call" | custom-call | tf_op jit(solution)/shard_map/route_and_pack/pallas_call | solution.py:638
  4.5 1.7 %collective-permute-start.1 = (f32[40,256]{1,0:T(8,128)S(1)}, f32[40,256]{1,0:T(8,128)S(1)}, u32[]{:S(2)}, u32[]{:S(2)}) collective-permute-start(f32[40,256]{1,0:T(8,128)S(1)} %get-tuple-element.44.own0), channel_id=1, source_target_pairs={{0,8},{8,0},{16,24},{24,16},{32,40},{40,32},{48,56},{56,48},{64,72... | collective-permute-start | bytes 122888 | tf_op jit(solution)/shard_map/ppermute | solution.py:584
  6.2 4.5 %collective-permute-start.2 = (f32[40,256]{1,0:T(8,128)S(1)}, f32[40,256]{1,0:T(8,128)S(1)}, u32[]{:S(2)}, u32[]{:S(2)}) collective-permute-start(f32[40,256]{1,0:T(8,128)S(1)} %get-tuple-element.45.own1), channel_id=1, source_target_pairs={{8,16},{16,8},{24,32},{32,24},{40,48},{48,40},{56,64},{64,56},{72,... | collective-permute-start | bytes 122888 | tf_op jit(solution)/shard_map/ppermute | solution.py:584
  10.7 0.0 collective-permute-start.3
  10.7 4.1 %collective-permute-start.4 = (f32[32,256]{1,0:T(8,128)S(1)}, f32[32,256]{1,0:T(8,128)S(1)}, u32[]{:S(2)}, u32[]{:S(2)}) collective-permute-start(f32[32,256]{1,0:T(8,128)S(1)} %get-tuple-element.47.own3), channel_id=1, source_target_pairs={{1,2},{2,1},{3,4},{4,3},{5,6},{6,5},{7,0},{0,7},{9,10},{10,9},{11,... | collective-permute-start | bytes 98312 | tf_op jit(solution)/shard_map/ppermute | solution.py:584
  14.9 0.0 collective-permute-start
  14.9 4.5 %links.1 = (f32[6,1024,256]{2,1,0:T(8,128)S(1)}, f32[1024,256]{1,0:T(8,128)S(1)}, f32[1024,256]{1,0:T(8,128)S(1)}, f32[1024,256]{1,0:T(8,128)S(1)}, f32[1024,256]{1,0:T(8,128)S(1)}) custom-call(s32[8,128]{1,0:T(8,128)S(1)} %get-tuple-element.36.table, f32[1040,256]{1,0:T(8,128)S(1)} %get-tuple-element.37.ext.field_ref, ...), custom_call_target="tpu_custom_call" | custom-call | tf_op jit(solution)/shard_map/links/pallas_call | solution.py:661
  19.3 0.4 collective-permute-done.other_ref
  19.7 0.0 collective-permute-done.3.m2
  19.7 0.0 collective-permute-done.4.m3
  19.7 0.0 collective-permute-done.1.m0
  19.7 0.0 collective-permute-done.2.m1
  19.7 2.1 %first_sweep.1 = (f32[1024,256]{1,0:T(8,128)S(1)}, f32[1040,256]{1,0:T(8,128)S(1)}, f32[1024,256]{1,0:T(8,128)S(1)}, f32[8,128]{1,0:T(8,128)S(1)}, f32[16,256]{1...) custom-call(s32[8,128]{1,0:T(8,128)S(1)} %get-tuple-element.36.table, ...), custom_call_target="tpu_custom_call" | custom-call | tf_op jit(solution)/shard_map/first_sweep/pallas_call | solution.py:672
  21.8 0.1 collective-permute-start.6
  21.9 2.1 %collective-permute-start.7 = (f32[24,256]{1,0:T(8,128)S(1)}, f32[24,256]{1,0:T(8,128)S(1)}, u32[]{:S(2)}, u32[]{:S(2)}) collective-permute-start(f32[24,256]{1,0:T(8,128)S(1)} %get-tuple-element.57), channel_id=1, source_target_pairs={{8,16},{16,8},{24,32},{32,24},{40,48},{48,40},{56,64},{64,56},{72,... | collective-permute-start | bytes 73736 | tf_op jit(solution)/shard_map/ppermute | solution.py:584
  24.1 0.0 collective-permute-start.8
  24.1 0.5 collective-permute-start.9
  24.6 1.7 %collective-permute-start.5 = (f32[8,128]{1,0:T(8,128)S(1)}, f32[8,128]{1,0:T(8,128)S(1)}, u32[]{:S(2)}, u32[]{:S(2)}) collective-permute-start(f32[8,128]{1,0:T(8,128)S(1)} %get-tuple-element.51.known_ref), channel_id=1, source_target_pairs={{0,64},{8,72},{16,80},{24,88},{32,96},{40,104},{48,112},{56,120},{... | collective-permute-start | bytes 12296 | tf_op jit(solution)/shard_map/ppermute | solution.py:589
  26.2 2.6 %next_sweep.1.new_in = f32[1024,256]{1,0:T(8,128)S(1)} custom-call(s32[8,128]{1,0:T(8,128)S(1)} %get-tuple-element.36.table, f32[1040,256]{1,0:T(8,128)S(1)} %get-tuple-element.48.ext, f32[1024,256]{1,0:T(8,128)S(1)} %get-tuple-element.41.source_ref, f32[6,1024,256]{2,1,0:T(8,128)S(1)} %get-tuple-element.49.coef_ref, f32[1024,256]{1,0:T(8,128)S(1)} %get-tuple-element.50.scale_ref), custom_call_target="tpu_custom_call" | custom-call | tf_op jit(solution)/shard_map/next_sweep/pallas_call | solution.py:682
  28.8 0.8 %collective-permute-done.5.other_ref = f32[8,128]{1,0:T(8,128)S(1)} collective-permute-done((f32[8,128]{1,0:T(8,128)S(1)}, f32[8,128]{1,0:T(8,128)S(1)}, u32[]{:S(2)}, u32[]{:S(2)}) %collective-permute-start.5) | collective-permute-done | bytes 4128 | tf_op jit(solution)/shard_map/ppermute | solution.py:589
  29.7 0.0 collective-permute-done.8.m2
  29.7 0.0 collective-permute-done.9.m3
  29.7 0.0 collective-permute-done.6.m0
  29.7 0.0 collective-permute-done.7.m1
  29.7 1.7 %next_sweep_rest.1 = (f32[1040,256]{1,0:T(8,128)S(1)}, f32[8,128]{1,0:T(8,128)S(1)}, f32[24,256]{1,0:T(8,128)S(1)}, f32[24,256]{1,0:T(8,128)S(1)}, f32[16,256]{1,0:T(8,128)S(1)}, /*index=5*/f32[16,256]{1,0:T(8,128)S(1)}) custom-call(s32[8,128]{1,0:T(8,128)S(1)} %get-tuple-element.36.table, f32[1024,256]{1,0:T(8,128)S(1)} %next_sweep.1.new_in, ...), custom_call_target="tpu_custom_call" | custom-call | tf_op jit(solution)/shard_map/next_sweep_rest/pallas_call | solution.py:688
  31.4 0.3 collective-permute-start.10
  31.6 4.6 %collective-permute-start.11 = (f32[24,256]{1,0:T(8,128)S(1)}, f32[24,256]{1,0:T(8,128)S(1)}, u32[]{:S(2)}, u32[]{:S(2)}) collective-permute-start(f32[24,256]{1,0:T(8,128)S(1)} %get-tuple-element.67), channel_id=1, source_target_pairs={{8,16},{16,8},{24,32},{32,24},{40,48},{48,40},{56,64},{64,56},{72,... | collective-permute-start | bytes 73736 | tf_op jit(solution)/shard_map/ppermute | solution.py:584
  36.3 0.0 collective-permute-start.12
  36.3 0.8 %collective-permute-start.13 = (f32[16,256]{1,0:T(8,128)S(1)}, f32[16,256]{1,0:T(8,128)S(1)}, u32[]{:S(2)}, u32[]{:S(2)}) collective-permute-start(f32[16,256]{1,0:T(8,128)S(1)} %get-tuple-element.69), channel_id=1, source_target_pairs={{1,2},{2,1},{3,4},{4,3},{5,6},{6,5},{7,0},{0,7},{9,10},{10,9},{11,... | collective-permute-start | bytes 49160 | tf_op jit(solution)/shard_map/ppermute | solution.py:584
  37.0 0.8 %coarse_coefficients.1.coarse_coefs = f32[8,32,256]{2,1,0:T(8,128)S(1)} custom-call(f32[1040,256]{1,0:T(8,128)S(1)} %get-tuple-element.38.kappa_ext.kappa_ref, f32[1024,256]{1,0:T(8,128)S(1)} %get-tuple-element.42.decay_ref), custom_call_target="tpu_custom_call" | custom-call | tf_op jit(solution)/shard_map/coarse_coefficients/pallas_call | solution.py:668
  37.8 2.6 %residual.1 = (f32[1024,128]{1,0:T(8,128)S(1)}, f32[1024,128]{1,0:T(8,128)S(1)}, f32[1024,256]{1,0:T(8,128)}) custom-call(s32[8,128]{1,0:T(8,128)S(1)} %get-tuple-element.36.table, f32[1040,256]{1,0:T(8,128)S(1)} %get-tuple-element.60.ext, f32[1024,256]{1,0:T(8,128)S(1)} %get-tuple-element.41.source_ref, f32[6,1024,256]{2,1,0:T(8,128)S(1)} %get-tuple-element.49.coef_ref, ...), custom_call_target="tpu_custom_call" | custom-call | tf_op jit(solution)/shard_map/residual/pallas_call | solution.py:696
  40.5 0.0 collective-permute-done.12.m2
  40.5 0.2 collective-permute-done.13.m3
  40.6 0.0 collective-permute-done.10.m0
  40.6 0.0 collective-permute-done.11.m1
  40.7 1.7 %residual_rest.1 = f32[16,48,256]{2,1,0:T(8,128)S(1)} custom-call(s32[8,128]{1,0:T(8,128)S(1)} %get-tuple-element.36.table, f32[1024,128]{1,0:T(8,128)S(1)} %get-tuple-element.63.low_in, f32[1024,128]{1,0:T(8,128)S(1)} %get-tuple-element.64.high_in, f32[8,128]{1,0:T(8,128)S(1)} %get-tuple-element.65.known_ref, ...), custom_call_target="tpu_custom_call" | custom-call | tf_op jit(solution)/shard_map/residual_rest/pallas_call | solution.py:704
  42.3 0.0 copy-start
  42.4 18.3 %all_to_all.5.arrived = f32[16,48,256]{2,1,0:T(8,128)S(1)} all-to-all(f32[16,48,256]{2,1,0:T(8,128)S(1)} %residual_rest.1), channel_id=1, replica_groups=mesh['brick'=16,'sub'=8] {'brick'}, dimensions={0} | all-to-all | bytes 1572864 | tf_op jit(solution)/shard_map/all_to_all | solution.py:718
  60.6 0.0 copy-done
  60.6 1.4 %place.1 = f32[8,48,256]{2,1,0:T(8,128)} custom-call(s32[8]{0:T(128)S(1)} %copy-done, f32[16,48,256]{2,1,0:T(8,128)S(1)} %all_to_all.5.arrived), custom_call_target="tpu_custom_call" | custom-call | tf_op jit(solution)/shard_map/place/pallas_call | solution.py:719
Async XLA Ops:
  4.5 15.2 %collective-permute-start.1 = (f32[40,256]{1,0:T(8,128)S(1)}, f32[40,256]{1,0:T(8,128)S(1)}, u32[]{:S(2)}, u32[]{:S(2)}) collective-permute-start(f32[40,256]{1,0:T(8,128)S(1)} %get-tuple-element.44.own0), channel_id=1, source_target_pairs={{0,8},{8,0},{16,24},{24,16},{32,40},{40,32},{48,56},{56,48},{64,72... | collective-permute-start | bytes 122888 | tf_op jit(solution)/shard_map/ppermute | solution.py:584
  6.2 13.5 %collective-permute-start.2 = (f32[40,256]{1,0:T(8,128)S(1)}, f32[40,256]{1,0:T(8,128)S(1)}, u32[]{:S(2)}, u32[]{:S(2)}) collective-permute-start(f32[40,256]{1,0:T(8,128)S(1)} %get-tuple-element.45.own1), channel_id=1, source_target_pairs={{8,16},{16,8},{24,32},{32,24},{40,48},{48,40},{56,64},{64,56},{72,... | collective-permute-start | bytes 122888 | tf_op jit(solution)/shard_map/ppermute | solution.py:584
  10.7 9.0 %collective-permute-start.3 = (f32[32,256]{1,0:T(8,128)S(1)}, f32[32,256]{1,0:T(8,128)S(1)}, u32[]{:S(2)}, u32[]{:S(2)}) collective-permute-start(f32[32,256]{1,0:T(8,128)S(1)} %get-tuple-element.46.own2), channel_id=1, source_target_pairs={{0,1},{1,0},{2,3},{3,2},{4,5},{5,4},{6,7},{7,6},{8,9},{9,8},{10,11... | collective-permute-start | bytes 98312 | tf_op jit(solution)/shard_map/ppermute | solution.py:584
  10.7 9.0 %collective-permute-start.4 = (f32[32,256]{1,0:T(8,128)S(1)}, f32[32,256]{1,0:T(8,128)S(1)}, u32[]{:S(2)}, u32[]{:S(2)}) collective-permute-start(f32[32,256]{1,0:T(8,128)S(1)} %get-tuple-element.47.own3), channel_id=1, source_target_pairs={{1,2},{2,1},{3,4},{4,3},{5,6},{6,5},{7,0},{0,7},{9,10},{10,9},{11,... | collective-permute-start | bytes 98312 | tf_op jit(solution)/shard_map/ppermute | solution.py:584
  14.9 4.8 %collective-permute-start = (f32[8,128]{1,0:T(8,128)S(1)}, f32[8,128]{1,0:T(8,128)S(1)}, u32[]{:S(2)}, u32[]{:S(2)}) collective-permute-start(f32[8,128]{1,0:T(8,128)S(1)} %get-tuple-element.43.known_ref), channel_id=1, source_target_pairs={{0,32},{8,40},{16,48},{24,56},{32,64},{40,72},{48,80},{56,88},{64,... | collective-permute-start | bytes 12296 | tf_op jit(solution)/shard_map/ppermute | solution.py:589
  21.8 7.8 %collective-permute-start.6 = (f32[24,256]{1,0:T(8,128)S(1)}, f32[24,256]{1,0:T(8,128)S(1)}, u32[]{:S(2)}, u32[]{:S(2)}) collective-permute-start(f32[24,256]{1,0:T(8,128)S(1)} %get-tuple-element.56), channel_id=1, source_target_pairs={{0,8},{8,0},{16,24},{24,16},{32,40},{40,32},{48,56},{56,48},{64,72... | collective-permute-start | bytes 73736 | tf_op jit(solution)/shard_map/ppermute | solution.py:584
  21.9 7.7 %collective-permute-start.7 = (f32[24,256]{1,0:T(8,128)S(1)}, f32[24,256]{1,0:T(8,128)S(1)}, u32[]{:S(2)}, u32[]{:S(2)}) collective-permute-start(f32[24,256]{1,0:T(8,128)S(1)} %get-tuple-element.57), channel_id=1, source_target_pairs={{8,16},{16,8},{24,32},{32,24},{40,48},{48,40},{56,64},{64,56},{72,... | collective-permute-start | bytes 73736 | tf_op jit(solution)/shard_map/ppermute | solution.py:584
  24.1 5.6 %collective-permute-start.8 = (f32[16,256]{1,0:T(8,128)S(1)}, f32[16,256]{1,0:T(8,128)S(1)}, u32[]{:S(2)}, u32[]{:S(2)}) collective-permute-start(f32[16,256]{1,0:T(8,128)S(1)} %get-tuple-element.58), channel_id=1, source_target_pairs={{0,1},{1,0},{2,3},{3,2},{4,5},{5,4},{6,7},{7,6},{8,9},{9,8},{10,11... | collective-permute-start | bytes 49160 | tf_op jit(solution)/shard_map/ppermute | solution.py:584
  24.1 5.6 %collective-permute-start.9 = (f32[16,256]{1,0:T(8,128)S(1)}, f32[16,256]{1,0:T(8,128)S(1)}, u32[]{:S(2)}, u32[]{:S(2)}) collective-permute-start(f32[16,256]{1,0:T(8,128)S(1)} %get-tuple-element.59), channel_id=1, source_target_pairs={{1,2},{2,1},{3,4},{4,3},{5,6},{6,5},{7,0},{0,7},{9,10},{10,9},{11,... | collective-permute-start | bytes 49160 | tf_op jit(solution)/shard_map/ppermute | solution.py:584
  24.6 5.1 %collective-permute-start.5 = (f32[8,128]{1,0:T(8,128)S(1)}, f32[8,128]{1,0:T(8,128)S(1)}, u32[]{:S(2)}, u32[]{:S(2)}) collective-permute-start(f32[8,128]{1,0:T(8,128)S(1)} %get-tuple-element.51.known_ref), channel_id=1, source_target_pairs={{0,64},{8,72},{16,80},{24,88},{32,96},{40,104},{48,112},{56,120},{... | collective-permute-start | bytes 12296 | tf_op jit(solution)/shard_map/ppermute | solution.py:589
  31.4 9.3 %collective-permute-start.10 = (f32[24,256]{1,0:T(8,128)S(1)}, f32[24,256]{1,0:T(8,128)S(1)}, u32[]{:S(2)}, u32[]{:S(2)}) collective-permute-start(f32[24,256]{1,0:T(8,128)S(1)} %get-tuple-element.66), channel_id=1, source_target_pairs={{0,8},{8,0},{16,24},{24,16},{32,40},{40,32},{48,56},{56,48},{64,72... | collective-permute-start | bytes 73736 | tf_op jit(solution)/shard_map/ppermute | solution.py:584
  31.6 9.0 %collective-permute-start.11 = (f32[24,256]{1,0:T(8,128)S(1)}, f32[24,256]{1,0:T(8,128)S(1)}, u32[]{:S(2)}, u32[]{:S(2)}) collective-permute-start(f32[24,256]{1,0:T(8,128)S(1)} %get-tuple-element.67), channel_id=1, source_target_pairs={{8,16},{16,8},{24,32},{32,24},{40,48},{48,40},{56,64},{64,56},{72,... | collective-permute-start | bytes 73736 | tf_op jit(solution)/shard_map/ppermute | solution.py:584
  36.3 4.2 %collective-permute-start.12 = (f32[16,256]{1,0:T(8,128)S(1)}, f32[16,256]{1,0:T(8,128)S(1)}, u32[]{:S(2)}, u32[]{:S(2)}) collective-permute-start(f32[16,256]{1,0:T(8,128)S(1)} %get-tuple-element.68), channel_id=1, source_target_pairs={{0,1},{1,0},{2,3},{3,2},{4,5},{5,4},{6,7},{7,6},{8,9},{9,8},{10,11... | collective-permute-start | bytes 49160 | tf_op jit(solution)/shard_map/ppermute | solution.py:584
  36.3 4.4 %collective-permute-start.13 = (f32[16,256]{1,0:T(8,128)S(1)}, f32[16,256]{1,0:T(8,128)S(1)}, u32[]{:S(2)}, u32[]{:S(2)}) collective-permute-start(f32[16,256]{1,0:T(8,128)S(1)} %get-tuple-element.69), channel_id=1, source_target_pairs={{1,2},{2,1},{3,4},{4,3},{5,6},{6,5},{7,0},{0,7},{9,10},{10,9},{11,... | collective-permute-start | bytes 49160 | tf_op jit(solution)/shard_map/ppermute | solution.py:584
  42.3 18.3 %copy-start = (s32[8]{0:T(128)S(1)}, s32[8]{0:T(128)}, u32[]{:S(2)}) copy-start(s32[8]{0:T(128)} %coarse_source.1) | copy-start | bytes 100
